TPU v7x, 32 devices: a whole 2x2x4 slice. The times are simulated.
32 devices in a mesh: grp: 4 (over y, x), dp: 8 (over z, core).
Axes of the slice: x: 2, y: 2, z: 4, core: 2. Of those that a mesh axis runs over, the one named last changes fastest.
Arguments:
- images: float32 [4, 24, 3, 1024], P('grp', 'dp'), may hold values from -6 to 6
- probes: float32 [4, 24, 3, 1024], P('grp', 'dp'), may hold values from -6 to 6
- out_cotangent: float32 [4, 24, 3, 1024], P('grp', 'dp'), may hold values from -3.2 to 4.8
- counts: int32 [4, 8], P('grp', 'dp'), may hold values from 1 to 3, 16 in all within a row
- terms: int32 [4, 24], P('grp', 'dp'), may hold values from 1 to 4, as said below
- power_left: float32 [4, 2, 512], P('grp'), may hold values from -6 to 6
- power_out: float32 [4, 3], P('grp'), may hold values from -6 to 6
- mid_weight: float32 [4, 512, 512], P('grp', None, 'dp')
- mid_first: float32 [4, 512, 512], P('grp', None, 'dp'), may hold values from -1.25 to 1.25
- mid_second: float32 [4, 512, 512], P('grp', None, 'dp'), may hold values from 0.0005138022 to 0.002055209
- side_weight: float32 [4, 58, 512], P('grp', None, 'dp')
- side_first: float32 [4, 58, 512], P('grp', None, 'dp')
- side_second: float32 [4, 58, 512], P('grp', None, 'dp')
- tiny_weight: float32 [4, 4, 3], P('grp')
- tiny_first: float32 [4, 4, 3], P('grp')
- tiny_second: float32 [4, 4, 3], P('grp')
- mid_outer: float32 [512, 512], P(None, 'dp')
- mid_momentum: float32 [512, 512], P(None, 'dp'), may hold values from -0.3125 to 0.3125
- side_outer: float32 [58, 512], P(None, 'dp')
- side_momentum: float32 [58, 512], P(None, 'dp'), may hold values from -0.3125 to 0.3125
- tiny_outer: float32 [4, 3], replicated
- tiny_momentum: float32 [4, 3], replicated, may hold values from -0.75 to 0.75
Outputs:
- flow_out: float32 [4, 24, 3, 1024], P('grp', 'dp')
- input_gradient: float32 [4, 24, 3, 1024], P('grp', 'dp')
- log_det: float32 [4, 24], P('grp', 'dp')
- log_det_mean: float32 [4], P('grp')
- mid_first_new: float32 [4, 512, 512], P('grp', None, 'dp')
- mid_second_new: float32 [4, 512, 512], P('grp', None, 'dp')
- mid_new: float32 [4, 512, 512], P('grp', None, 'dp')
- side_first_new: float32 [4, 58, 512], P('grp', None, 'dp')
- side_second_new: float32 [4, 58, 512], P('grp', None, 'dp')
- side_new: float32 [4, 58, 512], P('grp', None, 'dp')
- tiny_first_new: float32 [4, 4, 3], P('grp')
- tiny_second_new: float32 [4, 3, 3], P('grp')
- slope_second_new: float32 [4, 3], P('grp')
- tiny_new: float32 [4, 4, 3], P('grp')
- mid_delta: float32 [512, 512], P(None, 'dp')
- mid_momentum_new: float32 [512, 512], P(None, 'dp')
- mid_outer_new: float32 [512, 512], P(None, 'dp')
- side_delta: float32 [58, 512], P(None, 'dp')
- side_momentum_new: float32 [58, 512], P(None, 'dp')
- side_outer_new: float32 [58, 512], P(None, 'dp')
- tiny_delta: float32 [4, 3], replicated
- tiny_momentum_new: float32 [4, 3], replicated
- tiny_outer_new: float32 [4, 3], replicated
Inputs may be any that keep to these rules, and one draw needn't show every extreme that they name: In each group the devices' counts sum to 16, and some device holds 3. `terms`: in each group some valid image has 4.
All inputs are finite; a program needn't handle non-finite values.
Results may differ from a plain program's by a relative error of at most 0.0003.
Values sent between devices are 32-bit elements; how exact they have to be, the bound alone decides.
A program may use at most 128 MiB of HBM per device.

v0:
```python
import jax
import jax.numpy as jnp
from jax import lax
from jax.sharding import PartitionSpec as P

HIDDEN_SIZE = 512
COLORS = 3
HEIGHT = 32
WIDTH = 32
TERMS = 4
IMAGES_DEV = 2


highest = lax.Precision.HIGHEST
clip_level = 0.98
adam_first = 0.9
adam_second = 0.999
adam_eps = 1e-08
decay_rate = 0.01
step_count = 5.0
outer_rate = 0.7
outer_beta = 0.9


def tap_shift(field, tap):
    channels = field.shape[0]
    grid = field.reshape(channels, HEIGHT, WIDTH)
    padded = jnp.pad(grid, ((0, 0), (1, 1), (1, 1)))
    row_shift = tap // 3
    col_shift = tap % 3
    return padded[:, row_shift : row_shift + HEIGHT, col_shift : col_shift + WIDTH].reshape(
        channels, HEIGHT * WIDTH
    )


def lipswish(value, slope_raw):
    slope = jax.nn.softplus(slope_raw)[:, None]
    return value * jax.nn.sigmoid(slope * value) / 1.1


def unit(vector):
    return vector / jnp.sqrt(jnp.sum(vector * vector) + 1e-12)


def matrices(params):
    middle, side, tiny = params
    first = side[0:27].T
    last = side[31:58].reshape(COLORS, 9 * HIDDEN_SIZE)
    return (first, middle, last)


def power_pairs(params, lefts):
    pairs = []
    for matrix, left in zip(matrices(params), lefts):
        right = unit(jnp.dot(matrix.T, left, precision=highest))
        pairs.append((unit(jnp.dot(matrix, right, precision=highest)), right))
    return pairs


def normalized(matrix, pair):
    left, right = pair
    sigma = jnp.dot(left, jnp.dot(matrix, right, precision=highest), precision=highest)
    return matrix / jnp.maximum(1.0, sigma / clip_level)


def branch(params, pairs, field):
    middle, side, tiny = params
    mats = matrices(params)
    first = normalized(mats[0], pairs[0])
    second = normalized(mats[1], pairs[1])
    last = normalized(mats[2], pairs[2])
    act_zero = lipswish(field, tiny[3])
    stacked = jnp.stack([tap_shift(act_zero, tap) for tap in range(9)], 1).reshape(COLORS * 9, -1)
    hidden_one = jnp.dot(first, stacked, precision=highest) + side[27][:, None]
    act_one = lipswish(hidden_one, side[28])
    hidden_two = jnp.dot(second, act_one, precision=highest) + side[29][:, None]
    act_two = lipswish(hidden_two, side[30])
    per_tap = jnp.dot(last.reshape(COLORS * 9, HIDDEN_SIZE), act_two, precision=highest).reshape(
        COLORS, 9, -1
    )
    result = tap_shift(per_tap[:, 0], 0)
    for tap in range(1, 9):
        result = result + tap_shift(per_tap[:, tap], tap)
    return result + tiny[0][:, None]


def actnorm(tiny, image):
    return (image + tiny[1][:, None]) * jnp.exp(tiny[2])[:, None]


def image_pass(params, pairs, image, probe, cotangent, count):
    tiny = params[2]
    field = actnorm(tiny, image)
    output, pull = jax.vjp(lambda inner: branch(params, pairs, inner), field)
    vector = probe
    series = jnp.zeros((), jnp.float32)
    neumann = jnp.zeros_like(probe)
    for power in range(TERMS):
        live = (count > power).astype(jnp.float32)
        neumann = neumann + live * (-1.0) ** power * vector
        vector = pull(vector)[0]
        series = series + live * ((-1.0) ** power / (power + 1)) * jnp.sum(vector * probe)
    log_total = HEIGHT * WIDTH * jnp.sum(tiny[2]) + series

    def objective(weights, start):
        inner = actnorm(weights[2], start)
        result, back = jax.vjp(lambda value: branch(weights, pairs, value), inner)
        return (
            jnp.sum(cotangent * (inner + result))
            - HEIGHT * WIDTH * jnp.sum(weights[2][2])
            - jnp.sum(probe * back(neumann)[0])
        )

    gradients, image_gradient = jax.grad(objective, argnums=(0, 1))(params, image)
    return (field + output, image_gradient, log_total / (COLORS * HEIGHT * WIDTH), gradients)


def run_images(params, pairs, batch, series, keep):
    empty = jax.tree.map(jnp.zeros_like, params)

    def visit(carry, item):
        image, probe, cotangent, count, weight = item
        output, image_gradient, log_part, gradients = image_pass(
            params, pairs, image, probe, cotangent, count
        )
        carry = jax.tree.map(
            lambda running, gradient: running + weight * gradient, carry, gradients
        )
        return (carry, (weight * output, weight * image_gradient, weight * log_part))

    return lax.scan(visit, empty, (batch[0], batch[1], batch[2], series, keep))


def adam_update(weight, gradient, first, second, rate):
    first = adam_first * first + (1.0 - adam_first) * gradient
    second = adam_second * second + (1.0 - adam_second) * gradient * gradient
    first_hat = first / (1.0 - adam_first**step_count)
    second_hat = second / (1.0 - adam_second**step_count)
    return (
        weight - rate * (first_hat / (jnp.sqrt(second_hat) + adam_eps) + decay_rate * weight),
        first,
        second,
    )


def update_all(params, gradients, firsts, seconds):
    rows = jnp.arange(params[1].shape[0])[:, None]
    rates = (0.01, jnp.where(rows >= 31, 0.004, 0.05), 0.05)
    updated = []
    for kind in range(3):
        updated.append(
            adam_update(params[kind], gradients[kind], firsts[kind], seconds[kind], rates[kind])
        )
    return updated


def on_device(
    images,
    probes,
    out_cotangent,
    counts,
    terms,
    power_left,
    power_out,
    mid_weight,
    mid_first,
    mid_second,
    side_weight,
    side_first,
    side_second,
    tiny_weight,
    tiny_first,
    tiny_second,
    mid_outer,
    mid_momentum,
    side_outer,
    side_momentum,
    tiny_outer,
    tiny_momentum,
):
    group_images = IMAGES_DEV * lax.axis_size("dp")
    mid_full, side_full = (
        lax.all_gather(mid_weight[0], "dp", axis=1, tiled=True),
        lax.all_gather(side_weight[0], "dp", axis=1, tiled=True),
    )
    params = (mid_full, side_full, tiny_weight[0])
    pairs = power_pairs(params, (power_left[0, 0], power_left[0, 1], power_out[0]))
    slots = images.shape[1]
    keep = (jnp.arange(slots) < counts[0, 0]).astype(jnp.float32)
    totals, (flow, back, log_det) = run_images(
        params, pairs, (images[0], probes[0], out_cotangent[0]), terms[0], keep
    )
    log_local = jnp.sum(log_det)
    mid_grad, side_grad = (
        lax.psum_scatter(totals[0], "dp", scatter_dimension=1, tiled=True),
        lax.psum_scatter(totals[1], "dp", scatter_dimension=1, tiled=True),
    )
    tiny_grad, log_sum = lax.psum((totals[2], log_local), "dp")
    gradients = (mid_grad / group_images, side_grad / group_images, tiny_grad / group_images)
    updated = update_all(
        (mid_weight[0], side_weight[0], tiny_weight[0]),
        gradients,
        (mid_first[0], side_first[0], tiny_first[0]),
        (mid_second[0], side_second[0], tiny_second[0]),
    )
    outers = (mid_outer, side_outer, tiny_outer)
    momenta = (mid_momentum, side_momentum, tiny_momentum)
    summed = lax.psum(
        (outers[0] - updated[0][0], outers[1] - updated[1][0], outers[2] - updated[2][0]), "grp"
    )
    groups = lax.axis_size("grp")
    globals_new = []
    for kind in range(3):
        delta = summed[kind] / groups
        momentum_new = outer_beta * momenta[kind] + delta
        globals_new.append(
            (delta, momentum_new, outers[kind] - outer_rate * (delta + outer_beta * momentum_new))
        )
    return (
        flow[None],
        back[None],
        log_det[None],
        (log_sum / group_images).reshape(1),
        updated[0][1][None],
        updated[0][2][None],
        updated[0][0][None],
        updated[1][1][None],
        updated[1][2][None],
        updated[1][0][None],
        updated[2][1][None],
        updated[2][2][0:3][None],
        updated[2][2][3][None],
        updated[2][0][None],
        globals_new[0][0],
        globals_new[0][1],
        globals_new[0][2],
        globals_new[1][0],
        globals_new[1][1],
        globals_new[1][2],
        globals_new[2][0],
        globals_new[2][1],
        globals_new[2][2],
    )


def solution(mesh):
    return jax.shard_map(
        on_device,
        mesh=mesh,
        in_specs=(
            P("grp", "dp", None, None),
            P("grp", "dp", None, None),
            P("grp", "dp", None, None),
            P("grp", "dp"),
            P("grp", "dp"),
            P("grp", None, None),
            P("grp", None),
            P("grp", None, "dp"),
            P("grp", None, "dp"),
            P("grp", None, "dp"),
            P("grp", None, "dp"),
            P("grp", None, "dp"),
            P("grp", None, "dp"),
            P("grp", None, None),
            P("grp", None, None),
            P("grp", None, None),
            P(None, "dp"),
            P(None, "dp"),
            P(None, "dp"),
            P(None, "dp"),
            P(),
            P(),
        ),
        out_specs=(
            P("grp", "dp", None, None),
            P("grp", "dp", None, None),
            P("grp", "dp"),
            P("grp"),
            P("grp", None, "dp"),
            P("grp", None, "dp"),
            P("grp", None, "dp"),
            P("grp", None, "dp"),
            P("grp", None, "dp"),
            P("grp", None, "dp"),
            P("grp", None, None),
            P("grp", None, None),
            P("grp", None),
            P("grp", None, None),
            P(None, "dp"),
            P(None, "dp"),
            P(None, "dp"),
            P(None, "dp"),
            P(None, "dp"),
            P(None, "dp"),
            P(),
            P(),
            P(),
        ),
        check_vma=False,
    )
```

profile of v0, /device:TPU:0, one launch (start us, length us, event | category | flops | bytes accessed | tf_op | source)
XLA Modules:
  0.0 770.5 jit_solution(11946554038272706317)
XLA Ops:
  9.9 15.9 %all-gather = f32[1,58,512]{1,0,2:T(1,128)S(1)} all-gather(f32[1,58,64]{1,0,2:T(1,128)S(1)} %copy.288), channel_id=2, replica_groups=mesh['grp'=4,'dp'=8] {'dp'}, dimensions={2}, use_global_device_ids=true | all-gather | bytes 133632 | tf_op jit(solution)/shard_map/all_gather | solution.py:184
  55.6 594.6 %while.23 = (s32[]{:T(128)}, f32[512,512]{1,0:T(8,128)}, f32[58,512]{1,0:T(8,128)}, f32[4,3]{1,0:T(4,128)}, f32[3,3,1024]{2,0,1:T(4,128)}, /*index=5*/f32[3,3,10...) while((s32[]{:T(128)}, f32[512,512]{1,0:T(8,128)}, ...), condition=%wide.region_26.28_spmd.clone, body=%wide.region_7.27_spmd.clone.sunk | while | flops 38785781760 | bytes 296004160 | solution.py:131
  79.7 5.0 fusion.441
  101.2 4.7 fusion.448
  114.9 4.5 fusion.451
  131.2 4.5 fusion.466
  156.3 9.2 %multiply_reduce_fusion.22 = (f32[512]{0:T(512)}, f32[512]{0:T(512)}, f32[512]{0:T(512)}, f32[512,1024]{1,0:T(8,128)}, f32[512,1024]{1,0:T(8,128)S(1)}, /*index=5*/f32[512,1024]{1,0:T(8,128)S(1)}) fusion(f32[512,1024]{1,0:T(8,128)S(1)} %fusion.444, f32[512]{0:T(512)S(1)} %copy-done.85, f32[512,1024]{1,0:T(8,128)S(1)} %fusion.446, ...), kind=kOutput, calls=%fused_computation.47.clone.1 | convolution fusion | flops 3243506176 | bytes 15740932 | tf_op jit(solution)/shard_map/while/body/eval_jaxpr/jvp(jvp())/dot_general | solution.py:76
  172.6 5.3 fusion.454
  178.5 5.9 multiply_reduce_fusion.23
  188.7 8.7 %multiply_reduce_fusion.24 = (f32[512]{0:T(512)}, f32[512]{0:T(512)}, f32[512]{0:T(512)}, f32[512,1024]{1,0:T(8,128)S(1)}, f32[512,1024]{1,0:T(8,128)S(1)}) fusion(f32[512,1024]{1,0:T(8,128)S(1)} %copy-done.10, f32[512,1024]{1,0:T(8,128)} %get-tuple-element.1715, f32[512,1024]{1,0:T(8,128)S(1)} %fusion.455, f32[512]{0:T(512)S(1)} %copy-done.84, ...), kind=kOutput, calls=%fused_computation.40.clone.1 | convolution fusion | flops 3239836160 | bytes 13639684 | tf_op jit(solution)/shard_map/while/body/eval_jaxpr/transpose(jvp(jvp()))/dot_general | solution.py:76
  272.8 4.1 fusion.439
  276.9 4.8 fusion.441
  298.2 5.0 fusion.448
  312.2 4.5 fusion.451
  328.4 4.5 fusion.466
  353.3 9.4 %multiply_reduce_fusion.22 = (f32[512]{0:T(512)}, f32[512]{0:T(512)}, f32[512]{0:T(512)}, f32[512,1024]{1,0:T(8,128)}, f32[512,1024]{1,0:T(8,128)S(1)}, /*index=5*/f32[512,1024]{1,0:T(8,128)S(1)}) fusion(f32[512,1024]{1,0:T(8,128)S(1)} %fusion.444, f32[512]{0:T(512)S(1)} %copy-done.85, f32[512,1024]{1,0:T(8,128)S(1)} %fusion.446, ...), kind=kOutput, calls=%fused_computation.47.clone.1 | convolution fusion | flops 3243506176 | bytes 15740932 | tf_op jit(solution)/shard_map/while/body/eval_jaxpr/jvp(jvp())/dot_general | solution.py:76
  369.8 5.3 fusion.454
  375.7 5.9 multiply_reduce_fusion.23
  385.8 8.5 %multiply_reduce_fusion.24 = (f32[512]{0:T(512)}, f32[512]{0:T(512)}, f32[512]{0:T(512)}, f32[512,1024]{1,0:T(8,128)S(1)}, f32[512,1024]{1,0:T(8,128)S(1)}) fusion(f32[512,1024]{1,0:T(8,128)S(1)} %copy-done.10, f32[512,1024]{1,0:T(8,128)} %get-tuple-element.1715, f32[512,1024]{1,0:T(8,128)S(1)} %fusion.455, f32[512]{0:T(512)S(1)} %copy-done.84, ...), kind=kOutput, calls=%fused_computation.40.clone.1 | convolution fusion | flops 3239836160 | bytes 13639684 | tf_op jit(solution)/shard_map/while/body/eval_jaxpr/transpose(jvp(jvp()))/dot_general | solution.py:76
  474.5 4.7 fusion.441
  495.7 4.8 fusion.448
  509.5 4.5 fusion.451
  526.0 4.5 fusion.466
  550.9 9.2 %multiply_reduce_fusion.22 = (f32[512]{0:T(512)}, f32[512]{0:T(512)}, f32[512]{0:T(512)}, f32[512,1024]{1,0:T(8,128)}, f32[512,1024]{1,0:T(8,128)S(1)}, /*index=5*/f32[512,1024]{1,0:T(8,128)S(1)}) fusion(f32[512,1024]{1,0:T(8,128)S(1)} %fusion.444, f32[512]{0:T(512)S(1)} %copy-done.85, f32[512,1024]{1,0:T(8,128)S(1)} %fusion.446, ...), kind=kOutput, calls=%fused_computation.47.clone.1 | convolution fusion | flops 3243506176 | bytes 15740932 | tf_op jit(solution)/shard_map/while/body/eval_jaxpr/jvp(jvp())/dot_general | solution.py:76
  567.2 5.3 fusion.454
  573.1 6.1 multiply_reduce_fusion.23
  583.4 8.5 %multiply_reduce_fusion.24 = (f32[512]{0:T(512)}, f32[512]{0:T(512)}, f32[512]{0:T(512)}, f32[512,1024]{1,0:T(8,128)S(1)}, f32[512,1024]{1,0:T(8,128)S(1)}) fusion(f32[512,1024]{1,0:T(8,128)S(1)} %copy-done.10, f32[512,1024]{1,0:T(8,128)} %get-tuple-element.1715, f32[512,1024]{1,0:T(8,128)S(1)} %fusion.455, f32[512]{0:T(512)S(1)} %copy-done.84, ...), kind=kOutput, calls=%fused_computation.40.clone.1 | convolution fusion | flops 3239836160 | bytes 13639684 | tf_op jit(solution)/shard_map/while/body/eval_jaxpr/transpose(jvp(jvp()))/dot_general | solution.py:76
  655.8 18.0 %all-reduce.170 = (f32[]{:T(128)}, f32[4,3]{1,0:T(4,128)S(1)}) all-reduce(f32[]{:T(128)} %reduce_sum.331, f32[4,3]{1,0:T(4,128)S(1)} %copy-done.79), channel_id=1, replica_groups=mesh['grp'=4,'dp'=8] {'dp'}, use_global_device_ids=true, to_apply=%region_28.30 | all-reduce | flops 13 | bytes 104 | tf_op jit(solution)/shard_map/psum | solution.py:198
  678.8 5.4 reduce-scatter.7.cloned.1.call-done
  687.1 16.5 %all-reduce.171 = (f32[58,64]{1,0:T(8,128)S(1)}, f32[4,3]{1,0:T(4,128)S(1)}) all-reduce(f32[58,64]{1,0:T(8,128)S(1)} %get-tuple-element.1023, f32[4,3]{1,0:T(4,128)S(1)} %get-tuple-element.1021), channel_id=1, replica_groups=mesh['grp'=4,'dp'=8] {'grp'}, use_global_device_ids=true, to_apply=%region_33.35 | all-reduce | flops 3724 | bytes 29792 | tf_op jit(solution)/shard_map/psum | solution.py:208
  704.3 12.7 %reduce-scatter.5.cloned.1.call-done = f32[512,64]{0,1:T(8,128)} async-done(((f32[512,512]{0,1:T(8,128)}), f32[512,64]{0,1:T(8,128)}) %reduce-scatter.5.cloned.1.call-update) | async-done | bytes 131088 | tf_op jit(solution)/shard_map/reduce_scatter | solution.py:195
  719.4 41.5 %all-reduce.174.cloned.1.call-done = f32[512,64]{0,1:T(8,128)} async-done(((f32[512,64]{0,1:T(8,128)}), f32[512,64]{0,1:T(8,128)}) %all-reduce.174.cloned.1.call-update) | async-done | bytes 131088 | tf_op jit(solution)/shard_map/psum | solution.py:208
  (1582 shorter events, 457.0 us)
Async XLA Ops:
  7.2 37.8 %all-gather.4.cloned.1.call-start = ((), (), s32[]{:S(2)}) async-start(), calls=%async_computation.4 | async-start | bytes 1179648 | tf_op jit(solution)/shard_map/all_gather | solution.py:183
  9.0 675.2 %reduce-scatter.7.cloned.1.call-start = ((), (), s32[]{:S(2)}) async-start(), calls=%async_computation.5 | async-start | bytes 294912
  56.0 70.2 %copy-start.31 = (f32[1,3]{1,0:T(1,128)}, f32[1,3]{1,0:T(1,128)S(1)}, u32[]{:S(2)}) copy-start(f32[1,3]{1,0:T(1,128)S(1)} %get-tuple-element.1959) | copy-start | bytes 40 | tf_op jit(solution)/shard_map/while
  61.7 64.4 %copy-start.52 = (f32[3]{0:T(128)}, f32[3]{0:T(128)S(1)}, u32[]{:S(2)}) copy-start(f32[3]{0:T(128)S(1)} %slice_bitcast_fusion.6) | copy-start | bytes 40 | tf_op jit(solution)/shard_map/while
  63.7 62.5 %copy-start.54 = (f32[3]{0:T(128)}, f32[3]{0:T(128)S(1)}, u32[]{:S(2)}) copy-start(f32[3]{0:T(128)S(1)} %get-tuple-element.1607) | copy-start | bytes 40 | tf_op jit(solution)/shard_map/while
  64.4 83.0 %copy-start.83 = (f32[512]{0:T(512)}, f32[512]{0:T(512)S(1)}, u32[]{:S(2)}) copy-start(f32[512]{0:T(512)S(1)} %get-tuple-element.1622) | copy-start | bytes 6148 | tf_op jit(solution)/shard_map/while
  70.8 74.8 %copy-start.11 = (f32[27,1024]{1,0:T(8,128)}, f32[27,1024]{1,0:T(8,128)S(1)}, u32[]{:S(2)}) copy-start(f32[27,1024]{1,0:T(8,128)S(1)} %reshape.2641) | copy-start | bytes 331780 | tf_op jit(solution)/shard_map/while
  98.2 49.2 %copy-start.13 = (f32[27,1024]{1,0:T(8,128)}, f32[27,1024]{1,0:T(8,128)S(1)}, u32[]{:S(2)}) copy-start(f32[27,1024]{1,0:T(8,128)S(1)} %reshape.2631) | copy-start | bytes 331780 | tf_op jit(solution)/shard_map/while
  253.1 70.2 %copy-start.31 = (f32[1,3]{1,0:T(1,128)}, f32[1,3]{1,0:T(1,128)S(1)}, u32[]{:S(2)}) copy-start(f32[1,3]{1,0:T(1,128)S(1)} %get-tuple-element.1959) | copy-start | bytes 40 | tf_op jit(solution)/shard_map/while
  258.9 64.4 %copy-start.52 = (f32[3]{0:T(128)}, f32[3]{0:T(128)S(1)}, u32[]{:S(2)}) copy-start(f32[3]{0:T(128)S(1)} %slice_bitcast_fusion.6) | copy-start | bytes 40 | tf_op jit(solution)/shard_map/while
  260.9 62.5 %copy-start.54 = (f32[3]{0:T(128)}, f32[3]{0:T(128)S(1)}, u32[]{:S(2)}) copy-start(f32[3]{0:T(128)S(1)} %get-tuple-element.1607) | copy-start | bytes 40 | tf_op jit(solution)/shard_map/while
  261.6 82.8 %copy-start.83 = (f32[512]{0:T(512)}, f32[512]{0:T(512)S(1)}, u32[]{:S(2)}) copy-start(f32[512]{0:T(512)S(1)} %get-tuple-element.1622) | copy-start | bytes 6148 | tf_op jit(solution)/shard_map/while
  268.0 74.6 %copy-start.11 = (f32[27,1024]{1,0:T(8,128)}, f32[27,1024]{1,0:T(8,128)S(1)}, u32[]{:S(2)}) copy-start(f32[27,1024]{1,0:T(8,128)S(1)} %reshape.2641) | copy-start | bytes 331780 | tf_op jit(solution)/shard_map/while
  295.2 49.2 %copy-start.13 = (f32[27,1024]{1,0:T(8,128)}, f32[27,1024]{1,0:T(8,128)S(1)}, u32[]{:S(2)}) copy-start(f32[27,1024]{1,0:T(8,128)S(1)} %reshape.2631) | copy-start | bytes 331780 | tf_op jit(solution)/shard_map/while
  450.7 70.2 %copy-start.31 = (f32[1,3]{1,0:T(1,128)}, f32[1,3]{1,0:T(1,128)S(1)}, u32[]{:S(2)}) copy-start(f32[1,3]{1,0:T(1,128)S(1)} %get-tuple-element.1959) | copy-start | bytes 40 | tf_op jit(solution)/shard_map/while
  456.5 64.4 %copy-start.52 = (f32[3]{0:T(128)}, f32[3]{0:T(128)S(1)}, u32[]{:S(2)}) copy-start(f32[3]{0:T(128)S(1)} %slice_bitcast_fusion.6) | copy-start | bytes 40 | tf_op jit(solution)/shard_map/while
  458.5 62.5 %copy-start.54 = (f32[3]{0:T(128)}, f32[3]{0:T(128)S(1)}, u32[]{:S(2)}) copy-start(f32[3]{0:T(128)S(1)} %get-tuple-element.1607) | copy-start | bytes 40 | tf_op jit(solution)/shard_map/while
  459.2 82.8 %copy-start.83 = (f32[512]{0:T(512)}, f32[512]{0:T(512)S(1)}, u32[]{:S(2)}) copy-start(f32[512]{0:T(512)S(1)} %get-tuple-element.1622) | copy-start | bytes 6148 | tf_op jit(solution)/shard_map/while
  465.6 74.6 %copy-start.11 = (f32[27,1024]{1,0:T(8,128)}, f32[27,1024]{1,0:T(8,128)S(1)}, u32[]{:S(2)}) copy-start(f32[27,1024]{1,0:T(8,128)S(1)} %reshape.2641) | copy-start | bytes 331780 | tf_op jit(solution)/shard_map/while
  492.8 49.2 %copy-start.13 = (f32[27,1024]{1,0:T(8,128)}, f32[27,1024]{1,0:T(8,128)S(1)}, u32[]{:S(2)}) copy-start(f32[27,1024]{1,0:T(8,128)S(1)} %reshape.2631) | copy-start | bytes 331780 | tf_op jit(solution)/shard_map/while
  650.2 34.8 %copy-start.74 = (f32[58,64]{1,0:T(8,128)S(1)}, f32[58,64]{1,0:T(8,128)}, u32[]{:S(2)}) copy-start(f32[58,64]{1,0:T(8,128)} %param.43) | copy-start | bytes 44548
  650.2 34.8 %copy-start.76 = (f32[1,58,64]{2,0,1:T(1,128)S(1)}, f32[1,58,64]{2,0,1:T(1,128)}, u32[]{:S(2)}) copy-start(f32[1,58,64]{2,0,1:T(1,128)} %param.35) | copy-start | bytes 44548
  652.1 51.5 %copy-start.95 = (f32[58,64]{1,0:T(8,128)S(1)}, f32[58,64]{1,0:T(8,128)}, u32[]{:S(2)}) copy-start(f32[58,64]{1,0:T(8,128)} %param.44) | copy-start | bytes 44548
  652.1 64.8 %copy-start.64 = (f32[1,512,64]{1,2,0:T(8,128)S(1)}, f32[1,512,64]{1,2,0:T(8,128)}, u32[]{:S(2)}) copy-start(f32[1,512,64]{1,2,0:T(8,128)} %param.32) | copy-start | bytes 393220
  652.1 64.8 %copy-start.65 = (f32[512,64]{0,1:T(8,128)S(1)}, f32[512,64]{0,1:T(8,128)}, u32[]{:S(2)}) copy-start(f32[512,64]{0,1:T(8,128)} %param.41) | copy-start | bytes 393220
  652.1 64.8 %copy-start.72 = (f32[1,512,64]{1,2,0:T(8,128)S(1)}, f32[1,512,64]{1,2,0:T(8,128)}, u32[]{:S(2)}) copy-start(f32[1,512,64]{1,2,0:T(8,128)} %param.34) | copy-start | bytes 393220
  652.1 64.8 %copy-start.73 = (f32[1,512,64]{1,2,0:T(8,128)S(1)}, f32[1,512,64]{1,2,0:T(8,128)}, u32[]{:S(2)}) copy-start(f32[1,512,64]{1,2,0:T(8,128)} %param.33) | copy-start | bytes 393220
  652.1 64.8 %reduce-scatter.5.cloned.1.call-start = ((), (), s32[]{:S(2)}) async-start(), calls=%async_computation.2 | async-start | bytes 1179648 | tf_op jit(solution)/shard_map/reduce_scatter | solution.py:195
  654.9 63.9 %copy-start.104 = (f32[4,3]{1,0:T(4,128)S(1)}, f32[4,3]{1,0:T(4,128)}, u32[]{:S(2)}) copy-start(f32[4,3]{1,0:T(4,128)} %param.46) | copy-start | bytes 148
  654.9 106.0 %copy-start.75 = (f32[512,64]{0,1:T(8,128)S(1)}, f32[512,64]{0,1:T(8,128)}, u32[]{:S(2)}) copy-start(f32[512,64]{0,1:T(8,128)} %param.42) | copy-start | bytes 393220
  654.9 107.7 %copy-start.1 = (f32[1,3]{1,0:T(1,128)S(1)}, f32[1,3]{1,0:T(1,128)}, u32[]{:S(2)}) copy-start(f32[1,3]{1,0:T(1,128)} %param.31) | copy-start | bytes 40
  654.9 106.0 %all-reduce.174.cloned.1.call-start = ((), (), s32[]{:S(2)}) async-start(), calls=%async_computation.3 | async-start | bytes 262144 | tf_op jit(solution)/shard_map/psum | solution.py:208
  (261 other events, 1655.0 us)
Sparse Core Ops, SparseCore 0:
  10.2 25.1 all-gather.3
  652.2 31.9 reduce-scatter.6
  686.6 30.3 reduce-scatter.4
  720.5 40.3 all-reduce.173
where the time goes:
time: 780 us; the launch traced here: 770 us
  matrix products  320 us (41%)
  local copies, waits for them, and re-layouts  200 us (26%)
  other arithmetic  84.3 us (11%)
  waiting for transfers between devices  59.6 us (8%)
  blocking collectives  50.4 us (6%)
  loops' own time  32.2 us (4%)
  between operations  23.8 us (3%)
    dot_general x33, matrix products, branch(): hidden_two = jnp.dot(second, act_one, precision=highest) + side[29][:, None]  177 us
    dot_general x30, matrix products, branch(): hidden_one = jnp.dot(first, stacked, precision=highest) + side[27][:, None]  73.8 us
    dot_general x27, matrix products, branch(): jnp.dot(last.reshape(COLORS * 9, HIDDEN_SIZE), act_two, precision=highest)  62.7 us
    psum x1, waiting for transfers between devices, on_device(): lax.psum((outers[0] - updated[0][0], outers[1] - updated[1][0], outers[2]...  41.5 us
    another operation x159, local copies, waits for them, and re-layouts, tap_shift(): padded[:, row_shift:row_shift + HEIGHT, col_shift:col_shift + WIDTH]  39.8 us
    reshape x96, local copies, waits for them, and re-layouts, tap_shift(): grid = field.reshape(channels, HEIGHT, WIDTH)  37.8 us
    another operation x1, loops' own time, run_images(): return lax.scan(visit, empty, (batch[0], batch[1], batch[2], series, keep))  32.2 us
    add x9, other arithmetic, visit(): running + weight * gradient  20.1 us
  transfers between devices with their start and end apart: 4, of which 3 were waited for; matrix products, arithmetic and copies ran while one was open for 3% of the time, Pallas kernels for 0%

commit v1 on v0

v1 whole, which is shorter than its diff:
```python
import functools

import jax, jax.numpy as jnp
from jax import lax
from jax.experimental import pallas as pl
from jax.experimental.pallas import tpu as pltpu
from jax.sharding import PartitionSpec as P

bf16, f32 = jnp.bfloat16, jnp.float32
HIGH = lax.Precision.HIGHEST
C, PX, TILE = 512, 1024, 512
CLIP = 0.98
LIP = 2.2


def dot_nn(a, b):
    return jnp.dot(a, b, preferred_element_type=f32)


def dot_tn(a, b):
    return lax.dot_general(a, b, (((0,), (0,)), ((), ())), preferred_element_type=f32)


def dot_nt(a, b):
    return lax.dot_general(a, b, (((1,), (1,)), ((), ())), preferred_element_type=f32)


def tap_masks():
    lane = lax.broadcasted_iota(jnp.int32, (8, PX), 1)
    row, col = lane // 32, lane % 32
    masks = []
    for tap in range(9):
        down, right = tap // 3 - 1, tap % 3 - 1
        ok = (row + down >= 0) & (row + down < 32) & (col + right >= 0) & (col + right < 32)
        masks.append(ok)
    return masks


def shift(field, tap, masks):
    if tap == 4:
        return field
    offset = (tap // 3 - 1) * 32 + tap % 3 - 1
    return jnp.where(masks[tap], pltpu.roll(field, (-offset) % PX, 1), 0.0)


def expand(field, flip, one, masks):
    high = field.astype(bf16).astype(f32)
    low = field - high
    row = lax.broadcasted_iota(jnp.int32, (8, PX), 0)
    base = jnp.where(row < 3, high, jnp.where(row < 6, pltpu.roll(low, 3, 0), one))
    parts = [shift(base, 8 - tap if flip else tap, masks) for tap in range(9)]
    return jnp.concatenate(parts + [jnp.zeros((8, PX), f32)], 0).astype(bf16)


def collapse(prod, flip, masks):
    total = prod[32:40]
    for tap in (0, 1, 2, 3, 5, 6, 7, 8):
        total = total + shift(prod[8 * tap : 8 * tap + 8], 8 - tap if flip else tap, masks)
    return total + pltpu.roll(total, 5, 0)


def pieces(h, slope_half):
    x = slope_half * h
    t = jnp.tanh(x)
    e = 1.0 - t * t
    return x, t, e


def softplus(raw):
    return jnp.maximum(raw, 0.0) + jnp.log1p(jnp.exp(-jnp.abs(raw)))


def sigmoid(raw):
    return 1.0 / (1.0 + jnp.exp(-raw))


def wide(ref, width):
    block = ref[...]
    return jnp.concatenate([block] * (width // 128), 1)


def to_column(row):
    return jnp.transpose(jnp.broadcast_to(row, (128, C)))


def prepare_side(side, lefts, out_left, stage, wa1, wp1, wa3, wp3, cols):
    rows = lax.broadcasted_iota(jnp.int32, (80, C), 0)
    stage[...] = jnp.zeros_like(stage)
    for color in range(3):
        for tap in range(9):
            stage[0, 8 * tap + color : 8 * tap + color + 1, :] = side[9 * color + tap : 9 * color + tap + 1, :]
            at = 31 + 9 * color + tap
            stage[1, 8 * tap + color : 8 * tap + color + 1, :] = side[at : at + 1, :]
    first = stage[0]
    u = lefts[0:1, :]
    right1 = jnp.sum(first * u, axis=1, keepdims=True)
    right1 = right1 / jnp.sqrt(jnp.sum(right1 * right1) + 1e-12)
    y1 = jnp.sum(first * right1, axis=0, keepdims=True)
    left1 = y1 / jnp.sqrt(jnp.sum(y1 * y1) + 1e-12)
    sigma1 = jnp.sum(left1 * y1)
    last = stage[1]
    inner = rows % 8
    weight = jnp.where(inner == 0, out_left[0], jnp.where(inner == 1, out_left[1], out_left[2]))
    mixed = jnp.where(inner < 3, last * weight, 0.0)
    right3 = mixed + pltpu.roll(mixed, 79, 0) + pltpu.roll(mixed, 78, 0)
    right3 = jnp.where(inner == 0, right3, 0.0)
    right3 = right3 / jnp.sqrt(jnp.sum(right3 * right3) + 1e-12)
    right3 = right3 + pltpu.roll(right3, 1, 0) + pltpu.roll(right3, 2, 0)
    prod = last * right3
    y3 = [jnp.sum(jnp.where(inner == k, prod, 0.0)) for k in range(3)]
    norm3 = jnp.sqrt(y3[0] * y3[0] + y3[1] * y3[1] + y3[2] * y3[2] + 1e-12)
    left3 = [value / norm3 for value in y3]
    sigma3 = left3[0] * y3[0] + left3[1] * y3[1] + left3[2] * y3[2]
    outer3 = jnp.where(inner == 0, left3[0], jnp.where(inner == 1, left3[1], left3[2])) * right3
    outer1 = right1 * left1
    q1, q3 = jnp.maximum(1.0, sigma1 / CLIP), jnp.maximum(1.0, sigma3 / CLIP)
    for at, q, wa, wp in ((0, q1, wa1, wp1), (1, q3, wa3, wp3)):
        scaled = stage[at] / (LIP * q)
        high = scaled.astype(bf16).astype(f32)
        low = scaled - high
        top = high + pltpu.roll(high, 3, 0)
        if at == 0:
            bias = side[27:28, :]
            bias_high = bias.astype(bf16).astype(f32)
            top = jnp.where(rows == 38, bias_high, jnp.where(rows == 39, bias - bias_high, top))
        wa[0:80, :] = top.astype(bf16)
        wa[80:160, :] = (low + pltpu.roll(low, 3, 0)).astype(bf16)
        wp[...] = (high + pltpu.roll(low, 3, 0)).astype(bf16)
    cols[0] = to_column(0.5 * softplus(side[28:29, :]))
    cols[1] = to_column(side[29:30, :])
    cols[2] = to_column(0.5 * softplus(side[30:31, :]))
    cols[3] = to_column(lefts[1:2, :])
    return (q1, sigma1, outer1), (q3, sigma3, outer3)


def prepare_mid(mid, cols, m_high, m_low):
    full = mid[...]
    right = jnp.sum(full * wide(cols.at[3], C), axis=0, keepdims=True)
    right = right / jnp.sqrt(jnp.sum(right * right) + 1e-12)
    y = jnp.sum(full * right, axis=1, keepdims=True)
    left = y / jnp.sqrt(jnp.sum(y * y) + 1e-12)
    sigma = jnp.sum(left * y)
    q = jnp.maximum(1.0, sigma / CLIP)
    scaled = full / (LIP * q)
    high = scaled.astype(bf16)
    m_high[...] = high
    m_low[...] = (scaled - high.astype(f32)).astype(bf16)
    return q, sigma, left, right


def correction(raw_grad, weight, q, sigma):
    ratio = sigma / CLIP
    active = jnp.where(ratio > 1.0, 1.0, jnp.where(ratio == 1.0, 0.5, 0.0))
    return 1.0 / (LIP * q), -active * jnp.sum(raw_grad * weight) / (LIP * q * q * CLIP)


def color_column(values):
    row = lax.broadcasted_iota(jnp.int32, (8, 1), 0)
    return jnp.where(row == 0, values[0], jnp.where(row == 1, values[1], values[2]))


PARTS = PX // TILE


def tile_at(image, part):
    if isinstance(image, int):
        return slice(image * PX + part * TILE, image * PX + (part + 1) * TILE)
    return pl.ds(pl.multiple_of(image * PX + part * TILE, TILE), TILE)


def each_image(body):
    lax.fori_loop(0, 2, lambda b, c: (body(b), c)[1], 0)


def compute(side, mid, lefts, out_left, tiny, live, images, probes, cotangents, s, o):
    side1, side3 = prepare_side(side, lefts, out_left, s["stage"], s["wa1"], s["wp1"], s["wa3"], s["wp3"], s["cols"])
    bias_col = color_column([tiny[0, k] for k in range(3)])
    shift_col = color_column([tiny[1, k] for k in range(3)])
    scale_col = jnp.exp(color_column([tiny[2, k] for k in range(3)]))
    slope_raw = color_column([tiny[3, k] for k in range(3)])
    slope0 = 0.5 * softplus(slope_raw)
    wa1, wp1, wa3, wp3 = s["wa1"], s["wp1"], s["wa3"], s["wp3"]
    slope1 = lambda: wide(s["cols"].at[0], TILE)
    bias2 = lambda: wide(s["cols"].at[1], TILE)
    slope2 = lambda: wide(s["cols"].at[2], TILE)
    valid = lambda: lax.broadcasted_iota(jnp.int32, (8, PX), 0) < 3
    s["small"][...] = jnp.zeros_like(s["small"])
    SZ, SP, SC, SD, SV, SN, SS, ST, SA, SB = range(10)

    def alive(b, step):
        row = live[pl.ds(b * 4 + step, 1), :]
        return jnp.concatenate([row] * (PX // 128), 1)

    def doubled(index, part):
        block = s["field"][index, :, part * TILE : (part + 1) * TILE]
        return jnp.concatenate([block, block], 0)

    def layer_one(b):
        masks = tap_masks()
        s["small"][SZ, b, 0:3] = images[b]
        s["small"][SP, b, 0:3] = probes[b]
        s["small"][SC, b, 0:3] = cotangents[b]
        field = (s["small"][SZ, b] + shift_col) * scale_col
        p = s["small"][SP, b]
        s["small"][SZ, b] = field
        x, t, e = pieces(field, slope0)
        d0 = 1.0 + t + x * e
        s["small"][SD, b] = d0
        s["field"][b] = expand(field + field * t, False, 1.0, masks)
        s["field"][2 + b] = expand(d0 * p, False, 0.0, masks)
        s["field"][4 + b] = expand(s["small"][SC, b], True, 0.0, masks)
        s["small"][SV, b] = p
        s["small"][SN, b] = -alive(b, 0) * p
        s["small"][SS, b] = alive(b, 0) * p
        for part in range(PARTS):
            at = tile_at(b, part)
            h = dot_tn(wa1[...], doubled(b, part))
            x, t, e = pieces(h, slope1())
            d = 1.0 + t + x * e
            dh = dot_tn(wa1[...], doubled(2 + b, part))
            s["h1"][:, at] = h
            s["g1"][:, at] = dh
            s["d1"][:, at] = d.astype(bf16)
            s["a1"][:, at] = (h + h * t).astype(bf16)
            s["b1"][:, at] = (d * dh).astype(bf16)

    each_image(layer_one)
    q2, sigma2, left2, right2 = prepare_mid(mid, s["cols"], s["mh"], s["ml"])

    def layer_two(b):
        masks = tap_masks()
        prods, dprods = [], []
        for part in range(PARTS):
            at = tile_at(b, part)
            a1 = s["a1"][:, at]
            h = dot_nn(s["mh"][...], a1) + dot_nn(s["ml"][...], a1) + bias2()
            x, t, e = pieces(h, slope2())
            d = 1.0 + t + x * e
            dh = dot_nn(s["mh"][...], s["b1"][:, at])
            s["h2"][:, at] = h
            s["g2"][:, at] = dh
            s["d2"][:, at] = d.astype(bf16)
            a2 = (h + h * t).astype(bf16)
            b2 = (d * dh).astype(bf16)
            s["a2"][:, at] = a2
            s["b2"][:, at] = b2
            prods.append(dot_nn(wp3[...], a2))
            dprods.append(dot_nn(wp3[...], b2))
        g = collapse(jnp.concatenate(prods, 1), False, masks)
        o["flow"][b] = (s["small"][SZ, b] + g + bias_col)[0:3]
        s["small"][ST, b] = jnp.where(valid(), collapse(jnp.concatenate(dprods, 1), False, masks), 0.0)

    each_image(layer_two)

    def pull(step, sign):
        masks = tap_masks()
        for b in range(2):
            spread = expand(s["small"][SV, b], True, 0.0, masks)
            prods = []
            for part in range(PARTS):
                at = tile_at(b, part)
                block = spread[:, part * TILE : (part + 1) * TILE]
                u2 = dot_tn(wa3[...], jnp.concatenate([block, block], 0)).astype(bf16) * s["d2"][:, at]
                u1 = dot_tn(s["mh"][...], u2).astype(bf16) * s["d1"][:, at]
                prods.append(dot_nn(wp1[...], u1))
            v = jnp.where(valid(), s["small"][SD, b] * collapse(jnp.concatenate(prods, 1), True, masks), 0.0)
            on = sign * alive(b, step + 1)
            s["small"][SV, b] = v
            s["small"][SN, b] = s["small"][SN, b] - on * v
            s["small"][SS, b] = s["small"][SS, b] + (on / (step + 2).astype(f32)) * v
        return -sign

    lax.fori_loop(0, 3, pull, jnp.float32(-1.0))
    s["sums"][...] = jnp.zeros_like(s["sums"])

    def back_two(b):
        masks = tap_masks()
        s["field"][6 + b] = expand(s["small"][SN, b], True, 0.0, masks)
        slope_sum, bias_sum = s["sums"][1], s["sums"][0]
        for part in range(PARTS):
            at = tile_at(b, part)
            h = s["h2"][:, at]
            sl = slope2()
            x, t, e = pieces(h, sl)
            d = 1.0 + t + x * e
            c_a = dot_tn(wa3[...], doubled(4 + b, part))
            t_a = dot_tn(wa3[...], doubled(6 + b, part))
            q = (2.0 * e * (1.0 - x * t)) * s["g2"][:, at] * t_a
            c_h = d * c_a + sl * q
            grad = h * (c_a * h * e + q)
            for k in range(TILE // 128):
                slope_sum = slope_sum + grad[:, k * 128 : (k + 1) * 128]
                bias_sum = bias_sum + c_h[:, k * 128 : (k + 1) * 128]
            s["c2"][:, at] = c_h.astype(bf16)
            s["t2"][:, at] = (d * t_a).astype(bf16)
        s["sums"][1] = slope_sum
        s["sums"][0] = bias_sum

    each_image(back_two)
    raw = dot_nt(s["c2"][...], s["a1"][...]) + dot_nt(s["t2"][...], s["b1"][...])
    straight, across = correction(raw, mid[...], q2, sigma2)
    o["mid"][...] = straight * raw + (across * left2) * right2
    g3 = dot_nt(s["field"][4], s["a2"][:, 0:PX]) + dot_nt(s["field"][6], s["b2"][:, 0:PX])
    s["stage2"][1] = g3 + dot_nt(s["field"][5], s["a2"][:, PX:]) + dot_nt(s["field"][7], s["b2"][:, PX:])

    def back_one(b):
        masks = tap_masks()
        slope_sum = s["sums"][2]
        prods, dprods = [], []
        for part in range(PARTS):
            at = tile_at(b, part)
            h = s["h1"][:, at]
            sl = slope1()
            x, t, e = pieces(h, sl)
            d = 1.0 + t + x * e
            c2 = s["c2"][:, at]
            c_a = dot_tn(s["mh"][...], c2) + dot_tn(s["ml"][...], c2)
            t_a = dot_tn(s["mh"][...], s["t2"][:, at])
            q = (2.0 * e * (1.0 - x * t)) * s["g1"][:, at] * t_a
            c_h = (d * c_a + sl * q).astype(bf16)
            t_h = (d * t_a).astype(bf16)
            grad = h * (c_a * h * e + q)
            for k in range(TILE // 128):
                slope_sum = slope_sum + grad[:, k * 128 : (k + 1) * 128]
            prods.append(dot_nn(wp1[...], c_h))
            dprods.append(dot_nn(wp1[...], t_h))
            s["a2"][:, at] = c_h
            s["b2"][:, at] = t_h
        s["sums"][2] = slope_sum
        s["small"][SA, b] = collapse(jnp.concatenate(prods, 1), True, masks)
        s["small"][SB, b] = collapse(jnp.concatenate(dprods, 1), True, masks)

    each_image(back_one)
    g1 = dot_nt(s["field"][0], s["a2"][:, 0:PX]) + dot_nt(s["field"][2], s["b2"][:, 0:PX])
    g1 = g1 + dot_nt(s["field"][1], s["a2"][:, PX:]) + dot_nt(s["field"][3], s["b2"][:, PX:])
    g3 = s["stage2"][1]
    lane = lax.broadcasted_iota(jnp.int32, (8, 128), 1)
    sub = lax.broadcasted_iota(jnp.int32, (8, 128), 0)
    total_scale = tiny[2, 0] + tiny[2, 1] + tiny[2, 2]
    tile = jnp.zeros((8, 128), f32)
    for b in range(2):
        field, p, cot = s["small"][SZ, b], s["small"][SP, b], s["small"][SC, b]
        c_a, t_a = s["small"][SA, b], s["small"][SB, b]
        x, t, e = pieces(field, slope0)
        q = 2.0 * e * (1.0 - x * t) * p * t_a
        c_z = jnp.where(valid(), cot + (1.0 + t + x * e) * c_a + slope0 * q, 0.0)
        slope_grad = jnp.where(valid(), field * (c_a * field * e + q), 0.0)
        o["back"][b] = (c_z * scale_col)[0:3]
        sums = [
            jnp.sum(cot, axis=1, keepdims=True),
            jnp.sum(c_z, axis=1, keepdims=True) * scale_col,
            jnp.sum(c_z * field, axis=1, keepdims=True) - 1024.0,
            jnp.sum(slope_grad, axis=1, keepdims=True) * (0.5 * sigmoid(slope_raw)),
        ]
        for r in range(4):
            tile = tile + jnp.where((lane == r) & (sub < 3), sums[r], 0.0)
        log_part = (1024.0 * total_scale + jnp.sum(s["small"][SS, b] * s["small"][ST, b])) / 3072.0
        tile = tile + jnp.where((lane == 4) & (sub == b), log_part, 0.0)
    eye = (sub == lane).astype(f32)
    flipped = lax.dot_general(tile, eye, (((0,), (0,)), ((), ())), precision=HIGH, preferred_element_type=f32)
    o["tiny"][...] = flipped[0:8]
    ones = jnp.ones((8, 128), f32)
    lanes_to_row = lambda acc: lax.dot_general(ones, acc, (((1,), (1,)), ((), ())), precision=HIGH, preferred_element_type=f32)[0:1]
    o["side"][27:28, :] = g1[38:39]
    o["side"][28:29, :] = lanes_to_row(s["sums"][2]) * (0.5 * sigmoid(side[28:29, :]))
    o["side"][29:30, :] = lanes_to_row(s["sums"][0])
    o["side"][30:31, :] = lanes_to_row(s["sums"][1]) * (0.5 * sigmoid(side[30:31, :]))
    o["side"][58:64, :] = jnp.zeros((6, C), f32)
    inner = lax.broadcasted_iota(jnp.int32, (80, C), 0) % 8
    for at, (q, sigma, outer), raw, start in ((0, side1, g1, 0), (1, side3, g3, 31)):
        joined = jnp.where(inner < 3, raw + pltpu.roll(raw, 77, 0), 0.0)
        joined = jnp.where(lax.broadcasted_iota(jnp.int32, (80, C), 0) < 72, joined, 0.0)
        straight, across = correction(joined, s["stage"][at], q, sigma)
        s["stage2"][at] = straight * joined + across * outer
        for color in range(3):
            for tap in range(9):
                to = start + 9 * color + tap
                o["side"][to : to + 1, :] = s["stage2"][at, 8 * tap + color : 8 * tap + color + 1, :]


def big(dtype):
    return pltpu.VMEM((C, 2 * PX), dtype)


SCRATCH = dict(
    stage=pltpu.VMEM((2, 80, C), f32),
    stage2=pltpu.VMEM((2, 80, C), f32),
    wa1=pltpu.VMEM((160, C), bf16),
    wp1=pltpu.VMEM((80, C), bf16),
    wa3=pltpu.VMEM((160, C), bf16),
    wp3=pltpu.VMEM((80, C), bf16),
    cols=pltpu.VMEM((4, C, 128), f32),
    small=pltpu.VMEM((10, 2, 8, PX), f32),
    sums=pltpu.VMEM((3, C, 128), f32),
    field=pltpu.VMEM((8, 80, PX), bf16),
    mh=pltpu.VMEM((C, C), bf16),
    ml=pltpu.VMEM((C, C), bf16),
    h1=big(f32), g1=big(f32), h2=big(f32), g2=big(f32),
    d1=big(bf16), a1=big(bf16), b1=big(bf16),
    d2=big(bf16), a2=big(bf16), b2=big(bf16),
    c2=big(bf16), t2=big(bf16),
)
NAMES = list(SCRATCH)


def kernel(side, mid, lefts, out_left, tiny, live, images, probes, cotangents, flow, back, mid_grad, side_grad, tiny_out, *scratch):
    s = dict(zip(NAMES, scratch))
    o = dict(flow=flow, back=back, mid=mid_grad, side=side_grad, tiny=tiny_out)
    ol = [out_left[0, k] for k in range(3)]
    compute(side, mid, lefts, ol, tiny, live, images, probes, cotangents, s, o)


def core(side, mid, lefts, out_left, tiny, live, images, probes, cotangents):
    vm = pl.BlockSpec(memory_space=pltpu.VMEM)
    sm = pl.BlockSpec(memory_space=pltpu.SMEM)
    sd = jax.ShapeDtypeStruct
    return pl.pallas_call(
        kernel,
        in_specs=[vm, vm, vm, sm, sm, vm, vm, vm, vm],
        out_specs=[vm] * 5,
        out_shape=[sd((2, 3, PX), f32), sd((2, 3, PX), f32), sd((C, C), f32), sd((64, C), f32), sd((8, 128), f32)],
        scratch_shapes=list(SCRATCH.values()),
        compiler_params=pltpu.CompilerParams(vmem_limit_bytes=60 << 20),
    )(side, mid, lefts, out_left, tiny, live, images, probes, cotangents)


MESH = pl.DeviceIdType.MESH


def scale_sizes(n):
    w = C // n
    fold = 128 // w
    return w, fold, C // fold, 64 // fold


def pack(block, fold):
    rows = block.shape[0] // fold
    return jnp.concatenate([block[i * rows : (i + 1) * rows] for i in range(fold)], 1)


def unpack(block, fold):
    w = 128 // fold
    return jnp.concatenate([block[:, i * w : (i + 1) * w] for i in range(fold)], 0)


def spread_rows(blocks, fold):
    w = 128 // fold
    return [jnp.concatenate([block[:, i * w : (i + 1) * w] for block in blocks], 1) for i in range(fold)]


class Gather:
    def __init__(self, n, buf, sems):
        self.n, self.m, self.buf, self.sems = n, n // 2, buf, sems
        self.me = lax.axis_index("dp")
        self.chip, self.core = self.me // 2, self.me % 2
        self.pair = self.me + 1 - 2 * self.core

    def copy(self, slot, sem, target):
        return pltpu.make_async_remote_copy(
            src_ref=self.buf.at[slot],
            dst_ref=self.buf.at[slot],
            send_sem=self.sems.at[0, sem],
            recv_sem=self.sems.at[1, sem],
            device_id={"dp": target},
            device_id_type=MESH,
        )

    def peer(self, j):
        return lax.rem(self.chip + j, self.m) * 2 + self.core

    def start(self):
        for j in range(1, self.m):
            self.copy(self.me, j, self.peer(j)).start()
        self.copy(self.me, self.m, self.pair).start()

    def forward(self):
        for j in range(1, self.m):
            source = self.peer(j)
            self.copy(source, self.m - j, source).wait_recv()
            self.copy(source, self.m + j, self.pair).start()

    def finish(self):
        for j in range(self.m):
            self.copy(self.me, self.m + j, self.pair).wait_recv()
        for j in range(1, 2 * self.m):
            self.copy(self.me, j, self.pair).wait_send()


def barrier(n, groups):
    me, grp = lax.axis_index("dp"), lax.axis_index("grp")
    sem = pltpu.get_barrier_semaphore()
    m = n // 2
    chip, core = me // 2, me % 2
    for j in range(1, m):
        pl.semaphore_signal(sem, inc=1, device_id={"dp": lax.rem(chip + j, m) * 2 + core}, device_id_type=MESH)
    pl.semaphore_signal(sem, inc=1, device_id={"dp": me + 1 - 2 * core}, device_id_type=MESH)
    for j in range(1, groups):
        pl.semaphore_signal(sem, inc=1, device_id={"grp": lax.rem(grp + j, groups)}, device_id_type=MESH)
    pl.semaphore_wait(sem, m + groups - 1)


def put_chunks(ref, lead, base, field):
    rows = field.shape[0]
    for k in range(8):
        ref[lead, base + k * rows : base + (k + 1) * rows, :] = field[:, k * 128 : (k + 1) * 128]


def get_chunks(block, base, rows):
    return jnp.concatenate([block[base + k * rows : base + (k + 1) * rows] for k in range(8)], 1)


def match(counts, me, wanted_mine, wanted_theirs):
    n = len(counts)
    zero = jnp.zeros((1, 128), f32)
    mine, my_rank = zero, zero
    for d in range(n):
        hit = jnp.where(counts[d] == wanted_mine, 1.0, 0.0)
        my_rank = my_rank + jnp.where(d < me, hit, zero)
        mine = mine + jnp.where(d == me, hit, zero)
    rank, masks = zero, []
    for d in range(n):
        hit = jnp.where(counts[d] == wanted_theirs, 1.0, 0.0)
        masks.append(jnp.where(rank == my_rank, hit * mine, zero))
        rank = rank + hit
    return masks


def gather_kernel(n, groups, mid_w, side_w, images, probes, cotangents, counts, terms,
                  mid, side, im, pr, co, live, early, late, early_sem, late_sem):
    w, fold, mid_rows, side_rows = scale_sizes(n)
    me = lax.axis_index("dp")
    first, second = Gather(n, early, early_sem), Gather(n, late, late_sem)
    early[me, 0:side_rows, :] = pack(jnp.concatenate([side_w[...], jnp.zeros((6, w), f32)], 0), fold)
    third = jnp.concatenate([images[2], probes[2], cotangents[2]], 0)
    put_chunks(early, me, side_rows, third)
    lane = lax.broadcasted_iota(jnp.int32, (8, 128), 1)
    meta = jnp.where(lane == 0, counts[0, 0].astype(f32), terms[0, 2].astype(f32))
    early[me, side_rows + 72 : side_rows + 80, :] = meta
    late[me] = pack(mid_w[...], fold)
    barrier(n, groups)
    first.start()
    second.start()
    first.forward()
    first.finish()
    blocks = [early[d] for d in range(n)]
    rows = spread_rows([block[0:side_rows] for block in blocks], fold)
    for i in range(fold):
        side[i * side_rows : (i + 1) * side_rows, :] = rows[i]
    metas = [block[side_rows + 72 : side_rows + 73] for block in blocks]
    count_rows = [jnp.broadcast_to(meta[:, 0:1], (1, 128)) for meta in metas]
    term_rows = [jnp.broadcast_to(meta[:, 1:2], (1, 128)) for meta in metas]
    masks = match(count_rows, me, 1.0, 3.0)
    picked, term = jnp.zeros((72, 128), f32), jnp.zeros((1, 128), f32)
    helper = jnp.zeros((1, 128), f32)
    for d in range(n):
        picked = jnp.where(masks[d] > 0.0, blocks[d][side_rows : side_rows + 72], picked)
        term = jnp.where(masks[d] > 0.0, term_rows[d], term)
        helper = helper + masks[d]
    other = get_chunks(picked, 0, 9)
    wide_helper = jnp.concatenate([helper] * 8, 1)
    for at, (out, own) in enumerate(((im, images), (pr, probes), (co, cotangents))):
        out[0] = own[0]
        out[1] = jnp.where(wide_helper > 0.0, other[3 * at : 3 * at + 3], own[1])
    sub = lax.broadcasted_iota(jnp.int32, (8, 128), 0)
    second_term = jnp.where(helper > 0.0, term, terms[0, 1].astype(f32))
    limit = jnp.where(sub < 4, terms[0, 0].astype(f32), second_term)
    live[...] = jnp.where(limit > (sub % 4).astype(f32), 1.0, 0.0)
    second.forward()
    second.finish()
    rows = spread_rows([late[d] for d in range(n)], fold)
    for i in range(fold):
        mid[i * mid_rows : (i + 1) * mid_rows, :] = rows[i]


def adam(weight, gradient, first, second, rate):
    first = 0.9 * first + (1.0 - 0.9) * gradient
    second = 0.999 * second + (1.0 - 0.999) * gradient * gradient
    first_hat = first / (1.0 - 0.9**5.0)
    second_hat = second / (1.0 - 0.999**5.0)
    return weight - rate * (first_hat / (jnp.sqrt(second_hat) + 1e-8) + 0.01 * weight), first, second


def update_kernel(n, groups, mid_grad, side_grad, tiny_grad, flow_in, back_in, counts,
                  mid_w, mid_f, mid_s, side_w, side_f, side_s, tiny_w, tiny_f, tiny_s,
                  mid_o, mid_m, side_o, side_m, tiny_o, tiny_m,
                  flow, back, log_det, log_mean, mid_f_new, mid_s_new, mid_new, side_f_new, side_s_new, side_new,
                  tiny_f_new, tiny_s_new, slope_s_new, tiny_new, mid_d, mid_m_new, mid_o_new,
                  side_d, side_m_new, side_o_new, tiny_d, tiny_m_new, tiny_o_new,
                  to_pair, from_pair, chipsum, from_chips, results, quarters, whole, summed, tinies,
                  pair_sem, chip_sem, result_sem, quarter_sem, whole_sem, tiny_sem):
    w, fold, mid_rows, side_rows = scale_sizes(n)
    rows = mid_rows + side_rows
    m = n // 2
    me, grp = lax.axis_index("dp"), lax.axis_index("grp")
    chip, core = me // 2, me % 2
    pair = me + 1 - 2 * core
    share = Gather(n, results, result_sem)
    for k in range(m):
        packs = []
        for c in range(2):
            at = (2 * k + c) * w
            packs.append(jnp.concatenate([pack(mid_grad[:, at : at + w], fold), pack(side_grad[:, at : at + w], fold)], 0))
        to_pair[k] = jnp.where(core == 0, packs[1], packs[0])
        chipsum[k] = jnp.where(core == 0, packs[0], packs[1])
    put_chunks(results, me, 0, jnp.concatenate([flow_in[1], back_in[1]], 0))
    tile = tiny_grad[...]
    sub = lax.broadcasted_iota(jnp.int32, (8, 128), 0)
    results[me, 48:56, :] = jnp.where(sub == 5, counts[0, 0].astype(f32), tile)
    barrier(n, groups)
    swap = pltpu.make_async_remote_copy(
        src_ref=to_pair, dst_ref=from_pair, send_sem=pair_sem.at[0], recv_sem=pair_sem.at[1],
        device_id={"dp": pair}, device_id_type=MESH)
    swap.start()
    share.start()
    swap.wait_recv()
    for k in range(m):
        chipsum[k] = chipsum[k] + from_pair[k]

    def chip_copy(source, slot, j, target):
        return pltpu.make_async_remote_copy(
            src_ref=chipsum.at[source], dst_ref=from_chips.at[slot], send_sem=chip_sem.at[0, j], recv_sem=chip_sem.at[1, j],
            device_id={"dp": target}, device_id_type=MESH)

    for j in range(1, m):
        to = lax.rem(chip + j, m)
        chip_copy(to, j, j, to * 2 + core).start()
    share.forward()
    total = chipsum[chip]
    for j in range(1, m):
        chip_copy(chip, j, j, pair).wait_recv()
        total = total + from_chips[j]
    grad = total / (2.0 * n)
    mid_g, side_g = unpack(grad[0:mid_rows], fold), unpack(grad[mid_rows:rows], fold)[0:58]
    new, first, second = adam(mid_w[...], mid_g, mid_f[...], mid_s[...], 0.01)
    mid_f_new[...], mid_s_new[...], mid_new[...] = first, second, new
    mid_diff = mid_o[...] - new
    at = lax.broadcasted_iota(jnp.int32, (58, w), 0)
    new, first, second = adam(side_w[...], side_g, side_f[...], side_s[...], jnp.where(at >= 31, 0.004, 0.05))
    side_f_new[...], side_s_new[...], side_new[...] = first, second, new
    side_diff = jnp.concatenate([side_o[...] - new, jnp.zeros((6, w), f32)], 0)
    whole[0:mid_rows, :] = pack(mid_diff, fold)
    whole[mid_rows:rows, :] = pack(side_diff, fold)
    if whole.shape[0] > rows:
        whole[rows:, :] = jnp.zeros((whole.shape[0] - rows, 128), f32)
    piece = whole.shape[0] // groups

    def part(index):
        return pl.ds(pl.multiple_of(index * piece, 8), piece)

    def quarter_copy(index, j, target):
        return pltpu.make_async_remote_copy(
            src_ref=whole.at[part(index)], dst_ref=quarters.at[grp], send_sem=quarter_sem.at[0, j], recv_sem=quarter_sem.at[1, j],
            device_id={"grp": target}, device_id_type=MESH)

    for j in range(1, groups):
        to = lax.rem(grp + j, groups)
        quarter_copy(to, j, to).start()
    quarters[grp] = whole[part(grp), :]
    share.finish()
    blocks = [results[d] for d in range(n)]
    tiny_sum = blocks[0][48:56]
    for d in range(1, n):
        tiny_sum = tiny_sum + blocks[d][48:56]
    tiny_new_v, tiny_first, tiny_second = adam(tiny_w[...], tiny_sum[0:4, 0:3] / (2.0 * n), tiny_f[...], tiny_s[...], 0.05)
    tiny_f_new[...], tiny_new[...] = tiny_first, tiny_new_v
    tiny_s_new[...] = tiny_second[0:3]
    slope_s_new[...] = tiny_second[3:4]
    log_mean[...] = (tiny_sum[4:5, 0:1] + tiny_sum[4:5, 1:2]) / (2.0 * n)
    tinies[grp] = jnp.zeros((8, 128), f32)
    tinies[grp, 0:4, 0:3] = tiny_o[...] - tiny_new_v

    def tiny_copy(j, target):
        return pltpu.make_async_remote_copy(
            src_ref=tinies.at[grp], dst_ref=tinies.at[grp], send_sem=tiny_sem.at[0, j], recv_sem=tiny_sem.at[1, j],
            device_id={"grp": target}, device_id_type=MESH)

    for j in range(1, groups):
        tiny_copy(j, lax.rem(grp + j, groups)).start()
    for j in range(1, groups):
        quarter_copy(grp, j, grp).wait_recv()
    acc = quarters[0]
    for k in range(1, groups):
        acc = acc + quarters[k]
    summed[part(grp), :] = acc

    def whole_copy(j, target):
        return pltpu.make_async_remote_copy(
            src_ref=summed.at[part(grp)], dst_ref=summed.at[part(grp)], send_sem=whole_sem.at[0, j], recv_sem=whole_sem.at[1, j],
            device_id={"grp": target}, device_id_type=MESH)

    for j in range(1, groups):
        whole_copy(j, lax.rem(grp + j, groups)).start()
    count_rows = [jnp.broadcast_to(block[53:54, 0:1], (1, 128)) for block in blocks]
    masks = match(count_rows, me, 3.0, 1.0)
    picked, log_third = jnp.zeros((48, 128), f32), jnp.zeros((1, 128), f32)
    own_count = jnp.zeros((1, 128), f32) + counts[0, 0].astype(f32)
    for d in range(n):
        picked = jnp.where(masks[d] > 0.0, blocks[d][0:48], picked)
        log_third = jnp.where(masks[d] > 0.0, jnp.broadcast_to(blocks[d][52:53, 1:2], (1, 128)), log_third)
    other = get_chunks(picked, 0, 6)
    has_two = jnp.concatenate([own_count] * 8, 1) > 1.5
    for out, own, base in ((flow, flow_in, 0), (back, back_in, 3)):
        out[0] = own[0]
        out[1] = jnp.where(has_two, own[1], 0.0)
        out[2] = other[base : base + 3]
    lane = lax.broadcasted_iota(jnp.int32, (1, 128), 1)
    own_logs = tile[4:5]
    logs = jnp.where(lane == 0, own_logs, jnp.where(lane == 1, jnp.where(own_count > 1.5, own_logs, 0.0), log_third))
    log_det[...] = logs[:, 0:3]
    for j in range(1, groups):
        tiny_copy(j, grp).wait_recv()
    tiny_total = tinies[0]
    for k in range(1, groups):
        tiny_total = tiny_total + tinies[k]

    def outer(diff, o, mom, d_out, m_out, o_out):
        delta = diff / groups
        mom_new = 0.9 * mom[...] + delta
        d_out[...], m_out[...] = delta, mom_new
        o_out[...] = o[...] - 0.7 * (delta + 0.9 * mom_new)

    outer(tiny_total[0:4, 0:3], tiny_o, tiny_m, tiny_d, tiny_m_new, tiny_o_new)
    for j in range(1, groups):
        whole_copy(j, grp).wait_recv()
    outer(unpack(summed[0:mid_rows, :], fold), mid_o, mid_m, mid_d, mid_m_new, mid_o_new)
    outer(unpack(summed[mid_rows:rows, :], fold)[0:58], side_o, side_m, side_d, side_m_new, side_o_new)
    swap.wait_send()
    for j in range(1, m):
        chip_copy(chip, j, j, pair).wait_send()
    for j in range(1, groups):
        quarter_copy(grp, j, grp).wait_send()
        whole_copy(j, grp).wait_send()
        tiny_copy(j, grp).wait_send()


def on_device(images, probes, out_cotangent, counts, terms, power_left, power_out, mid_weight, mid_first, mid_second,
              side_weight, side_first, side_second, tiny_weight, tiny_first, tiny_second,
              mid_outer, mid_momentum, side_outer, side_momentum, tiny_outer, tiny_momentum):
    n, groups = lax.axis_size("dp"), lax.axis_size("grp")
    w, fold, mid_rows, side_rows = scale_sizes(n)
    rows = mid_rows + side_rows
    padded = -(-rows // (8 * groups)) * 8 * groups
    vm = pl.BlockSpec(memory_space=pltpu.VMEM)
    sm = pl.BlockSpec(memory_space=pltpu.SMEM)
    sd = lambda *shape: jax.ShapeDtypeStruct(shape, f32)
    dma = lambda *shape: pltpu.SemaphoreType.DMA(shape)
    mid, side, im, pr, co, live = pl.pallas_call(
        functools.partial(gather_kernel, n, groups),
        in_specs=[vm] * 5 + [sm] * 2,
        out_specs=[vm] * 6,
        out_shape=[sd(C, C), sd(64, C), sd(2, 3, PX), sd(2, 3, PX), sd(2, 3, PX), sd(8, 128)],
        scratch_shapes=[
            pltpu.VMEM((n, side_rows + 80, 128), f32),
            pltpu.VMEM((n, mid_rows, 128), f32),
            dma(2, n), dma(2, n),
        ],
        compiler_params=pltpu.CompilerParams(vmem_limit_bytes=60 << 20, collective_id=0, has_side_effects=True),
    )(mid_weight[0], side_weight[0], images[0], probes[0], out_cotangent[0], counts, terms)
    flow, back, mid_grad, side_grad, tiny_grad = core(side, mid, power_left[0], power_out, tiny_weight[0], live, im, pr, co)
    small = [sd(3, 3, PX), sd(3, 3, PX), sd(1, 3), sd(1, 1)]
    shard = [sd(C, w)] * 3 + [sd(58, w)] * 3
    outs = pl.pallas_call(
        functools.partial(update_kernel, n, groups),
        in_specs=[vm] * 5 + [sm] + [vm] * 15,
        out_specs=[vm] * 23,
        out_shape=small + shard + [sd(4, 3), sd(3, 3), sd(1, 3), sd(4, 3)] + shard + [sd(4, 3)] * 3,
        scratch_shapes=[
            pltpu.VMEM((n // 2, rows, 128), f32),
            pltpu.VMEM((n // 2, rows, 128), f32),
            pltpu.VMEM((n // 2, rows, 128), f32),
            pltpu.VMEM((n // 2, rows, 128), f32),
            pltpu.VMEM((n, 56, 128), f32),
            pltpu.VMEM((groups, padded // groups, 128), f32),
            pltpu.VMEM((padded, 128), f32),
            pltpu.VMEM((padded, 128), f32),
            pltpu.VMEM((groups, 8, 128), f32),
            dma(2), dma(2, n // 2), dma(2, n), dma(2, groups), dma(2, groups), dma(2, groups),
        ],
        compiler_params=pltpu.CompilerParams(vmem_limit_bytes=60 << 20, collective_id=1, has_side_effects=True),
    )(mid_grad, side_grad, tiny_grad, flow, back, counts,
      mid_weight[0], mid_first[0], mid_second[0], side_weight[0], side_first[0], side_second[0],
      tiny_weight[0], tiny_first[0], tiny_second[0],
      mid_outer, mid_momentum, side_outer, side_momentum, tiny_outer, tiny_momentum)
    outs = list(outs)
    outs[3] = outs[3].reshape(1)
    for k in (0, 1) + tuple(range(4, 12)) + (13,):
        outs[k] = outs[k][None]
    return tuple(outs)


def solution(mesh):
    split = P("grp", None, "dp")
    group = P("grp", None, None)
    image = P("grp", "dp", None, None)
    return jax.shard_map(
        on_device,
        mesh=mesh,
        in_specs=(image, image, image, P("grp", "dp"), P("grp", "dp"), group, P("grp", None),
                  split, split, split, split, split, split, group, group, group,
                  P(None, "dp"), P(None, "dp"), P(None, "dp"), P(None, "dp"), P(), P()),
        out_specs=(image, image, P("grp", "dp"), P("grp"), split, split, split, split, split, split,
                   group, group, P("grp", None), group) + (P(None, "dp"),) * 6 + (P(), P(), P()),
        check_vma=False,
    )
```

time: 780 us -> 129 us (0.17)
  matrix products: 320 us -> 0 us
  local copies, waits for them, and re-layouts: 200 us -> 30.5 us
  Pallas kernels: 0 us -> 93 us
  other arithmetic: 84.3 us -> 0 us
  waiting for transfers between devices: 59.6 us -> 0 us
  blocking collectives: 50.4 us -> 0 us
  loops' own time: 32.2 us -> 0 us
  between operations: 23.8 us -> 3.22 us
    dot_general x96 -> x0, matrix products: 320 us -> none  [the longest x33 177 us: branch(): hidden_two = jnp.dot(second, act_one, precision=highest) + side[29][:, None]]
    pallas_call x0 -> x3, Pallas kernels: none -> 93 us  [the longest x1 38.6 us: core(): pl.pallas_call(kernel, in_specs=[vm, vm, vm, sm, sm, vm, vm, vm, vm], out...]
    reshape x364 -> x0, local copies, waits for them, and re-layouts: 70.3 us -> none  [the longest x96 37.8 us: tap_shift(): grid = field.reshape(channels, HEIGHT, WIDTH)]
    another operation x183 -> x0, local copies, waits for them, and re-layouts: 53.6 us -> none  [the longest x159 39.8 us: tap_shift(): padded[:, row_shift:row_shift + HEIGHT, col_shift:col_shift + WIDTH]]
    psum x1 -> x0, waiting for transfers between devices: 41.5 us -> none  [on_device(): lax.psum((outers[0] - updated[0][0], outers[1] - updated[1][0], outers[2]...]
    psum x2 -> x0, blocking collectives: 34.5 us -> none  [the longest x1 18 us: on_device(): tiny_grad, log_sum = lax.psum((totals[2], log_local), 'dp')]
    another operation x1 -> x0, loops' own time: 32.2 us -> none  [run_images(): return lax.scan(visit, empty, (batch[0], batch[1], batch[2], series, keep))]
    add x15 -> x0, other arithmetic: 21 us -> none  [the longest x9 20.1 us: visit(): running + weight * gradient]
  transfers between devices with their start and end apart: 4 -> 0, of which waited for: 3 -> 0; matrix products, arithmetic and copies ran while one was open for 3% -> 0% of each run, Pallas kernels for 0% -> 0%
where the time goes in v1:
time: 129 us; the launch traced here: 127 us
  Pallas kernels  93 us (72%)
  local copies, waits for them, and re-layouts  30.5 us (24%)
  between operations  3.22 us (2%)
    pallas_call x1, Pallas kernels, core(): pl.pallas_call(kernel, in_specs=[vm, vm, vm, sm, sm, vm, vm, vm, vm], out...  38.6 us
    unnamed x92, local copies, waits for them, and re-layouts  30.5 us
    pallas_call x1, Pallas kernels, on_device(): pl.pallas_call(functools.partial(update_kernel, n, groups), in_specs=[vm]...  29.2 us
    pallas_call x1, Pallas kernels, on_device(): pl.pallas_call(functools.partial(gather_kernel, n, groups), in_specs=[vm]...  25.3 us

profile of v1, /device:TPU:0, one launch (start us, length us, event | category | flops | bytes accessed | tf_op | source)
XLA Modules:
  0.0 126.8 jit_solution(12887464043342041014)
XLA Ops:
  1.3 0.7 copy.46
  2.0 0.7 copy-done.25
  2.7 0.7 copy.49
  3.4 0.7 copy.50
  4.0 1.4 %copy.80 = f32[1,58,64]{2,1,0:T(8,128)} copy(f32[1,58,64]{2,0,1:T(1,128)} %param.32) | data formatting | bytes 29696
  5.4 0.6 copy.79
  6.2 0.6 copy_bitcast_fusion.3
  6.8 0.7 copy_bitcast_fusion
  7.5 0.8 copy.45
  8.4 0.9 copy.47
  9.3 0.8 copy.48
  10.2 0.8 copy.51.mid_o
  11.1 0.8 copy.52.mid_m
  11.9 25.3 %shard_map.389 = (f32[512,512]{1,0:T(8,128)}, f32[64,512]{1,0:T(8,128)}, f32[2,3,1024]{2,1,0:T(4,128)}, f32[2,3,1024]{2,1,0:T(4,128)}, f32[2,3,1024]{2,1,0:T(4,128)}, /*index=5*/f32[8,128]{1,0:T(8,128)}) custom-call(f32[512,64]{1,0:T(8,128)} %bitcast.33, f32[58,64]{1,0:T(8,128)} %bitcast.37, f32[3,3,1024]{2,1,0:T(4,128)} %bitcast.42, ...), custom_call_target="tpu_custom_call" | custom-call | tf_op jit(solution)/shard_map/pallas_call | solution.py:747
  37.2 38.6 %shard_map.390 = (f32[2,3,1024]{2,1,0:T(4,128)}, f32[2,3,1024]{2,1,0:T(4,128)}, f32[512,512]{1,0:T(8,128)}, f32[64,512]{1,0:T(8,128)}, f32[8,128]{1,0:T(8,128)}) custom-call(f32[64,512]{1,0:T(8,128)} %get-tuple-element.57.side, f32[512,512]{1,0:T(8,128)} %get-tuple-element.58.mid, f32[2,512]{1,0:T(2,128)} %bitcast.52, f32[1,3]{1,0:T(1,128)} %out_left.1, ...), custom_call_target="tpu_custom_call" | custom-call | tf_op jit(solution)/shard_map/pallas_call | solution.py:417
  75.8 29.2 %shard_map.391 = (f32[3,3,1024]{2,1,0:T(4,128)}, f32[3,3,1024]{2,1,0:T(4,128)}, f32[1,3]{1,0:T(1,128)}, f32[1,1]{1,0:T(1,128)}, f32[512,64]{1,0:T(8,128)}, /*ind...) custom-call(f32[512,512]{1,0:T(8,128)} %get-tuple-element.63.mid_gra, ...), custom_call_target="tpu_custom_call" | custom-call | tf_op jit(solution)/shard_map/pallas_call | solution.py:762
  105.0 1.5 %copy.53 = f32[1,3,3,1024]{3,0,2,1:T(1,128)} copy(f32[1,3,3,1024]{3,2,1,0:T(4,128)} %bitcast.44) | data formatting | bytes 73728
  106.5 1.5 %copy.54 = f32[1,3,3,1024]{3,0,2,1:T(1,128)} copy(f32[1,3,3,1024]{3,2,1,0:T(4,128)} %bitcast.43) | data formatting | bytes 73728
  107.9 1.3 %copy.61 = f32[1,4,3]{1,0,2:T(1,128)} copy(f32[1,4,3]{2,1,0:T(4,128)} %bitcast.55) | data formatting | bytes 96
  109.2 1.2 copy.62
  110.4 1.3 %copy.63 = f32[1,4,3]{1,0,2:T(1,128)} copy(f32[1,4,3]{2,1,0:T(4,128)} %bitcast.53) | data formatting | bytes 96
  111.7 1.4 %copy.58 = f32[1,58,64]{2,0,1:T(1,128)} copy(f32[1,58,64]{2,1,0:T(8,128)} %bitcast.47) | data formatting | bytes 29696
  113.2 0.6 copy.59
  113.8 0.6 copy.60
  114.4 0.8 copy.55
  115.2 0.8 copy.56
  116.2 0.8 copy.57
  117.1 0.8 copy.64
  118.1 0.8 copy.65
  119.0 0.8 copy.66
  121.5 0.6 copy.94
  122.3 0.6 copy.95
  (63 shorter events, 5.1 us)
Async XLA Ops:
  0.7 0.7 copy-start.24
  2.0 0.7 copy-start.25
  2.0 1.3 %copy-start.26 = (f32[1,4,3]{1,0,2:T(1,128)S(1)}, f32[1,4,3]{1,0,2:T(1,128)}, u32[]{:S(2)}) copy-start(f32[1,4,3]{1,0,2:T(1,128)} %param.37) | copy-start | bytes 148
  2.7 2.7 %copy-start.11 = (f32[1,3,3,1024]{3,0,2,1:T(1,128)S(1)}, f32[1,3,3,1024]{3,0,2,1:T(1,128)}, u32[]{:S(2)}) copy-start(f32[1,3,3,1024]{3,0,2,1:T(1,128)} %param.22) | copy-start | bytes 110596
  5.4 0.8 copy-start.19
  5.4 0.8 copy-start.20
  5.4 1.4 %copy-start.12 = (f32[1,3,3,1024]{3,0,2,1:T(1,128)S(1)}, f32[1,3,3,1024]{3,0,2,1:T(1,128)}, u32[]{:S(2)}) copy-start(f32[1,3,3,1024]{3,0,2,1:T(1,128)} %param.24) | copy-start | bytes 110596
  5.4 1.4 %copy-start.13 = (f32[1,3,3,1024]{3,0,2,1:T(1,128)S(1)}, f32[1,3,3,1024]{3,0,2,1:T(1,128)}, u32[]{:S(2)}) copy-start(f32[1,3,3,1024]{3,0,2,1:T(1,128)} %param.23) | copy-start | bytes 110596
  6.1 1.3 %copy-start.6 = (f32[1,512,64]{1,2,0:T(8,128)S(1)}, f32[1,512,64]{1,2,0:T(8,128)}, u32[]{:S(2)}) copy-start(f32[1,512,64]{1,2,0:T(8,128)} %param.29) | copy-start | bytes 393220
  7.5 0.9 copy-start.7
  8.4 0.9 copy-start.8
  9.3 0.9 copy-start.9
  10.2 0.9 copy-start.10
  105.0 9.5 %copy-start.5 = (f32[512,64]{1,0:T(8,128)S(1)}, f32[512,64]{1,0:T(8,128)}, u32[]{:S(2)}) copy-start(f32[512,64]{1,0:T(8,128)} %get-tuple-element.72) | copy-start | bytes 393220
  110.4 2.7 %copy-start.18 = (f32[58,64]{1,0:T(8,128)S(1)}, f32[58,64]{1,0:T(8,128)}, u32[]{:S(2)}) copy-start(f32[58,64]{1,0:T(8,128)} %get-tuple-element.76) | copy-start | bytes 44548
  111.7 2.1 %copy-start.17 = (f32[58,64]{1,0:T(8,128)S(1)}, f32[58,64]{1,0:T(8,128)}, u32[]{:S(2)}) copy-start(f32[58,64]{1,0:T(8,128)} %get-tuple-element.77) | copy-start | bytes 44548
  113.2 2.1 %copy-start.4 = (f32[512,64]{1,0:T(8,128)S(1)}, f32[512,64]{1,0:T(8,128)}, u32[]{:S(2)}) copy-start(f32[512,64]{1,0:T(8,128)} %get-tuple-element.73) | copy-start | bytes 393220
  115.2 1.0 copy-start.3
  116.2 0.9 copy-start.2
  117.1 0.9 copy-start.1
  118.1 0.9 copy-start
  119.0 0.8 copy-start.28
  119.0 2.5 %copy-start.16 = (f32[58,64]{1,0:T(8,128)S(1)}, f32[58,64]{1,0:T(8,128)}, u32[]{:S(2)}) copy-start(f32[58,64]{1,0:T(8,128)} %get-tuple-element.158) | copy-start | bytes 44548
  120.3 0.7 copy-start.27
  121.5 0.8 copy-start.15
  122.3 0.8 copy-start.14
  123.1 0.7 copy-start.23
  123.7 0.7 copy-start.22
  124.4 0.7 copy-start.21

commit v2 on v0

v2 whole, which is shorter than its diff:
```python
import functools
import types

import jax, jax.numpy as jnp
from jax import lax
from jax.experimental import pallas as pl
from jax.experimental.pallas import tpu as pltpu
from jax.sharding import PartitionSpec as P

bf16, f32 = jnp.bfloat16, jnp.float32
HIGH = lax.Precision.HIGHEST
C, PX, TILE = 512, 1024, 512
CLIP = 0.98
LIP = 2.2


def dot_nn(a, b):
    return jnp.dot(a, b, preferred_element_type=f32)


def dot_tn(a, b):
    return lax.dot_general(a, b, (((0,), (0,)), ((), ())), preferred_element_type=f32)


def dot_nt(a, b):
    return lax.dot_general(a, b, (((1,), (1,)), ((), ())), preferred_element_type=f32)


def tap_masks():
    lane = lax.broadcasted_iota(jnp.int32, (8, PX), 1)
    row, col = lane // 32, lane % 32
    masks = []
    for tap in range(9):
        down, right = tap // 3 - 1, tap % 3 - 1
        ok = (row + down >= 0) & (row + down < 32) & (col + right >= 0) & (col + right < 32)
        masks.append(ok)
    return masks


def shift(field, tap, masks):
    if tap == 4:
        return field
    offset = (tap // 3 - 1) * 32 + tap % 3 - 1
    return jnp.where(masks[tap], pltpu.roll(field, (-offset) % PX, 1), 0.0)


def expand(field, flip, one, masks):
    high = field.astype(bf16).astype(f32)
    low = field - high
    row = lax.broadcasted_iota(jnp.int32, (8, PX), 0)
    base = jnp.where(row < 3, high, jnp.where(row < 6, pltpu.roll(low, 3, 0), one))
    parts = [shift(base, 8 - tap if flip else tap, masks) for tap in range(9)]
    return jnp.concatenate(parts + [jnp.zeros((8, PX), f32)], 0).astype(bf16)


def collapse(prod, flip, masks):
    total = prod[32:40]
    for tap in (0, 1, 2, 3, 5, 6, 7, 8):
        total = total + shift(prod[8 * tap : 8 * tap + 8], 8 - tap if flip else tap, masks)
    return total + pltpu.roll(total, 5, 0)


def pieces(h, slope_half):
    x = slope_half * h
    t = jnp.tanh(x)
    e = 1.0 - t * t
    return x, t, e


def softplus(raw):
    return jnp.maximum(raw, 0.0) + jnp.log1p(jnp.exp(-jnp.abs(raw)))


def sigmoid(raw):
    return 1.0 / (1.0 + jnp.exp(-raw))


def wide(ref, width):
    block = ref[...]
    return jnp.concatenate([block] * (width // 128), 1)


def to_column(row):
    return jnp.transpose(jnp.broadcast_to(row, (128, C)))


def prepare_side(side, lefts, out_left, stage, wa1, wp1, wa3, wp3, cols):
    rows = lax.broadcasted_iota(jnp.int32, (80, C), 0)
    stage[...] = jnp.zeros_like(stage)
    for color in range(3):
        for tap in range(9):
            stage[0, 8 * tap + color : 8 * tap + color + 1, :] = side[9 * color + tap : 9 * color + tap + 1, :]
            at = 31 + 9 * color + tap
            stage[1, 8 * tap + color : 8 * tap + color + 1, :] = side[at : at + 1, :]
    first = stage[0]
    u = lefts[0:1, :]
    right1 = jnp.sum(first * u, axis=1, keepdims=True)
    right1 = right1 / jnp.sqrt(jnp.sum(right1 * right1) + 1e-12)
    y1 = jnp.sum(first * right1, axis=0, keepdims=True)
    left1 = y1 / jnp.sqrt(jnp.sum(y1 * y1) + 1e-12)
    sigma1 = jnp.sum(left1 * y1)
    last = stage[1]
    inner = rows % 8
    weight = jnp.where(inner == 0, out_left[0], jnp.where(inner == 1, out_left[1], out_left[2]))
    mixed = jnp.where(inner < 3, last * weight, 0.0)
    right3 = mixed + pltpu.roll(mixed, 79, 0) + pltpu.roll(mixed, 78, 0)
    right3 = jnp.where(inner == 0, right3, 0.0)
    right3 = right3 / jnp.sqrt(jnp.sum(right3 * right3) + 1e-12)
    right3 = right3 + pltpu.roll(right3, 1, 0) + pltpu.roll(right3, 2, 0)
    prod = last * right3
    y3 = [jnp.sum(jnp.where(inner == k, prod, 0.0)) for k in range(3)]
    norm3 = jnp.sqrt(y3[0] * y3[0] + y3[1] * y3[1] + y3[2] * y3[2] + 1e-12)
    left3 = [value / norm3 for value in y3]
    sigma3 = left3[0] * y3[0] + left3[1] * y3[1] + left3[2] * y3[2]
    outer3 = jnp.where(inner == 0, left3[0], jnp.where(inner == 1, left3[1], left3[2])) * right3
    outer1 = right1 * left1
    q1, q3 = jnp.maximum(1.0, sigma1 / CLIP), jnp.maximum(1.0, sigma3 / CLIP)
    for at, q, wa, wp in ((0, q1, wa1, wp1), (1, q3, wa3, wp3)):
        scaled = stage[at] / (LIP * q)
        high = scaled.astype(bf16).astype(f32)
        low = scaled - high
        top = high + pltpu.roll(high, 3, 0)
        if at == 0:
            bias = side[27:28, :]
            bias_high = bias.astype(bf16).astype(f32)
            top = jnp.where(rows == 38, bias_high, jnp.where(rows == 39, bias - bias_high, top))
        wa[0:80, :] = top.astype(bf16)
        wa[80:160, :] = (low + pltpu.roll(low, 3, 0)).astype(bf16)
        wp[...] = (high + pltpu.roll(low, 3, 0)).astype(bf16)
    cols[0] = to_column(0.5 * softplus(side[28:29, :]))
    cols[1] = to_column(side[29:30, :])
    cols[2] = to_column(0.5 * softplus(side[30:31, :]))
    return (q1, sigma1, outer1), (q3, sigma3, outer3)


def prepare_mid(mid, lefts, m_high, m_low, outer):
    right = jnp.sum(mid * lefts[1:2, :], axis=1, keepdims=True)
    right = right / jnp.sqrt(jnp.sum(right * right) + 1e-12)
    y = jnp.sum(mid * right, axis=0, keepdims=True)
    left = y / jnp.sqrt(jnp.sum(y * y) + 1e-12)
    sigma = jnp.sum(left * y)
    q = jnp.maximum(1.0, sigma / CLIP)
    scaled = mid / (LIP * q)
    high = scaled.astype(bf16)
    m_high[...] = high
    m_low[...] = (scaled - high.astype(f32)).astype(bf16)
    outer[0:8, :] = jnp.broadcast_to(left, (8, C))
    return q, sigma, right


def correction(raw_grad, weight, q, sigma):
    ratio = sigma / CLIP
    active = jnp.where(ratio > 1.0, 1.0, jnp.where(ratio == 1.0, 0.5, 0.0))
    return 1.0 / (LIP * q), -active * jnp.sum(raw_grad * weight) / (LIP * q * q * CLIP)


def color_column(values):
    row = lax.broadcasted_iota(jnp.int32, (8, 1), 0)
    return jnp.where(row == 0, values[0], jnp.where(row == 1, values[1], values[2]))


PARTS = PX // TILE


def tile_at(image, part):
    if isinstance(image, int):
        return slice(image * PX + part * TILE, image * PX + (part + 1) * TILE)
    return pl.ds(pl.multiple_of(image * PX + part * TILE, TILE), TILE)


def each_image(body):
    lax.fori_loop(0, 2, lambda b, c: (body(b), c)[1], 0)


MESH = pl.DeviceIdType.MESH
SZ, SP, SC, SD, SV, SN, SS, ST, SA, SB = range(10)


def scale_sizes(n):
    w = C // n
    fold = 128 // w
    return w, fold, 64 // fold


def pack(block, fold):
    rows = block.shape[0] // fold
    return jnp.concatenate([block[i * rows : (i + 1) * rows] for i in range(fold)], 1)


def unpack(block, fold):
    w = 128 // fold
    return jnp.concatenate([block[:, i * w : (i + 1) * w] for i in range(fold)], 0)


class Gather:
    def __init__(self, n, buf, sems):
        self.n, self.m, self.buf, self.sems = n, n // 2, buf, sems
        self.me = lax.axis_index("dp")
        self.chip, self.core = self.me // 2, self.me % 2
        self.pair = self.me + 1 - 2 * self.core

    def copy(self, slot, sem, target):
        return pltpu.make_async_remote_copy(
            src_ref=self.buf.at[slot],
            dst_ref=self.buf.at[slot],
            send_sem=self.sems.at[0, sem],
            recv_sem=self.sems.at[1, sem],
            device_id={"dp": target},
            device_id_type=MESH,
        )

    def peer(self, j):
        return lax.rem(self.chip + j, self.m) * 2 + self.core

    def start(self):
        for j in range(1, self.m):
            self.copy(self.me, j, self.peer(j)).start()
        self.copy(self.me, self.m, self.pair).start()

    def forward(self):
        for j in range(1, self.m):
            source = self.peer(j)
            self.copy(source, self.m - j, source).wait_recv()
            self.copy(source, self.m + j, self.pair).start()

    def finish(self):
        for j in range(self.m):
            self.copy(self.me, self.m + j, self.pair).wait_recv()
        for j in range(1, 2 * self.m):
            self.copy(self.me, j, self.pair).wait_send()


class Reduce:
    def __init__(self, n, source, from_pair, chipsum, from_chips, sems):
        self.n, self.m = n, n // 2
        self.source, self.from_pair, self.chipsum, self.from_chips, self.sems = source, from_pair, chipsum, from_chips, sems
        self.me = lax.axis_index("dp")
        self.chip, self.core = self.me // 2, self.me % 2
        self.pair = self.me + 1 - 2 * self.core

    def swap_copy(self, k):
        return pltpu.make_async_remote_copy(
            src_ref=self.source.at[2 * k + 1 - self.core], dst_ref=self.from_pair.at[k],
            send_sem=self.sems.at[0, k], recv_sem=self.sems.at[1, k],
            device_id={"dp": self.pair}, device_id_type=MESH)

    def chip_copy(self, slot, j, target):
        return pltpu.make_async_remote_copy(
            src_ref=self.chipsum.at[slot], dst_ref=self.from_chips.at[j],
            send_sem=self.sems.at[0, self.m + j], recv_sem=self.sems.at[1, self.m + j],
            device_id={"dp": target}, device_id_type=MESH)

    def start(self):
        for k in range(self.m):
            self.swap_copy(k).start()

    def forward(self):
        for k in range(self.m):
            self.swap_copy(k).wait_recv()
            self.chipsum[k] = self.source[2 * k + self.core] + self.from_pair[k]
        for j in range(1, self.m):
            to = lax.rem(self.chip + j, self.m)
            self.chip_copy(to, j, to * 2 + self.core).start()

    def finish(self):
        total = self.chipsum[self.chip]
        for j in range(1, self.m):
            self.chip_copy(self.chip, j, self.pair).wait_recv()
            total = total + self.from_chips[j]
        return total

    def drain(self):
        for k in range(self.m):
            self.swap_copy(k).wait_send()
        for j in range(1, self.m):
            self.chip_copy(self.chip, j, self.pair).wait_send()


class Across:
    def __init__(self, groups, sems):
        self.groups, self.sems, self.grp = groups, sems, lax.axis_index("grp")

    def copy(self, src, dst, j, target):
        return pltpu.make_async_remote_copy(
            src_ref=src, dst_ref=dst, send_sem=self.sems.at[0, j], recv_sem=self.sems.at[1, j],
            device_id={"grp": target}, device_id_type=MESH)

    def others(self):
        return [(j, lax.rem(self.grp + j, self.groups)) for j in range(1, self.groups)]


def barrier(n, groups):
    me, grp = lax.axis_index("dp"), lax.axis_index("grp")
    sem = pltpu.get_barrier_semaphore()
    m = n // 2
    chip, core = me // 2, me % 2
    for j in range(1, m):
        pl.semaphore_signal(sem, inc=1, device_id={"dp": lax.rem(chip + j, m) * 2 + core}, device_id_type=MESH)
    pl.semaphore_signal(sem, inc=1, device_id={"dp": me + 1 - 2 * core}, device_id_type=MESH)
    for j in range(1, groups):
        pl.semaphore_signal(sem, inc=1, device_id={"grp": lax.rem(grp + j, groups)}, device_id_type=MESH)
    pl.semaphore_wait(sem, m + groups - 1)


def match(counts, me, wanted_mine, wanted_theirs):
    zero = jnp.zeros((1, 128), f32)
    mine, my_rank = zero, zero
    for d in range(len(counts)):
        hit = jnp.where(counts[d] == wanted_mine, 1.0, 0.0)
        my_rank = my_rank + jnp.where(d < me, hit, zero)
        mine = mine + jnp.where(d == me, hit, zero)
    rank, masks = zero, []
    for d in range(len(counts)):
        hit = jnp.where(counts[d] == wanted_theirs, 1.0, 0.0)
        masks.append(jnp.where(rank == my_rank, hit * mine, zero))
        rank = rank + hit
    return masks


def adam(weight, gradient, first, second, rate):
    first = 0.9 * first + (1.0 - 0.9) * gradient
    second = 0.999 * second + (1.0 - 0.999) * gradient * gradient
    first_hat = first / (1.0 - 0.9**5.0)
    second_hat = second / (1.0 - 0.999**5.0)
    return weight - rate * (first_hat / (jnp.sqrt(second_hat) + 1e-8) + 0.01 * weight), first, second


def side_rate(w):
    return jnp.where(lax.broadcasted_iota(jnp.int32, (58, w), 0) >= 31, 0.004, 0.05)


def flip(tile):
    eye = lax.broadcasted_iota(jnp.int32, (8, 128), 0) == lax.broadcasted_iota(jnp.int32, (8, 128), 1)
    return lax.dot_general(tile, eye.astype(f32), (((0,), (0,)), ((), ())), precision=HIGH, preferred_element_type=f32)[0:8]


def spread_field(ref, base, small, at, b):
    for c in range(3):
        for k in range(8):
            small[at, b, c : c + 1, k * 128 : (k + 1) * 128] = ref[base + c, k : k + 1, :]


def fold_field(value, ref, base):
    for c in range(3):
        for k in range(8):
            ref[base + c, k : k + 1, :] = value[c : c + 1, k * 128 : (k + 1) * 128]


def main_kernel(n, groups, names, *refs):
    r = types.SimpleNamespace(**dict(zip(names, refs)))
    w, fold, side_rows = scale_sizes(n)
    m = n // 2
    me, grp = lax.axis_index("dp"), lax.axis_index("grp")
    counts, terms, tiny = r.counts, r.terms, r.tiny
    get_side = Gather(n, r.sides, r.sides_sem)
    get_third = Gather(n, r.thirds, r.thirds_sem)
    get_mid = Gather(n, r.mids, r.mids_sem)
    share = Gather(n, r.results, r.results_sem)
    r.sides[me] = pack(jnp.concatenate([r.side_w[:, 0, :], jnp.zeros((6, w), f32)], 0), fold)
    for at, ref in enumerate((r.images, r.probes, r.cots)):
        r.thirds[me, 3 * at : 3 * at + 3] = ref[6:9]
    lane = lax.broadcasted_iota(jnp.int32, (8, 128), 1)
    sub = lax.broadcasted_iota(jnp.int32, (8, 128), 0)
    own_count = jnp.broadcast_to(counts[0, 0].astype(f32), (1, 128))
    r.thirds[me, 9] = jnp.where(lane == 0, counts[0, 0].astype(f32), terms[0, 2].astype(f32))
    r.mids[me] = r.mid_w[...]
    barrier(n, groups)
    get_side.start()
    get_third.start()
    get_mid.start()
    small, side = r.small, r.side
    small[...] = jnp.zeros_like(small)
    for at, ref in ((SZ, r.images), (SP, r.probes), (SC, r.cots)):
        spread_field(ref, 0, small, at, 0)
    r.live[...] = jnp.where(terms[0, 0].astype(f32) > (sub % 4).astype(f32), 1.0, 0.0)
    get_side.forward()
    get_side.finish()
    for i in range(fold):
        side[i * side_rows : (i + 1) * side_rows, :] = jnp.concatenate(
            [r.sides[d][:, i * w : (i + 1) * w] for d in range(n)], 1)
    lefts = r.lefts
    side1, side3 = prepare_side(side, lefts, [r.out_left[0, k] for k in range(3)], r.stage,
                                r.wa1, r.wp1, r.wa3, r.wp3, r.cols)
    bias_col = color_column([tiny[k, 0, 0] for k in range(3)])
    shift_col = color_column([tiny[k, 0, 1] for k in range(3)])
    scale_col = jnp.exp(color_column([tiny[k, 0, 2] for k in range(3)]))
    slope_raw = color_column([tiny[k, 0, 3] for k in range(3)])
    slope0 = 0.5 * softplus(slope_raw)
    wa1, wp1, wa3, wp3 = r.wa1, r.wp1, r.wa3, r.wp3
    mh, ml = r.mh, r.ml
    slope1 = lambda: wide(r.cols.at[0], TILE)
    bias2 = lambda: wide(r.cols.at[1], TILE)
    slope2 = lambda: wide(r.cols.at[2], TILE)
    valid = lambda: lax.broadcasted_iota(jnp.int32, (8, PX), 0) < 3

    def alive(b, step):
        row = r.live[pl.ds(b * 4 + step, 1), :]
        return jnp.concatenate([row] * (PX // 128), 1)

    def doubled(index, part):
        block = r.field[index, :, part * TILE : (part + 1) * TILE]
        return jnp.concatenate([block, block], 0)

    def third_image():
        get_third.forward()
        get_third.finish()
        metas = [r.thirds[d, 9, 0:1, :] for d in range(n)]
        count_rows = [jnp.broadcast_to(meta[:, 0:1], (1, 128)) for meta in metas]
        masks = match(count_rows, me, 1.0, 3.0)
        helper, term = jnp.zeros((1, 128), f32), jnp.zeros((1, 128), f32) + terms[0, 1].astype(f32)
        for d in range(n):
            helper = helper + masks[d]
            term = jnp.where(masks[d] > 0.0, jnp.broadcast_to(metas[d][:, 1:2], (1, 128)), term)
        for at, ref in enumerate((r.images, r.probes, r.cots)):
            for c in range(3):
                picked = ref[3 + c]
                for d in range(n):
                    picked = jnp.where(masks[d] > 0.0, r.thirds[d, 3 * at + c], picked)
                r.picked[3 * at + c] = picked
        for at, place in ((0, SZ), (1, SP), (2, SC)):
            spread_field(r.picked, 3 * at, small, place, 1)
        r.live[...] = jnp.where(sub < 4, r.live[...], jnp.where(term > (sub % 4).astype(f32), 1.0, 0.0))

    def layer_one(b):
        pl.when(b == 1)(third_image)
        masks = tap_masks()
        field = (small[SZ, b] + shift_col) * scale_col
        p = small[SP, b]
        small[SZ, b] = field
        x, t, e = pieces(field, slope0)
        d0 = 1.0 + t + x * e
        small[SD, b] = d0
        r.field[b] = expand(field + field * t, False, 1.0, masks)
        r.field[2 + b] = expand(d0 * p, False, 0.0, masks)
        r.field[4 + b] = expand(small[SC, b], True, 0.0, masks)
        small[SV, b] = p
        small[SN, b] = -alive(b, 0) * p
        small[SS, b] = alive(b, 0) * p
        for part in range(PARTS):
            at = tile_at(b, part)
            h = dot_tn(wa1[...], doubled(b, part))
            x, t, e = pieces(h, slope1())
            d = 1.0 + t + x * e
            dh = dot_tn(wa1[...], doubled(2 + b, part))
            r.h1[:, at] = h
            r.g1[:, at] = dh
            r.d1[:, at] = d.astype(bf16)
            r.a1[:, at] = (h + h * t).astype(bf16)
            r.b1[:, at] = (d * dh).astype(bf16)

    each_image(layer_one)
    get_mid.forward()
    get_mid.finish()
    q2, sigma2, right2 = prepare_mid(r.mids[...].reshape(C, C), lefts, mh, ml, r.left2)

    def layer_two(b):
        masks = tap_masks()
        prods, dprods = [], []
        for part in range(PARTS):
            at = tile_at(b, part)
            a1 = r.a1[:, at]
            h = dot_tn(mh[...], a1) + dot_tn(ml[...], a1) + bias2()
            x, t, e = pieces(h, slope2())
            d = 1.0 + t + x * e
            dh = dot_tn(mh[...], r.b1[:, at])
            r.h2[:, at] = h
            r.g2[:, at] = dh
            r.d2[:, at] = d.astype(bf16)
            a2 = (h + h * t).astype(bf16)
            b2 = (d * dh).astype(bf16)
            r.a2[:, at] = a2
            r.b2[:, at] = b2
            prods.append(dot_nn(wp3[...], a2))
            dprods.append(dot_nn(wp3[...], b2))
        small[SA, b] = small[SZ, b] + collapse(jnp.concatenate(prods, 1), False, masks) + bias_col
        small[ST, b] = jnp.where(valid(), collapse(jnp.concatenate(dprods, 1), False, masks), 0.0)

    each_image(layer_two)
    fold_field(small[SA, 0], r.firsts, 0)
    fold_field(small[SA, 1], r.results.at[me], 0)

    def pull(step, sign):
        masks = tap_masks()
        for b in range(2):
            spread = expand(small[SV, b], True, 0.0, masks)
            prods = []
            for part in range(PARTS):
                at = tile_at(b, part)
                block = spread[:, part * TILE : (part + 1) * TILE]
                u2 = dot_tn(wa3[...], jnp.concatenate([block, block], 0)).astype(bf16) * r.d2[:, at]
                u1 = dot_nn(mh[...], u2).astype(bf16) * r.d1[:, at]
                prods.append(dot_nn(wp1[...], u1))
            v = jnp.where(valid(), small[SD, b] * collapse(jnp.concatenate(prods, 1), True, masks), 0.0)
            on = sign * alive(b, step + 1)
            small[SV, b] = v
            small[SN, b] = small[SN, b] - on * v
            small[SS, b] = small[SS, b] + (on / (step + 2).astype(f32)) * v
        return -sign

    lax.fori_loop(0, 3, pull, jnp.float32(-1.0))
    r.sums[...] = jnp.zeros_like(r.sums)

    def back_two(b):
        masks = tap_masks()
        r.field[6 + b] = expand(small[SN, b], True, 0.0, masks)
        slope_sum, bias_sum = r.sums[1], r.sums[0]
        for part in range(PARTS):
            at = tile_at(b, part)
            h = r.h2[:, at]
            sl = slope2()
            x, t, e = pieces(h, sl)
            d = 1.0 + t + x * e
            c_a = dot_tn(wa3[...], doubled(4 + b, part))
            t_a = dot_tn(wa3[...], doubled(6 + b, part))
            q = (2.0 * e * (1.0 - x * t)) * r.g2[:, at] * t_a
            c_h = d * c_a + sl * q
            grad = h * (c_a * h * e + q)
            for k in range(TILE // 128):
                slope_sum = slope_sum + grad[:, k * 128 : (k + 1) * 128]
                bias_sum = bias_sum + c_h[:, k * 128 : (k + 1) * 128]
            r.c2[:, at] = c_h.astype(bf16)
            r.t2[:, at] = (d * t_a).astype(bf16)
        r.sums[1] = slope_sum
        r.sums[0] = bias_sum

    each_image(back_two)
    raw = dot_nt(r.a1[...], r.c2[...]) + dot_nt(r.b1[...], r.t2[...])
    straight, across = correction(raw, r.mids[...].reshape(C, C), q2, sigma2)
    r.dmid[...] = (straight * raw + (across * right2) * r.left2[0:1, :]).reshape(n, w, C)
    sum_mid = Reduce(n, r.dmid, r.mid_pair, r.mid_chip, r.mid_chips, r.mid_sem)
    sum_mid.start()
    g3 = dot_nt(r.field[4], r.a2[:, 0:PX]) + dot_nt(r.field[6], r.b2[:, 0:PX])
    r.stage2[1] = g3 + dot_nt(r.field[5], r.a2[:, PX:]) + dot_nt(r.field[7], r.b2[:, PX:])

    def back_one(b):
        masks = tap_masks()
        slope_sum = r.sums[2]
        prods, dprods = [], []
        for part in range(PARTS):
            if part == 1:
                pl.when(b == 0)(sum_mid.forward)
            at = tile_at(b, part)
            h = r.h1[:, at]
            sl = slope1()
            x, t, e = pieces(h, sl)
            d = 1.0 + t + x * e
            c2 = r.c2[:, at]
            c_a = dot_nn(mh[...], c2) + dot_nn(ml[...], c2)
            t_a = dot_nn(mh[...], r.t2[:, at])
            q = (2.0 * e * (1.0 - x * t)) * r.g1[:, at] * t_a
            c_h = (d * c_a + sl * q).astype(bf16)
            t_h = (d * t_a).astype(bf16)
            grad = h * (c_a * h * e + q)
            for k in range(TILE // 128):
                slope_sum = slope_sum + grad[:, k * 128 : (k + 1) * 128]
            r.prod[0, :, part * TILE : (part + 1) * TILE] = dot_nn(wp1[...], c_h)
            r.prod[1, :, part * TILE : (part + 1) * TILE] = dot_nn(wp1[...], t_h)
            r.a2[:, at] = c_h
            r.b2[:, at] = t_h
            r.sums[2] = slope_sum
        small[SA, b] = collapse(r.prod[0], True, masks)
        small[SB, b] = collapse(r.prod[1], True, masks)

    each_image(back_one)
    g1 = dot_nt(r.field[0], r.a2[:, 0:PX]) + dot_nt(r.field[2], r.b2[:, 0:PX])
    g1 = g1 + dot_nt(r.field[1], r.a2[:, PX:]) + dot_nt(r.field[3], r.b2[:, PX:])
    ones = jnp.ones((8, 128), f32)
    row_of = lambda acc: lax.dot_general(
        ones, acc, (((1,), (1,)), ((), ())), precision=HIGH, preferred_element_type=f32)[0:1]
    dside = r.dside
    dside[27:28, :] = g1[38:39]
    dside[28:29, :] = row_of(r.sums[2]) * (0.5 * sigmoid(side[28:29, :]))
    dside[29:30, :] = row_of(r.sums[0])
    dside[30:31, :] = row_of(r.sums[1]) * (0.5 * sigmoid(side[30:31, :]))
    dside[58:64, :] = jnp.zeros((6, C), f32)
    row80 = lax.broadcasted_iota(jnp.int32, (80, C), 0)
    for at, (q, sigma, outer), grad, start in ((0, side1, g1, 0), (1, side3, r.stage2[1], 31)):
        joined = jnp.where((row80 % 8 < 3) & (row80 < 72), grad + pltpu.roll(grad, 77, 0), 0.0)
        straight, across = correction(joined, r.stage[at], q, sigma)
        r.stage2[at] = straight * joined + across * outer
        for color in range(3):
            for tap in range(9):
                to = start + 9 * color + tap
                dside[to : to + 1, :] = r.stage2[at, 8 * tap + color : 8 * tap + color + 1, :]
    for d in range(n):
        r.side_blocks[d] = pack(dside[:, d * w : (d + 1) * w], fold)
    sum_side = Reduce(n, r.side_blocks, r.side_pair, r.side_chip, r.side_chips, r.side_sem)
    sum_side.start()
    total_scale = tiny[0, 0, 2] + tiny[1, 0, 2] + tiny[2, 0, 2]
    tile = jnp.where(lane == 5, counts[0, 0].astype(f32), 0.0)
    for b in range(2):
        field, p, cot = small[SZ, b], small[SP, b], small[SC, b]
        c_a, t_a = small[SA, b], small[SB, b]
        x, t, e = pieces(field, slope0)
        q = 2.0 * e * (1.0 - x * t) * p * t_a
        c_z = jnp.where(valid(), cot + (1.0 + t + x * e) * c_a + slope0 * q, 0.0)
        slope_grad = jnp.where(valid(), field * (c_a * field * e + q), 0.0)
        fold_field(c_z * scale_col, r.firsts if b == 0 else r.results.at[me], 3)
        sums = [
            jnp.sum(cot, axis=1, keepdims=True),
            jnp.sum(c_z, axis=1, keepdims=True) * scale_col,
            jnp.sum(c_z * field, axis=1, keepdims=True) - 1024.0,
            jnp.sum(slope_grad, axis=1, keepdims=True) * (0.5 * sigmoid(slope_raw)),
        ]
        for k in range(4):
            tile = tile + jnp.where((lane == k) & (sub < 3), sums[k], 0.0)
        log_part = (1024.0 * total_scale + jnp.sum(small[SS, b] * small[ST, b])) / 3072.0
        tile = tile + jnp.where((lane == 4) & (sub == b), log_part, 0.0)
    r.results[me, 6] = tile
    share.start()
    mid_grad = sum_mid.finish() / (2.0 * n)
    r.mid_g[...] = mid_grad
    diff = r.mid_o[...] - adam(r.mid_w[...], mid_grad, r.mid_f[...], r.mid_s[...], 0.01)[0]
    chunk = C // groups
    for k in range(groups):
        r.mid_diff[k] = diff[:, k * chunk : (k + 1) * chunk]
    ring1, ring2 = Across(groups, r.ring1_sem), Across(groups, r.ring2_sem)
    ring3, ring4 = Across(groups, r.ring3_sem), Across(groups, r.ring4_sem)
    for j, to in ring1.others():
        ring1.copy(r.mid_diff.at[to], r.mid_parts.at[j], j, to).start()
    sum_side.forward()
    share.forward()
    total = r.mid_diff[grp]
    for j, to in ring1.others():
        ring1.copy(r.mid_diff.at[to], r.mid_parts.at[j], j, to).wait_recv()
        total = total + r.mid_parts[j]
    r.mid_sum[grp] = total
    for j, to in ring2.others():
        ring2.copy(r.mid_sum.at[grp], r.mid_sum.at[grp], j, to).start()
    side_grad = unpack(sum_side.finish(), fold)[0:58] / (2.0 * n)
    r.side_g[...] = side_grad
    new = adam(r.side_w[:, 0, :], side_grad, r.side_f[:, 0, :], r.side_s[:, 0, :], side_rate(w))[0]
    r.side_diff[grp] = pack(jnp.concatenate([r.side_o[...] - new, jnp.zeros((6, w), f32)], 0), fold)
    for j, to in ring3.others():
        ring3.copy(r.side_diff.at[grp], r.side_diff.at[grp], j, to).start()
    share.finish()
    tiny_sum = r.results[0, 6]
    for d in range(1, n):
        tiny_sum = tiny_sum + r.results[d, 6]
    r.out_small[0] = tiny_sum
    r.tiles[...] = jnp.zeros_like(r.tiles)
    for c in range(3):
        for k, ref in enumerate((r.tiny_w, r.tiny_f, r.tiny_s)):
            r.tiles[k, c : c + 1, 0:4] = ref[c, 0:1, :]
    r.tiles[3, 0:4, 0:3] = r.tiny_o[...]
    new = adam(r.tiles[0], tiny_sum / (2.0 * n), r.tiles[1], r.tiles[2], 0.05)[0]
    r.tiny_diff[grp] = r.tiles[3] - flip(jnp.where(lane < 4, new, 0.0))
    for j, to in ring4.others():
        ring4.copy(r.tiny_diff.at[grp], r.tiny_diff.at[grp], j, to).start()
    tiles = [r.results[d, 6] for d in range(n)]
    masks = match([jnp.broadcast_to(t[0:1, 5:6], (1, 128)) for t in tiles], me, 3.0, 1.0)
    log_third = jnp.zeros((1, 128), f32)
    for d in range(n):
        log_third = jnp.where(masks[d] > 0.0, jnp.broadcast_to(tiles[d][1:2, 4:5], (1, 128)), log_third)
    for k in range(6):
        out, c = (r.out_flow, k) if k < 3 else (r.out_back, k - 3)
        picked = jnp.zeros((8, 128), f32)
        for d in range(n):
            picked = jnp.where(masks[d] > 0.0, r.results[d, k], picked)
        out[c] = r.firsts[k]
        out[3 + c] = jnp.where(own_count > 1.5, r.results[me, k], 0.0)
        out[6 + c] = picked
    logs = [jnp.broadcast_to(tile[b : b + 1, 4:5], (1, 128)) for b in range(2)]
    logs[1] = jnp.where(own_count > 1.5, logs[1], 0.0)
    row_lane = lax.broadcasted_iota(jnp.int32, (1, 128), 1)
    r.out_small[1] = jnp.broadcast_to(
        jnp.where(row_lane == 0, logs[0], jnp.where(row_lane == 1, logs[1], log_third)), (8, 128))
    for j, to in ring3.others():
        ring3.copy(r.side_diff.at[grp], r.side_diff.at[grp], j, to).wait_recv()
    total = r.side_diff[0]
    for k in range(1, groups):
        total = total + r.side_diff[k]
    r.side_t[...] = unpack(total, fold)[0:58]
    for j, to in ring4.others():
        ring4.copy(r.tiny_diff.at[grp], r.tiny_diff.at[grp], j, to).wait_recv()
    total = r.tiny_diff[0]
    for k in range(1, groups):
        total = total + r.tiny_diff[k]
    r.out_small[2] = total
    for j, to in ring2.others():
        ring2.copy(r.mid_sum.at[grp], r.mid_sum.at[grp], j, to).wait_recv()
    for k in range(groups):
        r.mid_t[:, k * chunk : (k + 1) * chunk] = r.mid_sum[k]
    sum_mid.drain()
    sum_side.drain()
    for ring in (ring1, ring2):
        for j, to in ring.others():
            ring.copy(r.mid_sum.at[grp], r.mid_sum.at[grp], j, to).wait_send()
    for j, to in ring3.others():
        ring3.copy(r.side_diff.at[grp], r.side_diff.at[grp], j, to).wait_send()
    for j, to in ring4.others():
        ring4.copy(r.tiny_diff.at[grp], r.tiny_diff.at[grp], j, to).wait_send()


def last_kernel(n, groups, names, *refs):
    r = types.SimpleNamespace(**dict(zip(names, refs)))
    w = C // n
    lane = lax.broadcasted_iota(jnp.int32, (8, 128), 1)
    r.flow_o[...] = r.flow[...]
    r.back_o[...] = r.back[...]
    r.log_det[...] = r.small[1, 0:1, 0:3]
    tiny_sum = r.small[0]
    r.log_mean[...] = (tiny_sum[0:1, 4:5] + tiny_sum[1:2, 4:5]) / (2.0 * n)
    new, first, second = adam(r.mid_w[...], r.mid_g[...], r.mid_f[...], r.mid_s[...], 0.01)
    r.mid_f_new[...], r.mid_s_new[...], r.mid_new[...] = first, second, new
    new, first, second = adam(r.side_w[:, 0, :], r.side_g[...], r.side_f[:, 0, :], r.side_s[:, 0, :], side_rate(w))
    r.side_f_new[:, 0, :], r.side_s_new[:, 0, :], r.side_new[:, 0, :] = first, second, new
    r.tiles[...] = jnp.zeros_like(r.tiles)
    for c in range(3):
        for k, ref in enumerate((r.tiny_w, r.tiny_f, r.tiny_s)):
            r.tiles[k, c : c + 1, 0:4] = ref[c, 0:1, :]
    new, first, second = adam(r.tiles[0], tiny_sum / (2.0 * n), r.tiles[1], r.tiles[2], 0.05)
    for c in range(3):
        r.tiny_f_new[c, 0:1, :] = first[c : c + 1, 0:4]
        r.tiny_new[c, 0:1, :] = new[c : c + 1, 0:4]
    turned = flip(jnp.where(lane < 4, second, 0.0))
    for k in range(3):
        r.tiny_s_new[k, 0:1, :] = turned[k : k + 1, 0:3]
    r.slope_s_new[...] = turned[3:4, 0:3]

    def outer(diff, old, momentum, delta_out, momentum_out, out):
        delta = diff / groups
        mom = 0.9 * momentum[...] + delta
        delta_out[...], momentum_out[...] = delta, mom
        out[...] = old[...] - 0.7 * (delta + 0.9 * mom)

    outer(r.mid_t[...], r.mid_o, r.mid_m, r.mid_d, r.mid_m_new, r.mid_o_new)
    outer(r.side_t[...], r.side_o, r.side_m, r.side_d, r.side_m_new, r.side_o_new)
    outer(r.small[2, 0:4, 0:3], r.tiny_o, r.tiny_m, r.tiny_d, r.tiny_m_new, r.tiny_o_new)


def on_device(images, probes, out_cotangent, counts, terms, power_left, power_out, mid_weight, mid_first, mid_second,
              side_weight, side_first, side_second, tiny_weight, tiny_first, tiny_second,
              mid_outer, mid_momentum, side_outer, side_momentum, tiny_outer, tiny_momentum):
    n, groups = lax.axis_size("dp"), lax.axis_size("grp")
    w, fold, side_rows = scale_sizes(n)
    m = n // 2
    vm = pl.BlockSpec(memory_space=pltpu.VMEM)
    sm = pl.BlockSpec(memory_space=pltpu.SMEM)
    sd = lambda *shape: jax.ShapeDtypeStruct(shape, f32)
    dma = lambda *shape: pltpu.SemaphoreType.DMA(shape)
    vmem = lambda *shape: pltpu.VMEM(shape, f32)
    big = lambda dtype: pltpu.VMEM((C, 2 * PX), dtype)
    half = lambda *shape: pltpu.VMEM(shape, bf16)
    image = lambda x: x[0].reshape(9, 8, 128)
    turn = lambda x: jnp.swapaxes(x, -1, -2)
    row = lambda x: x[0][:, None, :]
    color = lambda x: jnp.transpose(x, (2, 0, 1))
    state = dict(
        mid_w=turn(mid_weight[0]), mid_f=turn(mid_first[0]), mid_s=turn(mid_second[0]), mid_o=turn(mid_outer),
        side_w=row(side_weight), side_f=row(side_first), side_s=row(side_second), side_o=side_outer,
        tiny_w=color(tiny_weight), tiny_f=color(tiny_first), tiny_s=color(tiny_second), tiny_o=tiny_outer,
    )
    vmem_in = dict(images=image(images), probes=image(probes), cots=image(out_cotangent), lefts=power_left[0], **state)
    smem_in = dict(counts=counts, terms=terms, out_left=power_out, tiny=color(tiny_weight))
    outs = dict(out_flow=sd(9, 8, 128), out_back=sd(9, 8, 128), out_small=sd(3, 8, 128), mid_g=sd(w, C), mid_t=sd(w, C),
                side_g=sd(58, w), side_t=sd(58, w))
    scratch = dict(
        stage=vmem(2, 80, C), stage2=vmem(2, 80, C), wa1=half(160, C), wp1=half(80, C), wa3=half(160, C), wp3=half(80, C),
        cols=vmem(3, C, 128), small=vmem(10, 2, 8, PX), sums=vmem(3, C, 128), field=half(8, 80, PX), prod=vmem(2, 80, PX),
        mh=half(C, C), ml=half(C, C), left2=vmem(8, C), live=vmem(8, 128), side=vmem(64, C),
        h1=big(f32), g1=big(f32), h2=big(f32), g2=big(f32),
        d1=big(bf16), a1=big(bf16), b1=big(bf16), d2=big(bf16), a2=big(bf16), b2=big(bf16), c2=big(bf16), t2=big(bf16),
        sides=vmem(n, side_rows, 128), thirds=vmem(n, 10, 8, 128), mids=vmem(n, w, C), results=vmem(n, 7, 8, 128),
        picked=vmem(9, 8, 128), firsts=vmem(6, 8, 128), dmid=vmem(n, w, C), dside=vmem(64, C),
        side_blocks=vmem(n, side_rows, 128),
        mid_pair=vmem(m, w, C), mid_chip=vmem(m, w, C), mid_chips=vmem(m, w, C),
        side_pair=vmem(m, side_rows, 128), side_chip=vmem(m, side_rows, 128), side_chips=vmem(m, side_rows, 128),
        mid_diff=vmem(groups, w, C // groups), mid_parts=vmem(groups, w, C // groups), mid_sum=vmem(groups, w, C // groups),
        side_diff=vmem(groups, side_rows, 128), tiny_diff=vmem(groups, 8, 128), tiles=vmem(4, 8, 128),
        sides_sem=dma(2, n), thirds_sem=dma(2, n), mids_sem=dma(2, n), results_sem=dma(2, n),
        mid_sem=dma(2, n), side_sem=dma(2, n),
        ring1_sem=dma(2, groups), ring2_sem=dma(2, groups), ring3_sem=dma(2, groups), ring4_sem=dma(2, groups),
    )
    ins = {**vmem_in, **smem_in}
    made = pl.pallas_call(
        functools.partial(main_kernel, n, groups, list(ins) + list(outs) + list(scratch)),
        in_specs=[vm] * len(vmem_in) + [sm] * len(smem_in),
        out_specs=[vm] * len(outs),
        out_shape=list(outs.values()),
        scratch_shapes=list(scratch.values()),
        compiler_params=pltpu.CompilerParams(vmem_limit_bytes=60 << 20, collective_id=0, has_side_effects=True),
    )(*ins.values())
    flow, back, small, mid_g, mid_t, side_g, side_t = made
    ins = dict(flow=flow, back=back, small=small, mid_g=mid_g, mid_t=mid_t, side_g=side_g, side_t=side_t, **state)
    ins.update(mid_m=turn(mid_momentum), side_m=side_momentum, tiny_m=tiny_momentum)
    scratch = dict(tiles=vmem(3, 8, 128))
    outs = dict(
        flow_o=sd(9, 8, 128), back_o=sd(9, 8, 128), log_det=sd(1, 3), log_mean=sd(1, 1),
        mid_f_new=sd(w, C), mid_s_new=sd(w, C), mid_new=sd(w, C),
        side_f_new=sd(58, 1, w), side_s_new=sd(58, 1, w), side_new=sd(58, 1, w),
        tiny_f_new=sd(3, 1, 4), tiny_s_new=sd(3, 1, 3), slope_s_new=sd(1, 3), tiny_new=sd(3, 1, 4),
        mid_d=sd(w, C), mid_m_new=sd(w, C), mid_o_new=sd(w, C),
        side_d=sd(58, w), side_m_new=sd(58, w), side_o_new=sd(58, w),
        tiny_d=sd(4, 3), tiny_m_new=sd(4, 3), tiny_o_new=sd(4, 3),
    )
    made = pl.pallas_call(
        functools.partial(last_kernel, n, groups, list(ins) + list(outs) + list(scratch)),
        in_specs=[vm] * len(ins),
        out_specs=[vm] * len(outs),
        out_shape=list(outs.values()),
        scratch_shapes=list(scratch.values()),
        compiler_params=pltpu.CompilerParams(vmem_limit_bytes=32 << 20),
    )(*ins.values())
    o = types.SimpleNamespace(**dict(zip(outs, made)))
    whole = lambda x: x.reshape(1, 3, 3, PX)
    back_turn = lambda x: turn(x)[None]
    return (
        whole(o.flow_o), whole(o.back_o), o.log_det, o.log_mean.reshape(1),
        back_turn(o.mid_f_new), back_turn(o.mid_s_new), back_turn(o.mid_new),
        o.side_f_new[:, 0][None], o.side_s_new[:, 0][None], o.side_new[:, 0][None],
        jnp.transpose(o.tiny_f_new, (1, 2, 0)), jnp.transpose(o.tiny_s_new, (1, 0, 2)), o.slope_s_new, jnp.transpose(o.tiny_new, (1, 2, 0)),
        turn(o.mid_d), turn(o.mid_m_new), turn(o.mid_o_new),
        o.side_d, o.side_m_new, o.side_o_new, o.tiny_d, o.tiny_m_new, o.tiny_o_new,
    )


def solution(mesh):
    split = P("grp", None, "dp")
    group = P("grp", None, None)
    image = P("grp", "dp", None, None)
    return jax.shard_map(
        on_device,
        mesh=mesh,
        in_specs=(image, image, image, P("grp", "dp"), P("grp", "dp"), group, P("grp", None),
                  split, split, split, split, split, split, group, group, group,
                  P(None, "dp"), P(None, "dp"), P(None, "dp"), P(None, "dp"), P(), P()),
        out_specs=(image, image, P("grp", "dp"), P("grp"), split, split, split, split, split, split,
                   group, group, P("grp", None), group) + (P(None, "dp"),) * 6 + (P(), P(), P()),
        check_vma=False,
    )
```

time: 780 us -> 90 us (0.12); the launches traced: 770 us -> 89.4 us
  matrix products: 320 us -> 0 us
  local copies, waits for them, and re-layouts: 200 us -> 8.23 us
  other arithmetic: 84.3 us -> 0 us
  Pallas kernels: 0 us -> 79.5 us
  waiting for transfers between devices: 59.6 us -> 0 us
  blocking collectives: 50.4 us -> 0 us
  loops' own time: 32.2 us -> 0 us
  between operations: 23.8 us -> 1.66 us
    dot_general x96 -> x0, matrix products: 320 us -> none  [the longest x33 177 us: branch(): hidden_two = jnp.dot(second, act_one, precision=highest) + side[29][:, None]]
    pallas_call x0 -> x2, Pallas kernels: none -> 79.5 us  [the longest x1 78.1 us: on_device(): pl.pallas_call(functools.partial(main_kernel, n, groups, list(ins) + list...]
    reshape x364 -> x0, local copies, waits for them, and re-layouts: 70.3 us -> none  [the longest x96 37.8 us: tap_shift(): grid = field.reshape(channels, HEIGHT, WIDTH)]
    another operation x183 -> x0, local copies, waits for them, and re-layouts: 53.6 us -> none  [the longest x159 39.8 us: tap_shift(): padded[:, row_shift:row_shift + HEIGHT, col_shift:col_shift + WIDTH]]
    psum x1 -> x0, waiting for transfers between devices: 41.5 us -> none  [on_device(): lax.psum((outers[0] - updated[0][0], outers[1] - updated[1][0], outers[2]...]
    psum x2 -> x0, blocking collectives: 34.5 us -> none  [the longest x1 18 us: on_device(): tiny_grad, log_sum = lax.psum((totals[2], log_local), 'dp')]
    another operation x1 -> x0, loops' own time: 32.2 us -> none  [run_images(): return lax.scan(visit, empty, (batch[0], batch[1], batch[2], series, keep))]
    add x15 -> x0, other arithmetic: 21 us -> none  [the longest x9 20.1 us: visit(): running + weight * gradient]
  transfers between devices with their start and end apart: 4 -> 0, of which waited for: 3 -> 0; matrix products, arithmetic and copies ran while one was open for 3% -> 0% of each run, Pallas kernels for 0% -> 0%
where the time goes in v2:
time: 90 us; the launch traced here: 89.4 us
  Pallas kernels  79.5 us (88%)
  local copies, waits for them, and re-layouts  8.23 us (9%)
  between operations  1.66 us (2%)
    pallas_call x1, Pallas kernels, on_device(): pl.pallas_call(functools.partial(main_kernel, n, groups, list(ins) + list...  78.1 us
    unnamed x44, local copies, waits for them, and re-layouts  8.23 us

profile of v2, /device:TPU:0, one launch (start us, length us, event | category | flops | bytes accessed | tf_op | source)
XLA Modules:
  0.0 89.4 jit_solution(12037457896231622187)
XLA Ops:
  1.3 0.0 copy-start.13
  1.3 0.0 copy-start
  1.3 0.0 copy-start.1
  1.3 0.0 copy-start.2
  1.4 0.0 copy-start.3
  1.4 0.0 copy-start.4
  1.4 78.1 %shard_map.389 = (f32[9,8,128]{2,1,0:T(8,128)}, f32[9,8,128]{2,1,0:T(8,128)}, f32[3,8,128]{2,1,0:T(8,128)}, f32[64,512]{1,0:T(8,128)}, f32[64,512]{1,0:T(8,128)}, /*index=5*/f32[58,64]{1,0:T(8,128)}, f32[58,64]{1,0:T(8,128)}) custom-call(f32[9,8,128]{2,1,0:T(8,128)} %bitcast.64, f32[9,8,128]{2,1,0:T(8,128)} %bitcast.65, f32[9,8,128]{2,1,0:T(8,128)} %bitcast.66, ...), custom_call_target="tpu_custom_call" | custom-call | tf_op jit(solution)/shard_map/pallas_call | solution.py:776
  79.6 0.0 copy-start.16
  79.6 0.0 copy-start.19
  79.6 0.0 copy-done.13
  79.6 0.0 copy-done
  79.6 0.0 copy-done.1
  79.6 0.0 copy-done.2
  79.6 0.0 copy-done.3
  79.6 0.0 copy-done.4
  79.6 0.0 copy-done.7
  79.7 0.0 copy-done.8
  79.7 0.0 copy-done.9
  79.7 0.0 copy-done.10
  79.7 0.6 copy-done.16
  80.2 0.0 copy-done.19
  80.3 0.9 %copy-done.5 = f32[64,512]{1,0:T(8,128)S(1)} copy-done((f32[64,512]{1,0:T(8,128)S(1)}, f32[64,512]{1,0:T(8,128)}, u32[]{:S(2)}) %copy-start.5) | copy-done | bytes 131096
  81.2 0.9 %copy-done.6 = f32[64,512]{1,0:T(8,128)S(1)} copy-done((f32[64,512]{1,0:T(8,128)S(1)}, f32[64,512]{1,0:T(8,128)}, u32[]{:S(2)}) %copy-start.6) | copy-done | bytes 131096
  82.1 0.8 copy-done.11
  82.8 0.8 copy-done.12
  83.6 0.8 copy-done.14
  84.4 0.8 copy-done.15
  85.1 0.7 copy-done.17
  85.8 0.7 copy-done.18
  86.5 0.7 copy-done.20
  87.2 0.7 copy-done.21
  87.9 1.4 %shard_map.390 = (f32[9,8,128]{2,1,0:T(8,128)}, f32[9,8,128]{2,1,0:T(8,128)}, f32[1,3]{1,0:T(1,128)}, f32[1,1]{1,0:T(1,128)}, f32[64,512]{1,0:T(8,128)}, /*index...) custom-call(f32[9,8,128]{2,1,0:T(8,128)S(1)} %copy-done.11, ...), custom_call_target="tpu_custom_call" | custom-call | tf_op jit(solution)/shard_map/pallas_call | solution.py:797
  (14 shorter events, 0.0 us)
Async XLA Ops:
  1.3 78.3 %copy-start.13 = (f32[58,64]{1,0:T(8,128)S(1)}, f32[58,64]{1,0:T(8,128)}, u32[]{:S(2)}) copy-start(f32[58,64]{1,0:T(8,128)} %refs_20_.1) | copy-start | bytes 44548
  1.3 78.3 %copy-start = (f32[1,512,64]{1,2,0:T(8,128)S(1)}, f32[1,512,64]{1,2,0:T(8,128)}, u32[]{:S(2)}) copy-start(f32[1,512,64]{1,2,0:T(8,128)} %param.29) | copy-start | bytes 393220
  1.3 78.3 %copy-start.1 = (f32[1,512,64]{1,2,0:T(8,128)S(1)}, f32[1,512,64]{1,2,0:T(8,128)}, u32[]{:S(2)}) copy-start(f32[1,512,64]{1,2,0:T(8,128)} %param.30) | copy-start | bytes 393220
  1.3 78.3 %copy-start.2 = (f32[1,512,64]{1,2,0:T(8,128)S(1)}, f32[1,512,64]{1,2,0:T(8,128)}, u32[]{:S(2)}) copy-start(f32[1,512,64]{1,2,0:T(8,128)} %param.31) | copy-start | bytes 393220
  1.4 78.3 %copy-start.3 = (f32[512,64]{0,1:T(8,128)S(1)}, f32[512,64]{0,1:T(8,128)}, u32[]{:S(2)}) copy-start(f32[512,64]{0,1:T(8,128)} %param.38) | copy-start | bytes 393220
  1.4 78.3 %copy-start.4 = (f32[512,64]{0,1:T(8,128)S(1)}, f32[512,64]{0,1:T(8,128)}, u32[]{:S(2)}) copy-start(f32[512,64]{0,1:T(8,128)} %param.39) | copy-start | bytes 393220
  1.4 78.3 %copy-start.7 = (f32[58,64]{1,0:T(8,128)S(1)}, f32[58,64]{1,0:T(8,128)}, u32[]{:S(2)}) copy-start(f32[58,64]{1,0:T(8,128)} %refs_14_.1) | copy-start | bytes 44548
  1.4 78.3 %copy-start.8 = (f32[1,58,64]{2,0,1:T(1,128)S(1)}, f32[1,58,64]{2,0,1:T(1,128)}, u32[]{:S(2)}) copy-start(f32[1,58,64]{2,0,1:T(1,128)} %param.32) | copy-start | bytes 44548
  1.4 78.3 %copy-start.9 = (f32[1,58,64]{2,0,1:T(1,128)S(1)}, f32[1,58,64]{2,0,1:T(1,128)}, u32[]{:S(2)}) copy-start(f32[1,58,64]{2,0,1:T(1,128)} %param.33) | copy-start | bytes 44548
  1.4 78.3 %copy-start.10 = (f32[1,58,64]{2,0,1:T(1,128)S(1)}, f32[1,58,64]{2,0,1:T(1,128)}, u32[]{:S(2)}) copy-start(f32[1,58,64]{2,0,1:T(1,128)} %param.34) | copy-start | bytes 44548
  79.6 0.7 copy-start.16
  79.6 0.7 copy-start.19
  80.3 0.9 %copy-start.5 = (f32[64,512]{1,0:T(8,128)S(1)}, f32[64,512]{1,0:T(8,128)}, u32[]{:S(2)}) copy-start(f32[64,512]{1,0:T(8,128)} %get-tuple-element.56.refs_3_) | copy-start | bytes 393220
  81.2 0.9 %copy-start.6 = (f32[64,512]{1,0:T(8,128)S(1)}, f32[64,512]{1,0:T(8,128)}, u32[]{:S(2)}) copy-start(f32[64,512]{1,0:T(8,128)} %get-tuple-element.57.refs_4_) | copy-start | bytes 393220
  82.1 0.8 copy-start.11
  82.8 0.8 copy-start.12
  83.6 0.8 copy-start.14
  84.4 0.8 copy-start.15
  85.1 0.7 copy-start.17
  85.8 0.7 copy-start.18
  86.5 0.7 copy-start.20
  87.2 0.7 copy-start.21

commit v3 on v2

--- a/solution.py
+++ b/solution.py
@@ -160,16 +160,22 @@
 
 
 PARTS = PX // TILE
-
-
-def tile_at(image, part):
-    if isinstance(image, int):
-        return slice(image * PX + part * TILE, image * PX + (part + 1) * TILE)
-    return pl.ds(pl.multiple_of(image * PX + part * TILE, TILE), TILE)
-
-
-def each_image(body):
-    lax.fori_loop(0, 2, lambda b, c: (body(b), c)[1], 0)
+RC = 32
+AT = [slice(k * TILE, (k + 1) * TILE) for k in range(2 * PARTS)]
+IM = (slice(0, PX), slice(PX, 2 * PX))
+CHUNKS = [slice(k, k + RC) for k in range(0, C, RC)]
+
+
+def pipeline(parts, dots, elem, after=None):
+    held = dots(parts[0])
+    for i, k in enumerate(parts):
+        ahead = dots(parts[i + 1]) if i + 1 < len(parts) else None
+        elem(k, *held)
+        if after is not None and i >= 1:
+            after(parts[i - 1])
+        held = ahead
+    if after is not None:
+        after(parts[-1])
 
 
 MESH = pl.DeviceIdType.MESH
@@ -238,10 +244,10 @@
         self.chip, self.core = self.me // 2, self.me % 2
         self.pair = self.me + 1 - 2 * self.core
 
-    def swap_copy(self, k):
+    def swap_copy(self, k, sem):
         return pltpu.make_async_remote_copy(
             src_ref=self.source.at[2 * k + 1 - self.core], dst_ref=self.from_pair.at[k],
-            send_sem=self.sems.at[0, k], recv_sem=self.sems.at[1, k],
+            send_sem=self.sems.at[0, sem], recv_sem=self.sems.at[1, sem],
             device_id={"dp": self.pair}, device_id_type=MESH)
 
     def chip_copy(self, slot, j, target):
@@ -251,16 +257,16 @@
             device_id={"dp": target}, device_id_type=MESH)
 
     def start(self):
-        for k in range(self.m):
-            self.swap_copy(k).start()
+        for j in range(1, self.m + 1):
+            self.swap_copy(lax.rem(self.chip + j, self.m), j % self.m).start()
 
     def forward(self):
-        for k in range(self.m):
-            self.swap_copy(k).wait_recv()
-            self.chipsum[k] = self.source[2 * k + self.core] + self.from_pair[k]
-        for j in range(1, self.m):
+        for j in range(1, self.m + 1):
             to = lax.rem(self.chip + j, self.m)
-            self.chip_copy(to, j, to * 2 + self.core).start()
+            self.swap_copy(to, j % self.m).wait_recv()
+            self.chipsum[to] = self.source[2 * to + self.core] + self.from_pair[to]
+            if j < self.m:
+                self.chip_copy(to, j, to * 2 + self.core).start()
 
     def finish(self):
         total = self.chipsum[self.chip]
@@ -271,7 +277,7 @@
 
     def drain(self):
         for k in range(self.m):
-            self.swap_copy(k).wait_send()
+            self.swap_copy(k, k).wait_send()
         for j in range(1, self.m):
             self.chip_copy(self.chip, j, self.pair).wait_send()
 
@@ -373,6 +379,32 @@
     for at, ref in ((SZ, r.images), (SP, r.probes), (SC, r.cots)):
         spread_field(ref, 0, small, at, 0)
     r.live[...] = jnp.where(terms[0, 0].astype(f32) > (sub % 4).astype(f32), 1.0, 0.0)
+    bias_col = color_column([tiny[k, 0, 0] for k in range(3)])
+    shift_col = color_column([tiny[k, 0, 1] for k in range(3)])
+    scale_col = jnp.exp(color_column([tiny[k, 0, 2] for k in range(3)]))
+    slope_raw = color_column([tiny[k, 0, 3] for k in range(3)])
+    slope0 = 0.5 * softplus(slope_raw)
+
+    def alive(b, step):
+        return jnp.concatenate([r.live[b * 4 + step : b * 4 + step + 1, :]] * (PX // 128), 1)
+
+    def prepare_image(b):
+        masks = tap_masks()
+        field = (small[SZ, b] + shift_col) * scale_col
+        p = small[SP, b]
+        small[SZ, b] = field
+        x, t, e = pieces(field, slope0)
+        d0 = 1.0 + t + x * e
+        small[SD, b] = d0
+        r.field[b] = expand(field + field * t, False, 1.0, masks)
+        r.field[2 + b] = expand(d0 * p, False, 0.0, masks)
+        r.field[4 + b] = expand(small[SC, b], True, 0.0, masks)
+        r.field[6 + b] = expand(p, True, 0.0, masks)
+        small[SV, b] = p
+        small[SN, b] = -alive(b, 0) * p
+        small[SS, b] = alive(b, 0) * p
+
+    prepare_image(0)
     get_side.forward()
     get_side.finish()
     for i in range(fold):
@@ -381,25 +413,64 @@
     lefts = r.lefts
     side1, side3 = prepare_side(side, lefts, [r.out_left[0, k] for k in range(3)], r.stage,
                                 r.wa1, r.wp1, r.wa3, r.wp3, r.cols)
-    bias_col = color_column([tiny[k, 0, 0] for k in range(3)])
-    shift_col = color_column([tiny[k, 0, 1] for k in range(3)])
-    scale_col = jnp.exp(color_column([tiny[k, 0, 2] for k in range(3)]))
-    slope_raw = color_column([tiny[k, 0, 3] for k in range(3)])
-    slope0 = 0.5 * softplus(slope_raw)
     wa1, wp1, wa3, wp3 = r.wa1, r.wp1, r.wa3, r.wp3
     mh, ml = r.mh, r.ml
-    slope1 = lambda: wide(r.cols.at[0], TILE)
-    bias2 = lambda: wide(r.cols.at[1], TILE)
-    slope2 = lambda: wide(r.cols.at[2], TILE)
     valid = lambda: lax.broadcasted_iota(jnp.int32, (8, PX), 0) < 3
 
-    def alive(b, step):
-        row = r.live[pl.ds(b * 4 + step, 1), :]
-        return jnp.concatenate([row] * (PX // 128), 1)
-
-    def doubled(index, part):
-        block = r.field[index, :, part * TILE : (part + 1) * TILE]
+    stages = []
+
+    def stage(body):
+        stages.append(body)
+        pl.when(me + len(stages) > 0)(body)
+
+    def doubled(index, k):
+        block = r.field[index + k // PARTS, :, (k % PARTS) * TILE : (k % PARTS + 1) * TILE]
         return jnp.concatenate([block, block], 0)
+
+    def column(which, rs):
+        return jnp.concatenate([r.cols[which, rs]] * (TILE // 128), 1)
+
+    one = (r.h1, r.g1, r.d1)
+    two = (r.h2, r.g2, r.d2)
+
+    def forward(kept, slope, bias, act, dact, k, h_all, dh_all):
+        at = AT[k]
+        hs, ys, ds = kept
+        for rs in CHUNKS:
+            h, dh = h_all[rs], dh_all[rs]
+            if bias is not None:
+                h = h + column(bias, rs)
+            x = column(slope, rs) * h
+            t = jnp.tanh(x)
+            e = 1.0 - t * t
+            d = 1.0 + t + x * e
+            hs[rs, at] = h
+            ds[rs, at] = d
+            ys[rs, at] = e * (1.0 - x * t) * dh
+            act[rs, at] = (h + h * t).astype(bf16)
+            dact[rs, at] = (d * dh).astype(bf16)
+
+    def backward(kept, slope, slope_to, bias_to, c_to, t_to, k, ca_all, ta_all):
+        at = AT[k]
+        hs, ys, ds = kept
+        for rs in CHUNKS:
+            h, d, c_a, t_a = hs[rs, at], ds[rs, at], ca_all[rs], ta_all[rs]
+            sl = column(slope, rs)
+            t = jnp.tanh(sl * h)
+            he = h * (0.5 - 0.5 * (t * t))
+            q = ys[rs, at] * t_a
+            c_h = d * c_a + (sl + sl) * q
+            grad = h * (c_a * he + q)
+            gs, cs = grad[:, 0:128], c_h[:, 0:128]
+            for j in range(1, TILE // 128):
+                gs = gs + grad[:, j * 128 : (j + 1) * 128]
+                if bias_to is not None:
+                    cs = cs + c_h[:, j * 128 : (j + 1) * 128]
+            r.sums[slope_to, rs] += gs
+            if bias_to is not None:
+                r.sums[bias_to, rs] += cs
+            c_to[rs, at] = c_h.astype(bf16)
+            t_to[rs, at] = (d * t_a).astype(bf16)
 
     def third_image():
         get_third.forward()
@@ -422,108 +493,75 @@
         r.live[...] = jnp.where(sub < 4, r.live[...], jnp.where(term > (sub % 4).astype(f32), 1.0, 0.0))
 
     def layer_one(b):
-        pl.when(b == 1)(third_image)
-        masks = tap_masks()
-        field = (small[SZ, b] + shift_col) * scale_col
-        p = small[SP, b]
-        small[SZ, b] = field
-        x, t, e = pieces(field, slope0)
-        d0 = 1.0 + t + x * e
-        small[SD, b] = d0
-        r.field[b] = expand(field + field * t, False, 1.0, masks)
-        r.field[2 + b] = expand(d0 * p, False, 0.0, masks)
-        r.field[4 + b] = expand(small[SC, b], True, 0.0, masks)
-        small[SV, b] = p
-        small[SN, b] = -alive(b, 0) * p
-        small[SS, b] = alive(b, 0) * p
-        for part in range(PARTS):
-            at = tile_at(b, part)
-            h = dot_tn(wa1[...], doubled(b, part))
-            x, t, e = pieces(h, slope1())
-            d = 1.0 + t + x * e
-            dh = dot_tn(wa1[...], doubled(2 + b, part))
-            r.h1[:, at] = h
-            r.g1[:, at] = dh
-            r.d1[:, at] = d.astype(bf16)
-            r.a1[:, at] = (h + h * t).astype(bf16)
-            r.b1[:, at] = (d * dh).astype(bf16)
-
-    each_image(layer_one)
+        @stage
+        def _():
+            pipeline([PARTS * b + k for k in range(PARTS)],
+                     lambda k: (dot_tn(wa1[...], doubled(0, k)), dot_tn(wa1[...], doubled(2, k))),
+                     functools.partial(forward, one, 0, None, r.a1, r.b1))
+            for k in range(PARTS * b, PARTS * b + PARTS):
+                r.ca[:, AT[k]] = dot_tn(wa3[...], doubled(4, k))
+                r.c2[:, AT[k]] = dot_tn(wa3[...], doubled(6, k)).astype(bf16)
+
+    layer_one(0)
+    third_image()
+    prepare_image(1)
+    layer_one(1)
     get_mid.forward()
     get_mid.finish()
     q2, sigma2, right2 = prepare_mid(r.mids[...].reshape(C, C), lefts, mh, ml, r.left2)
-
-    def layer_two(b):
+    r.sums[...] = jnp.zeros_like(r.sums)
+
+    @stage
+    def layer_two():
         masks = tap_masks()
-        prods, dprods = [], []
-        for part in range(PARTS):
-            at = tile_at(b, part)
-            a1 = r.a1[:, at]
-            h = dot_tn(mh[...], a1) + dot_tn(ml[...], a1) + bias2()
-            x, t, e = pieces(h, slope2())
-            d = 1.0 + t + x * e
-            dh = dot_tn(mh[...], r.b1[:, at])
-            r.h2[:, at] = h
-            r.g2[:, at] = dh
-            r.d2[:, at] = d.astype(bf16)
-            a2 = (h + h * t).astype(bf16)
-            b2 = (d * dh).astype(bf16)
-            r.a2[:, at] = a2
-            r.b2[:, at] = b2
-            prods.append(dot_nn(wp3[...], a2))
-            dprods.append(dot_nn(wp3[...], b2))
-        small[SA, b] = small[SZ, b] + collapse(jnp.concatenate(prods, 1), False, masks) + bias_col
-        small[ST, b] = jnp.where(valid(), collapse(jnp.concatenate(dprods, 1), False, masks), 0.0)
-
-    each_image(layer_two)
-    fold_field(small[SA, 0], r.firsts, 0)
-    fold_field(small[SA, 1], r.results.at[me], 0)
-
-    def pull(step, sign):
+
+        def dots(k):
+            a1 = r.a1[:, AT[k]]
+            return dot_tn(mh[...], a1) + dot_tn(ml[...], a1), dot_tn(mh[...], r.b1[:, AT[k]])
+
+        def after(k):
+            to = slice((k % PARTS) * TILE, (k % PARTS + 1) * TILE)
+            r.prod[0, :, to] = dot_nn(wp3[...], r.a2[:, AT[k]])
+            r.prod[1, :, to] = dot_nn(wp3[...], r.b2[:, AT[k]])
+            if k % PARTS == PARTS - 1:
+                b = k // PARTS
+                flow = small[SZ, b] + collapse(r.prod[0], False, masks) + bias_col
+                fold_field(flow, r.firsts if b == 0 else r.results.at[me], 0)
+                small[ST, b] = jnp.where(valid(), collapse(r.prod[1], False, masks), 0.0)
+
+        pipeline(range(2 * PARTS), dots, functools.partial(forward, two, 2, 1, r.a2, r.b2), after)
+
+    def pull(step):
         masks = tap_masks()
         for b in range(2):
-            spread = expand(small[SV, b], True, 0.0, masks)
-            prods = []
-            for part in range(PARTS):
-                at = tile_at(b, part)
-                block = spread[:, part * TILE : (part + 1) * TILE]
-                u2 = dot_tn(wa3[...], jnp.concatenate([block, block], 0)).astype(bf16) * r.d2[:, at]
-                u1 = dot_nn(mh[...], u2).astype(bf16) * r.d1[:, at]
-                prods.append(dot_nn(wp1[...], u1))
-            v = jnp.where(valid(), small[SD, b] * collapse(jnp.concatenate(prods, 1), True, masks), 0.0)
-            on = sign * alive(b, step + 1)
+            if step == 1:
+                r.c2[:, IM[b]] = (r.c2[:, IM[b]].astype(f32) * r.d2[:, IM[b]]).astype(bf16)
+            else:
+                spread = expand(small[SV, b], True, 0.0, masks)
+                wide_v = jnp.concatenate([spread, spread], 0)
+                r.c2[:, IM[b]] = (dot_tn(wa3[...], wide_v) * r.d2[:, IM[b]]).astype(bf16)
+        for b in range(2):
+            r.t2[:, IM[b]] = (dot_nn(mh[...], r.c2[:, IM[b]]) * r.d1[:, IM[b]]).astype(bf16)
+        sign = (-1.0) ** step
+        for b in range(2):
+            prod = dot_nn(wp1[...], r.t2[:, IM[b]])
+            v = jnp.where(valid(), small[SD, b] * collapse(prod, True, masks), 0.0)
             small[SV, b] = v
+            on = sign * alive(b, step)
             small[SN, b] = small[SN, b] - on * v
-            small[SS, b] = small[SS, b] + (on / (step + 2).astype(f32)) * v
-        return -sign
-
-    lax.fori_loop(0, 3, pull, jnp.float32(-1.0))
-    r.sums[...] = jnp.zeros_like(r.sums)
-
-    def back_two(b):
+            small[SS, b] = small[SS, b] + (on / (step + 1.0)) * v
+
+    for step in (1, 2, 3):
+        stage(functools.partial(pull, step))
+
+    @stage
+    def back_two():
         masks = tap_masks()
-        r.field[6 + b] = expand(small[SN, b], True, 0.0, masks)
-        slope_sum, bias_sum = r.sums[1], r.sums[0]
-        for part in range(PARTS):
-            at = tile_at(b, part)
-            h = r.h2[:, at]
-            sl = slope2()
-            x, t, e = pieces(h, sl)
-            d = 1.0 + t + x * e
-            c_a = dot_tn(wa3[...], doubled(4 + b, part))
-            t_a = dot_tn(wa3[...], doubled(6 + b, part))
-            q = (2.0 * e * (1.0 - x * t)) * r.g2[:, at] * t_a
-            c_h = d * c_a + sl * q
-            grad = h * (c_a * h * e + q)
-            for k in range(TILE // 128):
-                slope_sum = slope_sum + grad[:, k * 128 : (k + 1) * 128]
-                bias_sum = bias_sum + c_h[:, k * 128 : (k + 1) * 128]
-            r.c2[:, at] = c_h.astype(bf16)
-            r.t2[:, at] = (d * t_a).astype(bf16)
-        r.sums[1] = slope_sum
-        r.sums[0] = bias_sum
-
-    each_image(back_two)
+        for b in range(2):
+            r.field[6 + b] = expand(small[SN, b], True, 0.0, masks)
+        pipeline(range(2 * PARTS), lambda k: (r.ca[:, AT[k]], dot_tn(wa3[...], doubled(6, k))),
+                 functools.partial(backward, two, 2, 1, 0, r.c2, r.t2))
+
     raw = dot_nt(r.a1[...], r.c2[...]) + dot_nt(r.b1[...], r.t2[...])
     straight, across = correction(raw, r.mids[...].reshape(C, C), q2, sigma2)
     r.dmid[...] = (straight * raw + (across * right2) * r.left2[0:1, :]).reshape(n, w, C)
@@ -531,37 +569,26 @@
     sum_mid.start()
     g3 = dot_nt(r.field[4], r.a2[:, 0:PX]) + dot_nt(r.field[6], r.b2[:, 0:PX])
     r.stage2[1] = g3 + dot_nt(r.field[5], r.a2[:, PX:]) + dot_nt(r.field[7], r.b2[:, PX:])
-
-    def back_one(b):
+    sum_mid.forward()
+
+    @stage
+    def back_one():
         masks = tap_masks()
-        slope_sum = r.sums[2]
-        prods, dprods = [], []
-        for part in range(PARTS):
-            if part == 1:
-                pl.when(b == 0)(sum_mid.forward)
-            at = tile_at(b, part)
-            h = r.h1[:, at]
-            sl = slope1()
-            x, t, e = pieces(h, sl)
-            d = 1.0 + t + x * e
-            c2 = r.c2[:, at]
-            c_a = dot_nn(mh[...], c2) + dot_nn(ml[...], c2)
-            t_a = dot_nn(mh[...], r.t2[:, at])
-            q = (2.0 * e * (1.0 - x * t)) * r.g1[:, at] * t_a
-            c_h = (d * c_a + sl * q).astype(bf16)
-            t_h = (d * t_a).astype(bf16)
-            grad = h * (c_a * h * e + q)
-            for k in range(TILE // 128):
-                slope_sum = slope_sum + grad[:, k * 128 : (k + 1) * 128]
-            r.prod[0, :, part * TILE : (part + 1) * TILE] = dot_nn(wp1[...], c_h)
-            r.prod[1, :, part * TILE : (part + 1) * TILE] = dot_nn(wp1[...], t_h)
-            r.a2[:, at] = c_h
-            r.b2[:, at] = t_h
-            r.sums[2] = slope_sum
-        small[SA, b] = collapse(r.prod[0], True, masks)
-        small[SB, b] = collapse(r.prod[1], True, masks)
-
-    each_image(back_one)
+
+        def dots(k):
+            c2 = r.c2[:, AT[k]]
+            return dot_nn(mh[...], c2) + dot_nn(ml[...], c2), dot_nn(mh[...], r.t2[:, AT[k]])
+
+        def after(k):
+            to = slice((k % PARTS) * TILE, (k % PARTS + 1) * TILE)
+            r.prod[0, :, to] = dot_nn(wp1[...], r.a2[:, AT[k]])
+            r.prod[1, :, to] = dot_nn(wp1[...], r.b2[:, AT[k]])
+            if k % PARTS == PARTS - 1:
+                small[SA, k // PARTS] = collapse(r.prod[0], True, masks)
+                small[SB, k // PARTS] = collapse(r.prod[1], True, masks)
+
+        pipeline(range(2 * PARTS), dots, functools.partial(backward, one, 0, 2, None, r.a2, r.b2), after)
+
     g1 = dot_nt(r.field[0], r.a2[:, 0:PX]) + dot_nt(r.field[2], r.b2[:, 0:PX])
     g1 = g1 + dot_nt(r.field[1], r.a2[:, PX:]) + dot_nt(r.field[3], r.b2[:, PX:])
     ones = jnp.ones((8, 128), f32)
@@ -569,9 +596,9 @@
         ones, acc, (((1,), (1,)), ((), ())), precision=HIGH, preferred_element_type=f32)[0:1]
     dside = r.dside
     dside[27:28, :] = g1[38:39]
-    dside[28:29, :] = row_of(r.sums[2]) * (0.5 * sigmoid(side[28:29, :]))
+    dside[28:29, :] = row_of(r.sums[2]) * (sigmoid(side[28:29, :]))
     dside[29:30, :] = row_of(r.sums[0])
-    dside[30:31, :] = row_of(r.sums[1]) * (0.5 * sigmoid(side[30:31, :]))
+    dside[30:31, :] = row_of(r.sums[1]) * (sigmoid(side[30:31, :]))
     dside[58:64, :] = jnp.zeros((6, C), f32)
     row80 = lax.broadcasted_iota(jnp.int32, (80, C), 0)
     for at, (q, sigma, outer), grad, start in ((0, side1, g1, 0), (1, side3, r.stage2[1], 31)):
@@ -608,6 +635,8 @@
         tile = tile + jnp.where((lane == 4) & (sub == b), log_part, 0.0)
     r.results[me, 6] = tile
     share.start()
+    sum_side.forward()
+    share.forward()
     mid_grad = sum_mid.finish() / (2.0 * n)
     r.mid_g[...] = mid_grad
     diff = r.mid_o[...] - adam(r.mid_w[...], mid_grad, r.mid_f[...], r.mid_s[...], 0.01)[0]
@@ -618,15 +647,6 @@
     ring3, ring4 = Across(groups, r.ring3_sem), Across(groups, r.ring4_sem)
     for j, to in ring1.others():
         ring1.copy(r.mid_diff.at[to], r.mid_parts.at[j], j, to).start()
-    sum_side.forward()
-    share.forward()
-    total = r.mid_diff[grp]
-    for j, to in ring1.others():
-        ring1.copy(r.mid_diff.at[to], r.mid_parts.at[j], j, to).wait_recv()
-        total = total + r.mid_parts[j]
-    r.mid_sum[grp] = total
-    for j, to in ring2.others():
-        ring2.copy(r.mid_sum.at[grp], r.mid_sum.at[grp], j, to).start()
     side_grad = unpack(sum_side.finish(), fold)[0:58] / (2.0 * n)
     r.side_g[...] = side_grad
     new = adam(r.side_w[:, 0, :], side_grad, r.side_f[:, 0, :], r.side_s[:, 0, :], side_rate(w))[0]
@@ -647,6 +667,13 @@
     r.tiny_diff[grp] = r.tiles[3] - flip(jnp.where(lane < 4, new, 0.0))
     for j, to in ring4.others():
         ring4.copy(r.tiny_diff.at[grp], r.tiny_diff.at[grp], j, to).start()
+    total = r.mid_diff[grp]
+    for j, to in ring1.others():
+        ring1.copy(r.mid_diff.at[to], r.mid_parts.at[j], j, to).wait_recv()
+        total = total + r.mid_parts[j]
+    r.mid_sum[grp] = total
+    for j, to in ring2.others():
+        ring2.copy(r.mid_sum.at[grp], r.mid_sum.at[grp], j, to).start()
     tiles = [r.results[d, 6] for d in range(n)]
     masks = match([jnp.broadcast_to(t[0:1, 5:6], (1, 128)) for t in tiles], me, 3.0, 1.0)
     log_third = jnp.zeros((1, 128), f32)
@@ -760,8 +787,8 @@
         cols=vmem(3, C, 128), small=vmem(10, 2, 8, PX), sums=vmem(3, C, 128), field=half(8, 80, PX), prod=vmem(2, 80, PX),
         mh=half(C, C), ml=half(C, C), left2=vmem(8, C), live=vmem(8, 128), side=vmem(64, C),
         h1=big(f32), g1=big(f32), h2=big(f32), g2=big(f32),
-        d1=big(bf16), a1=big(bf16), b1=big(bf16), d2=big(bf16), a2=big(bf16), b2=big(bf16), c2=big(bf16), t2=big(bf16),
-        sides=vmem(n, side_rows, 128), thirds=vmem(n, 10, 8, 128), mids=vmem(n, w, C), results=vmem(n, 7, 8, 128),
+        d1=big(f32), a1=big(bf16), b1=big(bf16), d2=big(f32), a2=big(bf16), b2=big(bf16), c2=big(bf16), t2=big(bf16),
+        ca=big(f32), sides=vmem(n, side_rows, 128), thirds=vmem(n, 10, 8, 128), mids=vmem(n, w, C), results=vmem(n, 7, 8, 128),
         picked=vmem(9, 8, 128), firsts=vmem(6, 8, 128), dmid=vmem(n, w, C), dside=vmem(64, C),
         side_blocks=vmem(n, side_rows, 128),
         mid_pair=vmem(m, w, C), mid_chip=vmem(m, w, C), mid_chips=vmem(m, w, C),
@@ -800,7 +827,7 @@
         out_specs=[vm] * len(outs),
         out_shape=list(outs.values()),
         scratch_shapes=list(scratch.values()),
-        compiler_params=pltpu.CompilerParams(vmem_limit_bytes=32 << 20),
+        compiler_params=pltpu.CompilerParams(vmem_limit_bytes=60 << 20),
     )(*ins.values())
     o = types.SimpleNamespace(**dict(zip(outs, made)))
     whole = lambda x: x.reshape(1, 3, 3, PX)

time: 90 us -> 73.6 us (0.82)
  local copies, waits for them, and re-layouts: 8.23 us -> 0 us
  Pallas kernels: 79.5 us -> 71.9 us
    pallas_call x1, Pallas kernels: 78.1 us -> 69.2 us  [on_device(): pl.pallas_call(functools.partial(main_kernel, n, groups, list(ins) + list...]
    unnamed x44 -> x0, local copies, waits for them, and re-layouts: 8.23 us -> none
    pallas_call x1, Pallas kernels: 1.38 us -> 2.78 us  [on_device(): pl.pallas_call(functools.partial(last_kernel, n, groups, list(ins) + list...]
where the time goes in v3:
time: 73.6 us; the launch traced here: 73.4 us
  Pallas kernels  71.9 us (98%)
  between operations  1.49 us (2%)
    pallas_call x1, Pallas kernels, on_device(): pl.pallas_call(functools.partial(main_kernel, n, groups, list(ins) + list...  69.2 us
    pallas_call x1, Pallas kernels, on_device(): pl.pallas_call(functools.partial(last_kernel, n, groups, list(ins) + list...  2.78 us

profile of v3, /device:TPU:0, one launch (start us, length us, event | category | flops | bytes accessed | tf_op | source)
XLA Modules:
  0.0 73.4 jit_solution(13788442246855503060)
XLA Ops:
  1.3 69.2 %shard_map.389 = (f32[9,8,128]{2,1,0:T(8,128)}, f32[9,8,128]{2,1,0:T(8,128)}, f32[3,8,128]{2,1,0:T(8,128)}, f32[64,512]{1,0:T(8,128)}, f32[64,512]{1,0:T(8,128)}, /*index=5*/f32[58,64]{1,0:T(8,128)}, f32[58,64]{1,0:T(8,128)}) custom-call(f32[9,8,128]{2,1,0:T(8,128)} %bitcast.57, f32[9,8,128]{2,1,0:T(8,128)} %bitcast.58, f32[9,8,128]{2,1,0:T(8,128)} %bitcast.59, ...), custom_call_target="tpu_custom_call" | custom-call | tf_op jit(solution)/shard_map/pallas_call | solution.py:803
  70.5 2.8 %shard_map.390 = (f32[9,8,128]{2,1,0:T(8,128)}, f32[9,8,128]{2,1,0:T(8,128)}, f32[1,3]{1,0:T(1,128)}, f32[1,1]{1,0:T(1,128)}, f32[64,512]{1,0:T(8,128)}, /*index...) custom-call(f32[9,8,128]{2,1,0:T(8,128)} %get-tuple-element.53.refs_, ...), custom_call_target="tpu_custom_call" | custom-call | tf_op jit(solution)/shard_map/pallas_call | solution.py:824

commit v4 on v3

--- a/solution.py
+++ b/solution.py
@@ -237,12 +237,16 @@
 
 
 class Reduce:
-    def __init__(self, n, source, from_pair, chipsum, from_chips, sems):
-        self.n, self.m = n, n // 2
+    def __init__(self, n, pieces, source, from_pair, chipsum, from_chips, sems):
+        self.n, self.m, self.pieces = n, n // 2, pieces
+        self.rows = source.shape[1] // pieces
         self.source, self.from_pair, self.chipsum, self.from_chips, self.sems = source, from_pair, chipsum, from_chips, sems
         self.me = lax.axis_index("dp")
         self.chip, self.core = self.me // 2, self.me % 2
         self.pair = self.me + 1 - 2 * self.core
+
+    def piece(self, p):
+        return pl.ds(p * self.rows, self.rows)
 
     def swap_copy(self, k, sem):
         return pltpu.make_async_remote_copy(
@@ -250,10 +254,11 @@
             send_sem=self.sems.at[0, sem], recv_sem=self.sems.at[1, sem],
             device_id={"dp": self.pair}, device_id_type=MESH)
 
-    def chip_copy(self, slot, j, target):
+    def chip_copy(self, slot, j, p, target):
+        sem = self.m + p * self.m + j
         return pltpu.make_async_remote_copy(
-            src_ref=self.chipsum.at[slot], dst_ref=self.from_chips.at[j],
-            send_sem=self.sems.at[0, self.m + j], recv_sem=self.sems.at[1, self.m + j],
+            src_ref=self.chipsum.at[slot, self.piece(p)], dst_ref=self.from_chips.at[j, self.piece(p)],
+            send_sem=self.sems.at[0, sem], recv_sem=self.sems.at[1, sem],
             device_id={"dp": target}, device_id_type=MESH)
 
     def start(self):
@@ -261,25 +266,29 @@
             self.swap_copy(lax.rem(self.chip + j, self.m), j % self.m).start()
 
     def forward(self):
-        for j in range(1, self.m + 1):
-            to = lax.rem(self.chip + j, self.m)
-            self.swap_copy(to, j % self.m).wait_recv()
-            self.chipsum[to] = self.source[2 * to + self.core] + self.from_pair[to]
-            if j < self.m:
-                self.chip_copy(to, j, to * 2 + self.core).start()
-
-    def finish(self):
-        total = self.chipsum[self.chip]
+        for p in range(self.pieces):
+            for j in range(1, self.m):
+                to = lax.rem(self.chip + j, self.m)
+                if p == 0:
+                    self.swap_copy(to, j).wait_recv()
+                    self.chipsum[to] = self.source[2 * to + self.core] + self.from_pair[to]
+                self.chip_copy(to, j, p, to * 2 + self.core).start()
+        self.swap_copy(self.chip, 0).wait_recv()
+        self.chipsum[self.chip] = self.source[self.me] + self.from_pair[self.chip]
+
+    def finish(self, p):
+        total = self.chipsum[self.chip, self.piece(p)]
         for j in range(1, self.m):
-            self.chip_copy(self.chip, j, self.pair).wait_recv()
-            total = total + self.from_chips[j]
+            self.chip_copy(self.chip, j, p, self.pair).wait_recv()
+            total = total + self.from_chips[j, self.piece(p)]
         return total
 
     def drain(self):
         for k in range(self.m):
             self.swap_copy(k, k).wait_send()
-        for j in range(1, self.m):
-            self.chip_copy(self.chip, j, self.pair).wait_send()
+        for p in range(self.pieces):
+            for j in range(1, self.m):
+                self.chip_copy(self.chip, j, p, self.pair).wait_send()
 
 
 class Across:
@@ -362,6 +371,7 @@
     get_third = Gather(n, r.thirds, r.thirds_sem)
     get_mid = Gather(n, r.mids, r.mids_sem)
     share = Gather(n, r.results, r.results_sem)
+    share_flow = Gather(n, r.flows, r.flows_sem)
     r.sides[me] = pack(jnp.concatenate([r.side_w[:, 0, :], jnp.zeros((6, w), f32)], 0), fold)
     for at, ref in enumerate((r.images, r.probes, r.cots)):
         r.thirds[me, 3 * at : 3 * at + 3] = ref[6:9]
@@ -526,7 +536,7 @@
             if k % PARTS == PARTS - 1:
                 b = k // PARTS
                 flow = small[SZ, b] + collapse(r.prod[0], False, masks) + bias_col
-                fold_field(flow, r.firsts if b == 0 else r.results.at[me], 0)
+                fold_field(flow, r.firsts if b == 0 else r.flows.at[me], 0)
                 small[ST, b] = jnp.where(valid(), collapse(r.prod[1], False, masks), 0.0)
 
         pipeline(range(2 * PARTS), dots, functools.partial(forward, two, 2, 1, r.a2, r.b2), after)
@@ -551,8 +561,10 @@
             small[SN, b] = small[SN, b] - on * v
             small[SS, b] = small[SS, b] + (on / (step + 1.0)) * v
 
+    share_flow.start()
     for step in (1, 2, 3):
         stage(functools.partial(pull, step))
+    share_flow.forward()
 
     @stage
     def back_two():
@@ -565,10 +577,30 @@
     raw = dot_nt(r.a1[...], r.c2[...]) + dot_nt(r.b1[...], r.t2[...])
     straight, across = correction(raw, r.mids[...].reshape(C, C), q2, sigma2)
     r.dmid[...] = (straight * raw + (across * right2) * r.left2[0:1, :]).reshape(n, w, C)
-    sum_mid = Reduce(n, r.dmid, r.mid_pair, r.mid_chip, r.mid_chips, r.mid_sem)
+    sum_mid = Reduce(n, w // 16, r.dmid, r.mid_pair, r.mid_chip, r.mid_chips, r.mid_sem)
     sum_mid.start()
     g3 = dot_nt(r.field[4], r.a2[:, 0:PX]) + dot_nt(r.field[6], r.b2[:, 0:PX])
-    r.stage2[1] = g3 + dot_nt(r.field[5], r.a2[:, PX:]) + dot_nt(r.field[7], r.b2[:, PX:])
+    g3 = g3 + dot_nt(r.field[5], r.a2[:, PX:]) + dot_nt(r.field[7], r.b2[:, PX:])
+    ones = jnp.ones((8, 128), f32)
+    row_of = lambda acc: lax.dot_general(
+        ones, acc, (((1,), (1,)), ((), ())), precision=HIGH, preferred_element_type=f32)[0:1]
+    dside = r.dside
+
+    def put_taps(at, norm, grad, start):
+        q, sigma, outer = norm
+        row80 = lax.broadcasted_iota(jnp.int32, (80, C), 0)
+        joined = jnp.where((row80 % 8 < 3) & (row80 < 72), grad + pltpu.roll(grad, 77, 0), 0.0)
+        straight, across = correction(joined, r.stage[at], q, sigma)
+        r.stage2[at] = straight * joined + across * outer
+        for color in range(3):
+            for tap in range(9):
+                to = start + 9 * color + tap
+                dside[to : to + 1, :] = r.stage2[at, 8 * tap + color : 8 * tap + color + 1, :]
+
+    dside[29:30, :] = row_of(r.sums[0])
+    dside[30:31, :] = row_of(r.sums[1]) * sigmoid(side[30:31, :])
+    dside[58:64, :] = jnp.zeros((6, C), f32)
+    put_taps(1, side3, g3, 31)
     sum_mid.forward()
 
     @stage
@@ -591,27 +623,12 @@
 
     g1 = dot_nt(r.field[0], r.a2[:, 0:PX]) + dot_nt(r.field[2], r.b2[:, 0:PX])
     g1 = g1 + dot_nt(r.field[1], r.a2[:, PX:]) + dot_nt(r.field[3], r.b2[:, PX:])
-    ones = jnp.ones((8, 128), f32)
-    row_of = lambda acc: lax.dot_general(
-        ones, acc, (((1,), (1,)), ((), ())), precision=HIGH, preferred_element_type=f32)[0:1]
-    dside = r.dside
     dside[27:28, :] = g1[38:39]
-    dside[28:29, :] = row_of(r.sums[2]) * (sigmoid(side[28:29, :]))
-    dside[29:30, :] = row_of(r.sums[0])
-    dside[30:31, :] = row_of(r.sums[1]) * (sigmoid(side[30:31, :]))
-    dside[58:64, :] = jnp.zeros((6, C), f32)
-    row80 = lax.broadcasted_iota(jnp.int32, (80, C), 0)
-    for at, (q, sigma, outer), grad, start in ((0, side1, g1, 0), (1, side3, r.stage2[1], 31)):
-        joined = jnp.where((row80 % 8 < 3) & (row80 < 72), grad + pltpu.roll(grad, 77, 0), 0.0)
-        straight, across = correction(joined, r.stage[at], q, sigma)
-        r.stage2[at] = straight * joined + across * outer
-        for color in range(3):
-            for tap in range(9):
-                to = start + 9 * color + tap
-                dside[to : to + 1, :] = r.stage2[at, 8 * tap + color : 8 * tap + color + 1, :]
+    dside[28:29, :] = row_of(r.sums[2]) * sigmoid(side[28:29, :])
+    put_taps(0, side1, g1, 0)
     for d in range(n):
         r.side_blocks[d] = pack(dside[:, d * w : (d + 1) * w], fold)
-    sum_side = Reduce(n, r.side_blocks, r.side_pair, r.side_chip, r.side_chips, r.side_sem)
+    sum_side = Reduce(n, 1, r.side_blocks, r.side_pair, r.side_chip, r.side_chips, r.side_sem)
     sum_side.start()
     total_scale = tiny[0, 0, 2] + tiny[1, 0, 2] + tiny[2, 0, 2]
     tile = jnp.where(lane == 5, counts[0, 0].astype(f32), 0.0)
@@ -622,7 +639,7 @@
         q = 2.0 * e * (1.0 - x * t) * p * t_a
         c_z = jnp.where(valid(), cot + (1.0 + t + x * e) * c_a + slope0 * q, 0.0)
         slope_grad = jnp.where(valid(), field * (c_a * field * e + q), 0.0)
-        fold_field(c_z * scale_col, r.firsts if b == 0 else r.results.at[me], 3)
+        fold_field(c_z * scale_col, r.firsts if b == 0 else r.results.at[me], 3 if b == 0 else 0)
         sums = [
             jnp.sum(cot, axis=1, keepdims=True),
             jnp.sum(c_z, axis=1, keepdims=True) * scale_col,
@@ -633,30 +650,35 @@
             tile = tile + jnp.where((lane == k) & (sub < 3), sums[k], 0.0)
         log_part = (1024.0 * total_scale + jnp.sum(small[SS, b] * small[ST, b])) / 3072.0
         tile = tile + jnp.where((lane == 4) & (sub == b), log_part, 0.0)
-    r.results[me, 6] = tile
+    r.results[me, 3] = tile
     share.start()
     sum_side.forward()
+    ring1 = Across(groups, r.ring1_sem)
+    ring3, ring4 = Across(groups, r.ring3_sem), Across(groups, r.ring4_sem)
+    cuts = w // 16
+
+    def mid_copy(p, j, to):
+        rows = pl.ds(16 * p, 16)
+        return ring1.copy(r.mid_diff.at[grp, rows], r.mid_diff.at[grp, rows], p * groups + j, to)
+
+    for p in range(cuts):
+        rows = slice(16 * p, 16 * p + 16)
+        mid_grad = sum_mid.finish(p) / (2.0 * n)
+        r.mid_g[rows] = mid_grad
+        r.mid_diff[grp, rows] = r.mid_o[rows] - adam(r.mid_w[rows], mid_grad, r.mid_f[rows], r.mid_s[rows], 0.01)[0]
+        for j, to in ring1.others():
+            mid_copy(p, j, to).start()
     share.forward()
-    mid_grad = sum_mid.finish() / (2.0 * n)
-    r.mid_g[...] = mid_grad
-    diff = r.mid_o[...] - adam(r.mid_w[...], mid_grad, r.mid_f[...], r.mid_s[...], 0.01)[0]
-    chunk = C // groups
-    for k in range(groups):
-        r.mid_diff[k] = diff[:, k * chunk : (k + 1) * chunk]
-    ring1, ring2 = Across(groups, r.ring1_sem), Across(groups, r.ring2_sem)
-    ring3, ring4 = Across(groups, r.ring3_sem), Across(groups, r.ring4_sem)
-    for j, to in ring1.others():
-        ring1.copy(r.mid_diff.at[to], r.mid_parts.at[j], j, to).start()
-    side_grad = unpack(sum_side.finish(), fold)[0:58] / (2.0 * n)
+    side_grad = unpack(sum_side.finish(0), fold)[0:58] / (2.0 * n)
     r.side_g[...] = side_grad
     new = adam(r.side_w[:, 0, :], side_grad, r.side_f[:, 0, :], r.side_s[:, 0, :], side_rate(w))[0]
     r.side_diff[grp] = pack(jnp.concatenate([r.side_o[...] - new, jnp.zeros((6, w), f32)], 0), fold)
     for j, to in ring3.others():
         ring3.copy(r.side_diff.at[grp], r.side_diff.at[grp], j, to).start()
     share.finish()
-    tiny_sum = r.results[0, 6]
+    tiny_sum = r.results[0, 3]
     for d in range(1, n):
-        tiny_sum = tiny_sum + r.results[d, 6]
+        tiny_sum = tiny_sum + r.results[d, 3]
     r.out_small[0] = tiny_sum
     r.tiles[...] = jnp.zeros_like(r.tiles)
     for c in range(3):
@@ -667,26 +689,20 @@
     r.tiny_diff[grp] = r.tiles[3] - flip(jnp.where(lane < 4, new, 0.0))
     for j, to in ring4.others():
         ring4.copy(r.tiny_diff.at[grp], r.tiny_diff.at[grp], j, to).start()
-    total = r.mid_diff[grp]
-    for j, to in ring1.others():
-        ring1.copy(r.mid_diff.at[to], r.mid_parts.at[j], j, to).wait_recv()
-        total = total + r.mid_parts[j]
-    r.mid_sum[grp] = total
-    for j, to in ring2.others():
-        ring2.copy(r.mid_sum.at[grp], r.mid_sum.at[grp], j, to).start()
-    tiles = [r.results[d, 6] for d in range(n)]
+    tiles = [r.results[d, 3] for d in range(n)]
     masks = match([jnp.broadcast_to(t[0:1, 5:6], (1, 128)) for t in tiles], me, 3.0, 1.0)
     log_third = jnp.zeros((1, 128), f32)
     for d in range(n):
         log_third = jnp.where(masks[d] > 0.0, jnp.broadcast_to(tiles[d][1:2, 4:5], (1, 128)), log_third)
-    for k in range(6):
-        out, c = (r.out_flow, k) if k < 3 else (r.out_back, k - 3)
-        picked = jnp.zeros((8, 128), f32)
-        for d in range(n):
-            picked = jnp.where(masks[d] > 0.0, r.results[d, k], picked)
-        out[c] = r.firsts[k]
-        out[3 + c] = jnp.where(own_count > 1.5, r.results[me, k], 0.0)
-        out[6 + c] = picked
+    share_flow.finish()
+    for out, ref, base in ((r.out_flow, r.flows, 0), (r.out_back, r.results, 3)):
+        for c in range(3):
+            picked = jnp.zeros((8, 128), f32)
+            for d in range(n):
+                picked = jnp.where(masks[d] > 0.0, ref[d, c], picked)
+            out[c] = r.firsts[base + c]
+            out[3 + c] = jnp.where(own_count > 1.5, ref[me, c], 0.0)
+            out[6 + c] = picked
     logs = [jnp.broadcast_to(tile[b : b + 1, 4:5], (1, 128)) for b in range(2)]
     logs[1] = jnp.where(own_count > 1.5, logs[1], 0.0)
     row_lane = lax.broadcasted_iota(jnp.int32, (1, 128), 1)
@@ -704,15 +720,19 @@
     for k in range(1, groups):
         total = total + r.tiny_diff[k]
     r.out_small[2] = total
-    for j, to in ring2.others():
-        ring2.copy(r.mid_sum.at[grp], r.mid_sum.at[grp], j, to).wait_recv()
-    for k in range(groups):
-        r.mid_t[:, k * chunk : (k + 1) * chunk] = r.mid_sum[k]
+    for p in range(cuts):
+        rows = slice(16 * p, 16 * p + 16)
+        for j, to in ring1.others():
+            mid_copy(p, j, to).wait_recv()
+        total = r.mid_diff[0, rows]
+        for k in range(1, groups):
+            total = total + r.mid_diff[k, rows]
+        r.mid_t[rows] = total
     sum_mid.drain()
     sum_side.drain()
-    for ring in (ring1, ring2):
-        for j, to in ring.others():
-            ring.copy(r.mid_sum.at[grp], r.mid_sum.at[grp], j, to).wait_send()
+    for p in range(cuts):
+        for j, to in ring1.others():
+            mid_copy(p, j, to).wait_send()
     for j, to in ring3.others():
         ring3.copy(r.side_diff.at[grp], r.side_diff.at[grp], j, to).wait_send()
     for j, to in ring4.others():
@@ -788,16 +808,16 @@
         mh=half(C, C), ml=half(C, C), left2=vmem(8, C), live=vmem(8, 128), side=vmem(64, C),
         h1=big(f32), g1=big(f32), h2=big(f32), g2=big(f32),
         d1=big(f32), a1=big(bf16), b1=big(bf16), d2=big(f32), a2=big(bf16), b2=big(bf16), c2=big(bf16), t2=big(bf16),
-        ca=big(f32), sides=vmem(n, side_rows, 128), thirds=vmem(n, 10, 8, 128), mids=vmem(n, w, C), results=vmem(n, 7, 8, 128),
+        ca=big(f32), sides=vmem(n, side_rows, 128), thirds=vmem(n, 10, 8, 128), mids=vmem(n, w, C), results=vmem(n, 4, 8, 128), flows=vmem(n, 3, 8, 128), flows_sem=dma(2, n),
         picked=vmem(9, 8, 128), firsts=vmem(6, 8, 128), dmid=vmem(n, w, C), dside=vmem(64, C),
         side_blocks=vmem(n, side_rows, 128),
         mid_pair=vmem(m, w, C), mid_chip=vmem(m, w, C), mid_chips=vmem(m, w, C),
         side_pair=vmem(m, side_rows, 128), side_chip=vmem(m, side_rows, 128), side_chips=vmem(m, side_rows, 128),
-        mid_diff=vmem(groups, w, C // groups), mid_parts=vmem(groups, w, C // groups), mid_sum=vmem(groups, w, C // groups),
+        mid_diff=vmem(groups, w, C),
         side_diff=vmem(groups, side_rows, 128), tiny_diff=vmem(groups, 8, 128), tiles=vmem(4, 8, 128),
         sides_sem=dma(2, n), thirds_sem=dma(2, n), mids_sem=dma(2, n), results_sem=dma(2, n),
-        mid_sem=dma(2, n), side_sem=dma(2, n),
-        ring1_sem=dma(2, groups), ring2_sem=dma(2, groups), ring3_sem=dma(2, groups), ring4_sem=dma(2, groups),
+        mid_sem=dma(2, m * (1 + w // 16)), side_sem=dma(2, n),
+        ring1_sem=dma(2, groups * (w // 16)), ring3_sem=dma(2, groups), ring4_sem=dma(2, groups),
     )
     ins = {**vmem_in, **smem_in}
     made = pl.pallas_call(

time: 73.6 us -> 71.4 us (0.970)
  Pallas kernels: 71.9 us -> 69.7 us
    pallas_call x1, Pallas kernels: 69.2 us -> 67 us  [on_device(): pl.pallas_call(functools.partial(main_kernel, n, groups, list(ins) + list...]
where the time goes in v4:
time: 71.4 us; the launch traced here: 71.2 us
  Pallas kernels  69.7 us (98%)
  between operations  1.49 us (2%)
    pallas_call x1, Pallas kernels, on_device(): pl.pallas_call(functools.partial(main_kernel, n, groups, list(ins) + list...  67 us
    pallas_call x1, Pallas kernels, on_device(): pl.pallas_call(functools.partial(last_kernel, n, groups, list(ins) + list...  2.78 us

profile of v4, /device:TPU:0, one launch (start us, length us, event | category | flops | bytes accessed | tf_op | source)
XLA Modules:
  0.0 71.2 jit_solution(17865260117515590181)
XLA Ops:
  1.3 67.0 %shard_map.389 = (f32[9,8,128]{2,1,0:T(8,128)}, f32[9,8,128]{2,1,0:T(8,128)}, f32[3,8,128]{2,1,0:T(8,128)}, f32[64,512]{1,0:T(8,128)}, f32[64,512]{1,0:T(8,128)}, /*index=5*/f32[58,64]{1,0:T(8,128)}, f32[58,64]{1,0:T(8,128)}) custom-call(f32[9,8,128]{2,1,0:T(8,128)} %bitcast.57, f32[9,8,128]{2,1,0:T(8,128)} %bitcast.58, f32[9,8,128]{2,1,0:T(8,128)} %bitcast.59, ...), custom_call_target="tpu_custom_call" | custom-call | tf_op jit(solution)/shard_map/pallas_call | solution.py:823
  68.3 2.8 %shard_map.390 = (f32[9,8,128]{2,1,0:T(8,128)}, f32[9,8,128]{2,1,0:T(8,128)}, f32[1,3]{1,0:T(1,128)}, f32[1,1]{1,0:T(1,128)}, f32[64,512]{1,0:T(8,128)}, /*index...) custom-call(f32[9,8,128]{2,1,0:T(8,128)} %get-tuple-element.53.refs_, ...), custom_call_target="tpu_custom_call" | custom-call | tf_op jit(solution)/shard_map/pallas_call | solution.py:844

commit v5 on v4

--- a/solution.py
+++ b/solution.py
@@ -236,6 +236,27 @@
             self.copy(self.me, j, self.pair).wait_send()
 
 
+class Spread:
+    def __init__(self, n, buf, sems):
+        self.n, self.buf, self.sems, self.me = n, buf, sems, lax.axis_index("dp")
+
+    def copy(self, j):
+        return pltpu.make_async_remote_copy(
+            src_ref=self.buf.at[self.me], dst_ref=self.buf.at[self.me],
+            send_sem=self.sems.at[0, j], recv_sem=self.sems.at[1, j],
+            device_id={"dp": lax.rem(self.me + j, self.n)}, device_id_type=MESH)
+
+    def start(self):
+        for j in range(1, self.n):
+            self.copy(j).start()
+
+    def finish(self):
+        for j in range(1, self.n):
+            self.copy(j).wait_recv()
+        for j in range(1, self.n):
+            self.copy(j).wait_send()
+
+
 class Reduce:
     def __init__(self, n, pieces, source, from_pair, chipsum, from_chips, sems):
         self.n, self.m, self.pieces = n, n // 2, pieces
@@ -307,14 +328,11 @@
 def barrier(n, groups):
     me, grp = lax.axis_index("dp"), lax.axis_index("grp")
     sem = pltpu.get_barrier_semaphore()
-    m = n // 2
-    chip, core = me // 2, me % 2
-    for j in range(1, m):
-        pl.semaphore_signal(sem, inc=1, device_id={"dp": lax.rem(chip + j, m) * 2 + core}, device_id_type=MESH)
-    pl.semaphore_signal(sem, inc=1, device_id={"dp": me + 1 - 2 * core}, device_id_type=MESH)
+    for j in range(1, n):
+        pl.semaphore_signal(sem, inc=1, device_id={"dp": lax.rem(me + j, n)}, device_id_type=MESH)
     for j in range(1, groups):
         pl.semaphore_signal(sem, inc=1, device_id={"grp": lax.rem(grp + j, groups)}, device_id_type=MESH)
-    pl.semaphore_wait(sem, m + groups - 1)
+    pl.semaphore_wait(sem, n + groups - 2)
 
 
 def match(counts, me, wanted_mine, wanted_theirs):
@@ -515,8 +533,8 @@
     layer_one(0)
     third_image()
     prepare_image(1)
+    get_mid.forward()
     layer_one(1)
-    get_mid.forward()
     get_mid.finish()
     q2, sigma2, right2 = prepare_mid(r.mids[...].reshape(C, C), lefts, mh, ml, r.left2)
     r.sums[...] = jnp.zeros_like(r.sums)
@@ -541,29 +559,45 @@
 
         pipeline(range(2 * PARTS), dots, functools.partial(forward, two, 2, 1, r.a2, r.b2), after)
 
-    def pull(step):
+    share_flow.start()
+
+    @stage
+    def pulls():
         masks = tap_masks()
-        for b in range(2):
-            if step == 1:
+        v = [None, None]
+
+        def first(b):
+            if v[b] is None:
                 r.c2[:, IM[b]] = (r.c2[:, IM[b]].astype(f32) * r.d2[:, IM[b]]).astype(bf16)
-            else:
-                spread = expand(small[SV, b], True, 0.0, masks)
-                wide_v = jnp.concatenate([spread, spread], 0)
-                r.c2[:, IM[b]] = (dot_tn(wa3[...], wide_v) * r.d2[:, IM[b]]).astype(bf16)
-        for b in range(2):
+                return
+            spread = expand(v[b], True, 0.0, masks)
+            r.c2[:, IM[b]] = (dot_tn(wa3[...], jnp.concatenate([spread, spread], 0)) * r.d2[:, IM[b]]).astype(bf16)
+
+        def second(b):
             r.t2[:, IM[b]] = (dot_nn(mh[...], r.c2[:, IM[b]]) * r.d1[:, IM[b]]).astype(bf16)
-        sign = (-1.0) ** step
-        for b in range(2):
+
+        def third(b, step):
+            sign = (-1.0) ** step
             prod = dot_nn(wp1[...], r.t2[:, IM[b]])
-            v = jnp.where(valid(), small[SD, b] * collapse(prod, True, masks), 0.0)
-            small[SV, b] = v
+            v[b] = jnp.where(valid(), small[SD, b] * collapse(prod, True, masks), 0.0)
             on = sign * alive(b, step)
-            small[SN, b] = small[SN, b] - on * v
-            small[SS, b] = small[SS, b] + (on / (step + 1.0)) * v
-
-    share_flow.start()
-    for step in (1, 2, 3):
-        stage(functools.partial(pull, step))
+            small[SN, b] = small[SN, b] - on * v[b]
+            small[SS, b] = small[SS, b] + (on / (step + 1.0)) * v[b]
+
+        first(0)
+        second(0)
+        first(1)
+        third(0, 1)
+        second(1)
+        for step in (2, 3):
+            first(0)
+            third(1, step - 1)
+            second(0)
+            first(1)
+            third(0, step)
+            second(1)
+        third(1, 3)
+
     share_flow.forward()
 
     @stage
@@ -575,12 +609,12 @@
                  functools.partial(backward, two, 2, 1, 0, r.c2, r.t2))
 
     raw = dot_nt(r.a1[...], r.c2[...]) + dot_nt(r.b1[...], r.t2[...])
+    g3 = dot_nt(r.field[4], r.a2[:, 0:PX]) + dot_nt(r.field[6], r.b2[:, 0:PX])
+    g3 = g3 + dot_nt(r.field[5], r.a2[:, PX:]) + dot_nt(r.field[7], r.b2[:, PX:])
     straight, across = correction(raw, r.mids[...].reshape(C, C), q2, sigma2)
     r.dmid[...] = (straight * raw + (across * right2) * r.left2[0:1, :]).reshape(n, w, C)
     sum_mid = Reduce(n, w // 16, r.dmid, r.mid_pair, r.mid_chip, r.mid_chips, r.mid_sem)
     sum_mid.start()
-    g3 = dot_nt(r.field[4], r.a2[:, 0:PX]) + dot_nt(r.field[6], r.b2[:, 0:PX])
-    g3 = g3 + dot_nt(r.field[5], r.a2[:, PX:]) + dot_nt(r.field[7], r.b2[:, PX:])
     ones = jnp.ones((8, 128), f32)
     row_of = lambda acc: lax.dot_general(
         ones, acc, (((1,), (1,)), ((), ())), precision=HIGH, preferred_element_type=f32)[0:1]
@@ -650,9 +684,11 @@
             tile = tile + jnp.where((lane == k) & (sub < 3), sums[k], 0.0)
         log_part = (1024.0 * total_scale + jnp.sum(small[SS, b] * small[ST, b])) / 3072.0
         tile = tile + jnp.where((lane == 4) & (sub == b), log_part, 0.0)
-    r.results[me, 3] = tile
+    r.tiny_tiles[me] = tile
+    spread = Spread(n, r.tiny_tiles, r.tiny_tiles_sem)
+    sum_side.forward()
+    spread.start()
     share.start()
-    sum_side.forward()
     ring1 = Across(groups, r.ring1_sem)
     ring3, ring4 = Across(groups, r.ring3_sem), Across(groups, r.ring4_sem)
     cuts = w // 16
@@ -668,17 +704,16 @@
         r.mid_diff[grp, rows] = r.mid_o[rows] - adam(r.mid_w[rows], mid_grad, r.mid_f[rows], r.mid_s[rows], 0.01)[0]
         for j, to in ring1.others():
             mid_copy(p, j, to).start()
-    share.forward()
     side_grad = unpack(sum_side.finish(0), fold)[0:58] / (2.0 * n)
     r.side_g[...] = side_grad
     new = adam(r.side_w[:, 0, :], side_grad, r.side_f[:, 0, :], r.side_s[:, 0, :], side_rate(w))[0]
     r.side_diff[grp] = pack(jnp.concatenate([r.side_o[...] - new, jnp.zeros((6, w), f32)], 0), fold)
     for j, to in ring3.others():
         ring3.copy(r.side_diff.at[grp], r.side_diff.at[grp], j, to).start()
-    share.finish()
-    tiny_sum = r.results[0, 3]
+    spread.finish()
+    tiny_sum = r.tiny_tiles[0]
     for d in range(1, n):
-        tiny_sum = tiny_sum + r.results[d, 3]
+        tiny_sum = tiny_sum + r.tiny_tiles[d]
     r.out_small[0] = tiny_sum
     r.tiles[...] = jnp.zeros_like(r.tiles)
     for c in range(3):
@@ -689,12 +724,14 @@
     r.tiny_diff[grp] = r.tiles[3] - flip(jnp.where(lane < 4, new, 0.0))
     for j, to in ring4.others():
         ring4.copy(r.tiny_diff.at[grp], r.tiny_diff.at[grp], j, to).start()
-    tiles = [r.results[d, 3] for d in range(n)]
+    share.forward()
+    tiles = [r.tiny_tiles[d] for d in range(n)]
     masks = match([jnp.broadcast_to(t[0:1, 5:6], (1, 128)) for t in tiles], me, 3.0, 1.0)
     log_third = jnp.zeros((1, 128), f32)
     for d in range(n):
         log_third = jnp.where(masks[d] > 0.0, jnp.broadcast_to(tiles[d][1:2, 4:5], (1, 128)), log_third)
     share_flow.finish()
+    share.finish()
     for out, ref, base in ((r.out_flow, r.flows, 0), (r.out_back, r.results, 3)):
         for c in range(3):
             picked = jnp.zeros((8, 128), f32)
@@ -808,7 +845,7 @@
         mh=half(C, C), ml=half(C, C), left2=vmem(8, C), live=vmem(8, 128), side=vmem(64, C),
         h1=big(f32), g1=big(f32), h2=big(f32), g2=big(f32),
         d1=big(f32), a1=big(bf16), b1=big(bf16), d2=big(f32), a2=big(bf16), b2=big(bf16), c2=big(bf16), t2=big(bf16),
-        ca=big(f32), sides=vmem(n, side_rows, 128), thirds=vmem(n, 10, 8, 128), mids=vmem(n, w, C), results=vmem(n, 4, 8, 128), flows=vmem(n, 3, 8, 128), flows_sem=dma(2, n),
+        ca=big(f32), sides=vmem(n, side_rows, 128), thirds=vmem(n, 10, 8, 128), mids=vmem(n, w, C), results=vmem(n, 3, 8, 128), tiny_tiles=vmem(n, 8, 128), tiny_tiles_sem=dma(2, n), flows=vmem(n, 3, 8, 128), flows_sem=dma(2, n),
         picked=vmem(9, 8, 128), firsts=vmem(6, 8, 128), dmid=vmem(n, w, C), dside=vmem(64, C),
         side_blocks=vmem(n, side_rows, 128),
         mid_pair=vmem(m, w, C), mid_chip=vmem(m, w, C), mid_chips=vmem(m, w, C),

time: 71.4 us -> 71 us (level)
  no operation moved by 1% of the time
where the time goes in v5:
time: 71 us; the launch traced here: 70.8 us
  Pallas kernels  69.3 us (98%)
  between operations  1.49 us (2%)
    pallas_call x1, Pallas kernels, on_device(): pl.pallas_call(functools.partial(main_kernel, n, groups, list(ins) + list...  66.6 us
    pallas_call x1, Pallas kernels, on_device(): pl.pallas_call(functools.partial(last_kernel, n, groups, list(ins) + list...  2.78 us

profile of v5, /device:TPU:0, one launch (start us, length us, event | category | flops | bytes accessed | tf_op | source)
XLA Modules:
  0.0 70.8 jit_solution(12946540042765880004)
XLA Ops:
  1.3 66.6 %shard_map.389 = (f32[9,8,128]{2,1,0:T(8,128)}, f32[9,8,128]{2,1,0:T(8,128)}, f32[3,8,128]{2,1,0:T(8,128)}, f32[64,512]{1,0:T(8,128)}, f32[64,512]{1,0:T(8,128)}, /*index=5*/f32[58,64]{1,0:T(8,128)}, f32[58,64]{1,0:T(8,128)}) custom-call(f32[9,8,128]{2,1,0:T(8,128)} %bitcast.57, f32[9,8,128]{2,1,0:T(8,128)} %bitcast.58, f32[9,8,128]{2,1,0:T(8,128)} %bitcast.59, ...), custom_call_target="tpu_custom_call" | custom-call | tf_op jit(solution)/shard_map/pallas_call | solution.py:860
  67.9 2.8 %shard_map.390 = (f32[9,8,128]{2,1,0:T(8,128)}, f32[9,8,128]{2,1,0:T(8,128)}, f32[1,3]{1,0:T(1,128)}, f32[1,1]{1,0:T(1,128)}, f32[64,512]{1,0:T(8,128)}, /*index...) custom-call(f32[9,8,128]{2,1,0:T(8,128)} %get-tuple-element.53.refs_, ...), custom_call_target="tpu_custom_call" | custom-call | tf_op jit(solution)/shard_map/pallas_call | solution.py:881

commit v6 on v5

--- a/solution.py
+++ b/solution.py
@@ -325,14 +325,13 @@
         return [(j, lax.rem(self.grp + j, self.groups)) for j in range(1, self.groups)]
 
 
-def barrier(n, groups):
+def greet(n, groups):
     me, grp = lax.axis_index("dp"), lax.axis_index("grp")
     sem = pltpu.get_barrier_semaphore()
     for j in range(1, n):
         pl.semaphore_signal(sem, inc=1, device_id={"dp": lax.rem(me + j, n)}, device_id_type=MESH)
     for j in range(1, groups):
         pl.semaphore_signal(sem, inc=1, device_id={"grp": lax.rem(grp + j, groups)}, device_id_type=MESH)
-    pl.semaphore_wait(sem, n + groups - 2)
 
 
 def match(counts, me, wanted_mine, wanted_theirs):
@@ -385,6 +384,7 @@
     m = n // 2
     me, grp = lax.axis_index("dp"), lax.axis_index("grp")
     counts, terms, tiny = r.counts, r.terms, r.tiny
+    greet(n, groups)
     get_side = Gather(n, r.sides, r.sides_sem)
     get_third = Gather(n, r.thirds, r.thirds_sem)
     get_mid = Gather(n, r.mids, r.mids_sem)
@@ -398,7 +398,7 @@
     own_count = jnp.broadcast_to(counts[0, 0].astype(f32), (1, 128))
     r.thirds[me, 9] = jnp.where(lane == 0, counts[0, 0].astype(f32), terms[0, 2].astype(f32))
     r.mids[me] = r.mid_w[...]
-    barrier(n, groups)
+    pl.semaphore_wait(pltpu.get_barrier_semaphore(), n + groups - 2)
     get_side.start()
     get_third.start()
     get_mid.start()

time: 71 us -> 71 us (level)
  no operation moved by 1% of the time
where the time goes in v6:
time: 71 us; the launch traced here: 70.8 us
  Pallas kernels  69.3 us (98%)
  between operations  1.49 us (2%)
    pallas_call x1, Pallas kernels, on_device(): pl.pallas_call(functools.partial(main_kernel, n, groups, list(ins) + list...  66.5 us
    pallas_call x1, Pallas kernels, on_device(): pl.pallas_call(functools.partial(last_kernel, n, groups, list(ins) + list...  2.78 us

profile of v6, /device:TPU:0, one launch (start us, length us, event | category | flops | bytes accessed | tf_op | source)
XLA Modules:
  0.0 70.8 jit_solution(8615476764643665251)
XLA Ops:
  1.3 66.5 %shard_map.389 = (f32[9,8,128]{2,1,0:T(8,128)}, f32[9,8,128]{2,1,0:T(8,128)}, f32[3,8,128]{2,1,0:T(8,128)}, f32[64,512]{1,0:T(8,128)}, f32[64,512]{1,0:T(8,128)}, /*index=5*/f32[58,64]{1,0:T(8,128)}, f32[58,64]{1,0:T(8,128)}) custom-call(f32[9,8,128]{2,1,0:T(8,128)} %bitcast.57, f32[9,8,128]{2,1,0:T(8,128)} %bitcast.58, f32[9,8,128]{2,1,0:T(8,128)} %bitcast.59, ...), custom_call_target="tpu_custom_call" | custom-call | tf_op jit(solution)/shard_map/pallas_call | solution.py:860
  67.8 2.8 %shard_map.390 = (f32[9,8,128]{2,1,0:T(8,128)}, f32[9,8,128]{2,1,0:T(8,128)}, f32[1,3]{1,0:T(1,128)}, f32[1,1]{1,0:T(1,128)}, f32[64,512]{1,0:T(8,128)}, /*index...) custom-call(f32[9,8,128]{2,1,0:T(8,128)} %get-tuple-element.53.refs_, ...), custom_call_target="tpu_custom_call" | custom-call | tf_op jit(solution)/shard_map/pallas_call | solution.py:881
